TPU v7x, 32 devices: a whole 2x2x4 slice. The times are simulated.
32 devices in a mesh: parts: 2 (over x), seq: 16 (over z, y, core), tensor: 1.
Axes of the slice: x: 2, y: 2, z: 4, core: 2. Of those that a mesh axis runs over, the one named last changes fastest.
Arguments:
- stream_in: bfloat16 [8192, 2048], P(('parts', 'seq')), parts along dimension 0, may hold values from -6 to 6
- mr_features: bfloat16 [8192, 3, 2048], P(('parts', 'seq'), None, 'tensor'), parts along dimension 0, may hold values from -6 to 6
- mr_short: float32 [7, 3, 2048], P(None, None, 'tensor'), may hold values from -2 to 2
- medium_taps: float32 [128, 128], replicated, may hold values from -0.5 to 0.5
- mr_out_weight: bfloat16 [2048, 2048], P('tensor', 'seq'), may hold values from -0.125 to 0.125
- li_gain: float32 [2048], replicated, may hold values from 0.1 to 1.9
- li_in_weight: bfloat16 [2048, 3, 2048], P('seq', None, 'tensor'), may hold values from -0.125 to 0.125
- li_short: float32 [7, 3, 2048], P(None, None, 'tensor'), may hold values from -2 to 2
- li_rates: float32 [128, 16], replicated, may hold values from 0 to 1, as said below
- li_residues: float32 [128, 16], replicated, may hold values from -4 to 4
Outputs:
- stream: bfloat16 [8192, 2048], P(('parts', 'seq')), parts along dimension 0
- gated_li: bfloat16 [8192, 2048], P(('parts', 'seq'), 'tensor'), parts along dimension 0
There are 2 independent parts, one for each index of `parts`. A program takes and returns all parts, laid end to end along the dimension named above; an argument that names none is the same for every part. Nothing has to cross between parts.
Inputs may be any that keep to these rules, and one draw needn't show every extreme that they name: `li_rates`: positive decay rates.
All inputs are finite; a program needn't handle non-finite values.
Results may differ from a plain program's by a relative error of at most 0.024.
Values may be sent and summed in bfloat16 or wider, within the bound.
A program may use at most 128 MiB of HBM per device.

v0:
```python
import math

import jax
import jax.numpy as jnp
from jax import lax
from jax.sharding import PartitionSpec as P

GROUP = 16
ORDER = 16
SHORT = 7
MEDIUM = 128


HIGHEST = lax.Precision.HIGHEST


def shifted(value, axis, steps):
    count = lax.axis_size(axis)
    leading, last = (max(0, -steps), min(count, count - steps))
    return lax.ppermute(value, axis, [(source, source + steps) for source in range(leading, last)])


def root_norm(values, gain_vector):
    widened = values.astype(jnp.float32)
    mean_square = jnp.mean(widened * widened, axis=-1, keepdims=True)
    return (widened * lax.rsqrt(mean_square + 1e-06) * gain_vector).astype(jnp.bfloat16)


def short_filter(projected, filter_taps, border):
    length = projected.shape[0]
    extended = jnp.concatenate([border, projected], axis=0).astype(jnp.float32)
    running = jnp.zeros((length,) + projected.shape[1:], jnp.float32)
    for lagged in range(SHORT):
        running = (
            running
            + filter_taps[lagged] * extended[SHORT - 1 - lagged : SHORT - 1 - lagged + length]
        )
    return running


def medium_filter(extended, filter_taps):
    length = extended.shape[0] - (MEDIUM - 1)
    filter_count = filter_taps.shape[1]
    block_len = math.gcd(length, 128)
    block_count = length // block_len
    lag_table = (
        jnp.arange(block_len)[:, None] + (MEDIUM - 1) - jnp.arange(block_len + MEDIUM - 1)[None, :]
    )
    inside = (lag_table >= 0) & (lag_table < MEDIUM)
    band_matrix = jnp.where(inside[None], filter_taps.T[:, jnp.clip(lag_table, 0, MEDIUM - 1)], 0.0)
    widened = extended.astype(jnp.float32).reshape(-1, filter_count, GROUP)
    windows = jnp.stack(
        [
            widened[position * block_len : position * block_len + block_len + MEDIUM - 1]
            for position in range(block_count)
        ]
    )
    result = jnp.einsum("gts,nsgc->ntgc", band_matrix, windows, precision=HIGHEST)
    return result.reshape(length, filter_count * GROUP)


def modal_conv(signal, decay_rates, scaled):
    length, filter_count, per_unit = signal.shape
    block_len = math.gcd(length, 128)
    block_count = length // block_len
    offsets = jnp.arange(block_len, dtype=jnp.float32)
    decays = jnp.exp(-decay_rates[:, :, None] * offsets)
    kernel = jnp.einsum("uo,uob->ub", scaled, decays, precision=HIGHEST)
    lag_table = jnp.arange(block_len)[:, None] - jnp.arange(block_len)[None, :]
    toeplitz = jnp.where(lag_table[None] >= 0, kernel[:, jnp.maximum(lag_table, 0)], 0.0)
    blocks = signal.reshape(block_count, block_len, filter_count, per_unit)
    response_local = jnp.einsum("uts,nsup->ntup", toeplitz, blocks, precision=HIGHEST)
    tail_decay = jnp.exp(-decay_rates[:, :, None] * (block_len - offsets))
    end_sums = jnp.einsum("uos,nsup->nuop", tail_decay, blocks, precision=HIGHEST)
    block_index = jnp.arange(block_count)
    gap_table = block_index[:, None] - block_index[None, :] - 1
    gap_len = (block_len * jnp.maximum(gap_table, 0)).astype(jnp.float32)
    carry_matrix = jnp.where(
        gap_table[None, None] >= 0, jnp.exp(-decay_rates[:, :, None, None] * gap_len), 0.0
    )
    start_states = jnp.einsum("uoab,buop->auop", carry_matrix, end_sums, precision=HIGHEST)
    response_local = response_local + jnp.einsum(
        "uob,nuop->nbup", scaled[:, :, None] * decays, start_states, precision=HIGHEST
    )
    remaining = (block_len * (block_count - 1 - block_index)).astype(jnp.float32)
    weights = jnp.exp(-decay_rates[:, :, None] * remaining)
    end_state = jnp.einsum("uob,buop->uop", weights, end_sums, precision=HIGHEST)
    return (response_local.reshape(length, filter_count, per_unit), end_state)


def body(
    stream_in,
    mr_features,
    mr_short,
    medium_taps,
    mr_out_weight,
    li_gain,
    li_in_weight,
    li_short,
    li_rates,
    li_residues,
):
    tok_rows = stream_in.shape[0]
    channels = mr_features.shape[2]
    filter_count = channels // GROUP
    tensor_rank = lax.axis_index("tensor")
    local_taps = lax.dynamic_slice_in_dim(medium_taps, tensor_rank * filter_count, filter_count, 1)
    rim_rows = MEDIUM + SHORT - 2
    border = shifted(mr_features[tok_rows - rim_rows :], "seq", 1)
    joined = jnp.concatenate([border, mr_features], axis=0)
    filtered_all = short_filter(joined[SHORT - 1 :], mr_short, joined[: SHORT - 1])
    extended = (filtered_all[:, 1] * filtered_all[:, 2]).astype(jnp.bfloat16)
    filtered = filtered_all[MEDIUM - 1 :]
    gated_mr = (filtered[:, 0] * medium_filter(extended, local_taps)).astype(jnp.bfloat16)
    partial_out = jnp.dot(
        gated_mr,
        lax.all_gather(mr_out_weight, "seq", axis=1, tiled=True),
        preferred_element_type=jnp.float32,
    )
    summed = lax.psum(partial_out, "tensor")
    stream = (stream_in.astype(jnp.float32) + summed).astype(jnp.bfloat16)
    normed = root_norm(stream, li_gain)
    shard_rows = lax.all_gather(li_in_weight, "seq", axis=0, tiled=True)
    running = jnp.dot(
        normed, shard_rows.reshape(shard_rows.shape[0], -1), preferred_element_type=jnp.float32
    )
    projected = running.astype(jnp.bfloat16).reshape(tok_rows, 3, channels)
    border = shifted(projected[tok_rows - (SHORT - 1) :], "seq", 1)
    filtered = short_filter(projected, li_short, border)
    product = (filtered[:, 1] * filtered[:, 2]).astype(jnp.bfloat16)
    scaled_all = li_residues * jnp.sqrt(2.0 * li_rates / ORDER)
    seq_count = lax.axis_size("seq")
    slice_width = channels // seq_count
    seq_rank = lax.axis_index("seq")
    regrouped = lax.all_to_all(product, "seq", split_axis=1, concat_axis=0, tiled=True)
    first_channel = tensor_rank * channels + seq_rank * slice_width
    unit_count = slice_width // GROUP
    per_unit = GROUP
    decay_rates = lax.dynamic_slice_in_dim(li_rates, first_channel // GROUP, unit_count, 0)
    scaled = lax.dynamic_slice_in_dim(scaled_all, first_channel // GROUP, unit_count, 0)
    length = regrouped.shape[0]
    response_local, unused = modal_conv(
        regrouped.astype(jnp.float32).reshape(length, unit_count, per_unit), decay_rates, scaled
    )
    response = lax.all_to_all(
        response_local.reshape(length, slice_width).astype(jnp.bfloat16),
        "seq",
        split_axis=0,
        concat_axis=1,
        tiled=True,
    )
    gated_li = (filtered[:, 0] * response.astype(jnp.float32)).astype(jnp.bfloat16)
    return (stream, gated_li)


def solution(mesh):
    placed = (
        P(("parts", "seq"), None),
        P(("parts", "seq"), None, "tensor"),
        P(None, None, "tensor"),
        P(),
        P("tensor", "seq"),
        P(),
        P("seq", None, "tensor"),
        P(None, None, "tensor"),
        P(),
        P(),
    )
    return jax.shard_map(
        body,
        mesh=mesh,
        in_specs=placed,
        out_specs=(P(("parts", "seq"), None), P(("parts", "seq"), "tensor")),
        check_vma=False,
    )
```

profile of v0, /device:TPU:0, one launch (start us, length us, event | category | flops | bytes accessed | tf_op | source)
XLA Modules:
  0.0 426.7 jit_solution(8751422622988055465)
XLA Ops:
  7.2 0.0 copy-start
  7.2 0.0 all-gather.3.cloned.1.call-start
  7.2 0.7 all-gather.3.cloned.1.call-update
  7.9 0.0 all-gather.5.cloned.1.call-start
  8.0 2.8 copy.63
  10.7 0.0 all-gather.5.cloned.1.call-update
  10.8 1.6 slice.130
  12.4 3.5 collective-permute-start
  15.9 3.2 copy.59
  19.1 0.7 fusion.74
  19.8 0.6 copy.128
  20.5 0.1 compare_select_fusion
  20.6 0.3 reshape.194
  21.0 60.8 %gather_fusion = f32[32640,128]{1,0:T(8,128)} fusion(f32[128,128]{0,1:T(8,128)S(1)} %bitcast.111, s32[32768]{0:T(1024)S(1)} %pad_clamp_fusion), kind=kCustom, calls=%fused_computation | custom fusion | bytes 33553920 | tf_op jit(solution)/shard_map/gather | solution.py:50
  81.7 13.8 %reshape.197 = f32[128,255,128]{2,1,0:T(8,128)} reshape(f32[32640,128]{1,0:T(8,128)} %gather_fusion) | data formatting | bytes 33423360 | tf_op jit(solution)/shard_map/gather | solution.py:50
  95.6 0.1 fusion.57
  95.7 12.6 %select_bitcast_fusion = f32[128,128,255,1]{0,2,1,3:T(8,128)} fusion(f32[128,255,128]{2,1,0:T(8,128)} %reshape.197, pred[128,255]{1,0:T(8,128)(4,1)S(1)} %fusion.57), kind=kLoop, calls=%fused_computation.2 | loop fusion | flops 4177920 | bytes 33456000 | tf_op jit(solution)/shard_map/jit(_where)/select_n | solution.py:50
  108.3 17.8 %copy.78 = f32[128,128,255,1]{2,1,3,0:T(8,128)} copy(f32[128,128,255,1]{0,2,1,3:T(8,128)} %select_bitcast_fusion) | data formatting | bytes 33423360 | tf_op jit(solution)/shard_map/jit(_where)/select_n | solution.py:50
  126.2 0.8 copy_bitcast_fusion.11
  127.0 0.7 fusion.73
  127.8 0.6 copy_bitcast_fusion.2
  128.4 0.9 slice.174
  129.3 1.6 copy.60
  131.0 4.4 %copy.58 = bf16[133,3,2048]{0,2,1:T(8,128)(2,1)} copy(bf16[133,3,2048]{2,0,1:T(8,128)(2,1)} %collective-permute-done) | data formatting | bytes 3268608 | tf_op jit(solution)/shard_map/ppermute | solution.py:20
  135.3 4.7 %fusion.9 = f32[389,3,2048]{0,2,1:T(8,128)S(1)} fusion(bf16[256,3,2048]{0,2,1:T(8,128)(2,1)S(1)} %copy.59, bf16[133,3,2048]{0,2,1:T(8,128)(2,1)} %copy.58, bf16[6,3,2048]{0,2,1:T(8,128)(2,1)} %copy.60), kind=kLoop, calls=%fused_computation.21 | loop fusion | flops 19120128 | bytes 14413824 | tf_op jit(solution)/shard_map/convert_element_type | solution.py:31
  140.1 22.2 %fusion.1 = f32[383,3,2048]{0,2,1:T(8,128)S(1)} fusion(f32[389,3,2048]{0,2,1:T(8,128)S(1)} %fusion.9, f32[3,2048]{1,0:T(4,128)S(1)} %get-tuple-element.28, f32[3,2048]{1,0:T(4,128)S(1)} %get-tuple-element.29, f32[3,2048]{1,0:T(4,128)S(1)} %get-tuple-element.30, f32[3,2048]{1,0:T(4,128)S(1)} %get-tuple-element.31, f32[3,2048]{1,0:T(4,128)S(1)} %get-tuple-element.32, ...), kind=kLoop, calls=%fused_computation.6 | loop fusion | flops 30590976 | bytes 75472896 | tf_op jit(solution)/shard_map/add | solution.py:35
  162.3 0.3 fusion.36
  162.6 0.3 fusion.72
  162.9 3.2 copy-done.2
  166.1 19.4 %fusion.33 = f32[2,128,128,16]{1,3,0,2:T(8,128)S(1)} fusion(f32[128,128,255,1]{2,1,3,0:T(8,128)} %copy.78, f32[1,255,128,16]{1,3,0,2:T(8,128)S(1)} %bitcast.116, f32[1,255,128,16]{1,3,0,2:T(8,128)S(1)} %bitcast.115), kind=kOutput, calls=%fused_computation.62 | convolution fusion | flops 1605365760 | bytes 22986752 | tf_op jit(solution)/shard_map/gts,nsgc->ntgc/dot_general | solution.py:58
  185.6 1.1 copy.62
  186.7 0.0 all-gather.3.cloned.1.call-done
  186.7 8.0 %fusion.22 = (f32[256]{0:T(256)S(1)}, bf16[256,2048]{1,0:T(8,128)(2,1)}) fusion(bf16[2048,2048]{1,0:T(8,128)(2,1)} %all-gather.3.cloned.1.call-done, f32[256,8,2,128]{3,2,1,0:T(2,128)S(1)} %bitcast.112, f32[383,3,2048]{0,2,1:T(8,128)} %copy-done.2, bf16[256,2048]{1,0:T(8,128)(2,1)S(1)} %copy-done.5), kind=kOutput, calls=%fused_computation.46 | convolution fusion | flops 2151677696 | bytes 14681088 | tf_op jit(solution)/shard_map/dot_general | solution.py:115
  194.7 40.5 %all-gather.5.cloned.1.call-done = bf16[2048,3,2048]{0,2,1:T(8,128)(2,1)} async-done(((bf16[128,3,2048]{0,2,1:T(8,128)(2,1)}), bf16[2048,3,2048]{0,2,1:T(8,128)(2,1)}) %all-gather.5.cloned.1.call-update) | async-done | bytes 25165840 | tf_op jit(solution)/shard_map/all_gather | solution.py:123
  235.2 12.1 %convolution_convert_fusion = bf16[256,6144]{1,0:T(8,128)(2,1)S(1)} fusion(bf16[2048,6144]{0,1:T(8,128)(2,1)} %bitcast.120, bf16[256,2048]{1,0:T(8,128)(2,1)} %get-tuple-element.27, f32[2048]{0:T(1024)S(1)} %copy-done.16, f32[256]{0:T(256)S(1)} %add_rsqrt_fusion), kind=kOutput, calls=%fused_computation.18 | convolution fusion | flops 6446120960 | bytes 29369344 | tf_op jit(solution)/shard_map/dot_general | solution.py:124
  247.3 0.7 slice.187
  248.0 2.2 collective-permute-start.1
  250.3 3.2 copy.65
  253.5 1.6 copy.66
  255.1 7.0 %maximum_convert_fusion = f32[262,3,2048]{0,2,1:T(8,128)} fusion(bf16[256,3,2048]{0,2,1:T(8,128)(2,1)S(1)} %bitcast.113, bf16[6,3,2048]{0,2,1:T(8,128)(2,1)} %copy.66), kind=kLoop, calls=%fused_computation.35 | loop fusion | flops 6438912 | bytes 9658368 | tf_op jit(solution)/shard_map/convert_element_type | solution.py:31
  262.1 37.4 %fusion.10 = f32[256,3,2048]{0,2,1:T(8,128)} fusion(f32[262,3,2048]{0,2,1:T(8,128)} %maximum_convert_fusion, f32[3,2048]{1,0:T(4,128)S(1)} %get-tuple-element.34, f32[3,2048]{1,0:T(4,128)S(1)} %get-tuple-element.35, f32[3,2048]{1,0:T(4,128)S(1)} %get-tuple-element.36, f32[3,2048]{1,0:T(4,128)S(1)} %copy-done.9, f32[3,2048]{1,0:T(4,128)S(1)} %get-tuple-element.38, ...), kind=kLoop, calls=%fused_computation.23 | loop fusion | flops 20447232 | bytes 50503680 | tf_op jit(solution)/shard_map/add | solution.py:35
  299.5 3.4 fusion.26
  302.9 4.2 all-to-all-start
  307.2 0.1 dynamic-slice_multiply_fusion
  307.2 0.1 copy.102
  307.3 0.1 copy.103
  307.4 0.1 fusion.63
  307.5 0.1 copy.82
  307.6 54.8 %gather_fusion.1 = f32[16384,8]{1,0:T(8,128)} fusion(f32[8,128]{0,1:T(8,128)S(1)} %copy.82, s32[16384]{0:T(1024)S(1)} %bitcast_clamp_fusion), kind=kCustom, calls=%fused_computation.1 | custom fusion | bytes 1114112 | tf_op jit(solution)/shard_map/gather | solution.py:70
  362.5 5.9 %copy.69 = f32[128,128,8]{1,0,2:T(8,128)} copy(f32[128,128,8]{2,1,0:T(8,128)} %bitcast.114) | data formatting | bytes 1048576 | tf_op jit(solution)/shard_map/gather | solution.py:70
  368.4 0.6 copy.67
  369.0 0.4 reshape_reshape.4
  369.4 1.1 convolution_bitcast_fusion
  370.5 2.0 copy.72
  372.5 5.7 %fusion.37 = f32[32,8,16,16]{0,3,2,1:T(8,128)} fusion(f32[32,8,16,16]{0,3,2,1:T(8,128)} %copy.72, f32[32,32]{1,0:T(8,128)S(1)} %multiply_convert_fusion, f32[8,16]{1,0:T(8,128)S(1)} %neg.7, pred[32,32]{1,0:T(8,128)(4,1)S(1)} %fusion.68), kind=kOutput, calls=%fused_computation.65 | convolution fusion | flops 25427968 | bytes 529920 | tf_op jit(solution)/shard_map/uoab,buop->auop/dot_general | solution.py:81
  378.2 2.2 copy.74
  380.5 2.0 fusion.58
  382.4 2.4 fusion.40
  384.8 0.3 copy.75
  385.1 0.4 convert_element_type.84
  385.5 0.3 copy.76
  385.9 30.6 %all_to_all.23 = bf16[16,256,128]{1,2,0:T(8,128)(2,1)S(1)} all-to-all(bf16[16,256,128]{1,2,0:T(8,128)(2,1)S(1)} %copy.76), channel_id=1, replica_groups=mesh['parts'=2,'seq'=16,'tensor'=1] {'seq'}, dimensions={0} | all-to-all | bytes 2097152 | tf_op jit(solution)/shard_map/all_to_all | solution.py:145
  416.5 1.9 fusion.28
  418.4 1.4 copy.77
  (49 shorter events, 0.3 us)
Async XLA Ops:
  7.2 13.8 %copy-start = (f32[128,128]{1,0:T(8,128)S(1)}, f32[128,128]{1,0:T(8,128)}, u32[]{:S(2)}) copy-start(f32[128,128]{1,0:T(8,128)} %param.13) | copy-start | bytes 196612
  7.2 3.6 copy-start.3
  7.2 179.5 %all-gather.3.cloned.1.call-start = ((), (), s32[]{:S(2)}) async-start(), calls=%async_computation.2 | async-start | bytes 8912896 | tf_op jit(solution)/shard_map/all_gather | solution.py:117
  7.9 227.3 %all-gather.5.cloned.1.call-start = ((), (), s32[]{:S(2)}) async-start(), calls=%async_computation.3 | async-start | bytes 26738688 | tf_op jit(solution)/shard_map/all_gather | solution.py:123
  10.7 8.3 %copy-start.6 = (f32[7,3,2048]{2,0,1:T(8,128)S(1)}, f32[7,3,2048]{2,0,1:T(8,128)}, u32[]{:S(2)}) copy-start(f32[7,3,2048]{2,0,1:T(8,128)} %param.12) | copy-start | bytes 516100
  12.4 116.1 %collective-permute-start = (bf16[133,3,2048]{2,0,1:T(8,128)(2,1)}, bf16[133,3,2048]{2,0,1:T(8,128)(2,1)}, u32[]{:S(2)}, u32[]{:S(2)}) collective-permute-start(bf16[133,3,2048]{2,0,1:T(8,128)(2,1)} %slice.130), channel_id=1, source_target_pairs={{0,1},{1,2},{2,3},{3,4},{4,5},{5,6},{6,7},{7,8},{8,9},{9,10},{10,1... | collective-permute-start | bytes 4902920 | tf_op jit(solution)/shard_map/ppermute | solution.py:20
  108.3 17.8 %copy-start.13 = (f32[1,3,2048]{2,0,1:T(1,128)S(1)}, f32[1,3,2048]{2,0,1:T(1,128)}, u32[]{:S(2)}) copy-start(f32[1,3,2048]{2,0,1:T(1,128)} %get-tuple-element.23) | copy-start | bytes 73732
  108.3 18.7 %copy-start.7 = (f32[7,3,2048]{2,0,1:T(8,128)S(1)}, f32[7,3,2048]{2,0,1:T(8,128)}, u32[]{:S(2)}) copy-start(f32[7,3,2048]{2,0,1:T(8,128)} %param.17) | copy-start | bytes 516100
  135.3 4.7 %copy-start.8 = (f32[1,3,2048]{2,1,0:T(4,128)S(1)}, f32[1,3,2048]{2,1,0:T(4,128)}, u32[]{:S(2)}) copy-start(f32[1,3,2048]{2,1,0:T(4,128)} %copy.128) | copy-start | bytes 73732
  162.3 3.9 copy-start.2
  166.1 20.5 %copy-start.5 = (bf16[256,2048]{1,0:T(8,128)(2,1)S(1)}, bf16[256,2048]{1,0:T(8,128)(2,1)}, u32[]{:S(2)}) copy-start(bf16[256,2048]{1,0:T(8,128)(2,1)} %param.10) | copy-start | bytes 3145732
  186.7 48.5 %copy-start.16 = (f32[2048]{0:T(1024)S(1)}, f32[2048]{0:T(1024)}, u32[]{:S(2)}) copy-start(f32[2048]{0:T(1024)} %param.15) | copy-start | bytes 24580
  235.2 15.0 %copy-start.11 = (f32[1,3,2048]{2,0,1:T(1,128)S(1)}, f32[1,3,2048]{2,0,1:T(1,128)}, u32[]{:S(2)}) copy-start(f32[1,3,2048]{2,0,1:T(1,128)} %get-tuple-element.13) | copy-start | bytes 73732
  235.2 15.0 %copy-start.12 = (f32[1,3,2048]{2,0,1:T(1,128)S(1)}, f32[1,3,2048]{2,0,1:T(1,128)}, u32[]{:S(2)}) copy-start(f32[1,3,2048]{2,0,1:T(1,128)} %get-tuple-element.14) | copy-start | bytes 73732
  235.2 15.1 %copy-start.10 = (f32[1,3,2048]{2,0,1:T(1,128)S(1)}, f32[1,3,2048]{2,0,1:T(1,128)}, u32[]{:S(2)}) copy-start(f32[1,3,2048]{2,0,1:T(1,128)} %get-tuple-element.10) | copy-start | bytes 73732
  247.3 3.0 copy-start.4
  248.0 5.4 %collective-permute-start.1 = (bf16[6,3,2048]{2,0,1:T(8,128)(2,1)}, bf16[6,3,2048]{2,0,1:T(8,128)(2,1)S(1)}, u32[]{:S(2)}, u32[]{:S(2)}) collective-permute-start(bf16[6,3,2048]{2,0,1:T(8,128)(2,1)} %bitcast.8), channel_id=1, source_target_pairs={{0,1},{1,2},{2,3},{3,4},{4,5},{5,6},{6,7},{7,8},{8,9},{9,10},{10,1... | collective-permute-start | bytes 221192 | tf_op jit(solution)/shard_map/ppermute | solution.py:20
  255.1 7.0 %copy-start.9 = (f32[3,2048]{1,0:T(4,128)S(1)}, f32[3,2048]{1,0:T(4,128)}, u32[]{:S(2)}) copy-start(f32[3,2048]{1,0:T(4,128)} %get-tuple-element.37) | copy-start | bytes 73732
  299.5 7.6 %copy-start.14 = (f32[128,16]{0,1:T(8,128)S(1)}, f32[128,16]{0,1:T(8,128)}, u32[]{:S(2)}) copy-start(f32[128,16]{0,1:T(8,128)} %param.19) | copy-start | bytes 24580
  299.5 7.6 %copy-start.15 = (f32[128,16]{0,1:T(8,128)S(1)}, f32[128,16]{0,1:T(8,128)}, u32[]{:S(2)}) copy-start(f32[128,16]{0,1:T(8,128)} %param.18) | copy-start | bytes 24580
  302.9 65.4 %all-to-all-start = ((bf16[256,16,128]{0,2,1:T(8,128)(2,1)}), bf16[256,16,128]{0,2,1:T(8,128)(2,1)S(1)}, u32[]{:S(2)}, u32[]{:S(2)}) async-start(bf16[256,16,128]{0,2,1:T(8,128)(2,1)} %bitcast.11), calls=%async_computation | async-start | bytes 2097152 | tf_op jit(solution)/shard_map/all_to_all | solution.py:135
  384.8 35.0 %copy-start.1 = (f32[128,128]{1,0:T(8,128)S(1)}, f32[128,128]{1,0:T(8,128)}, u32[]{:S(2)}) copy-start(f32[128,128]{1,0:T(8,128)} %param.13) | copy-start | bytes 196612
Sparse Core Ops, SparseCore 0:
  10.2 88.2 all-gather.2
  100.0 135.1 all-gather.4
where the time goes:
time: 428 us; the launch traced here: 427 us
  local copies, waits for them, and re-layouts  190 us (44%)
  other arithmetic  90.1 us (21%)
  matrix products  50.6 us (12%)
  waiting for transfers between devices  41.2 us (10%)
  blocking collectives  30.6 us (7%)
  between operations  14.5 us (3%)
  starting transfers between devices  9.95 us (2%)
    gather x2, local copies, waits for them, and re-layouts, medium_filter(): filter_taps.T[:, jnp.clip(lag_table, 0, MEDIUM - 1)]  74.6 us
    gather x2, local copies, waits for them, and re-layouts, modal_conv(): kernel[:, jnp.maximum(lag_table, 0)]  60.7 us
    add x2, other arithmetic, short_filter(): running + filter_taps[lagged] * extended[SHORT - 1 - lagged:SHORT - 1 - l...  59.6 us
    all_gather x1, waiting for transfers between devices, body(): shard_rows = lax.all_gather(li_in_weight, 'seq', axis=0, tiled=True)  40.5 us
    all_to_all x1, blocking collectives, body(): lax.all_to_all(response_local.reshape(length, slice_width).astype(jnp.bfl...  30.6 us
    dot_general x1, matrix products, medium_filter(): jnp.einsum('gts,nsgc->ntgc', band_matrix, windows, precision=HIGHEST)  19.4 us
    select_n x1, local copies, waits for them, and re-layouts, medium_filter(): jnp.where(inside[None], filter_taps.T[:, jnp.clip(lag_table, 0, MEDIUM -...  17.8 us
    unnamed x47, local copies, waits for them, and re-layouts  13 us
  transfers between devices with their start and end apart: 5, of which 1 were waited for; matrix products, arithmetic and copies ran while one was open for 57% of the time, Pallas kernels for 0%

commit v1 on v0

v1 whole, which is shorter than its diff:
```python
import functools

import jax
import jax.numpy as jnp
from jax import lax
from jax.experimental import pallas as pl
from jax.experimental.pallas import tpu as pltpu
from jax.sharding import PartitionSpec as P

GROUP = 16
ORDER = 16
SHORT = 7
MEDIUM = 128
BLK = 128
LANES = 128
PER = LANES // GROUP
RIM = 16
bf16 = jnp.bfloat16
f32 = jnp.float32


def cost(flops, nbytes):
    return pl.CostEstimate(flops=flops, bytes_accessed=nbytes, transcendentals=0)


def params():
    return pltpu.CompilerParams(vmem_limit_bytes=40 * 1024 * 1024)


def toeplitz_kernel(base_ref, out_ref):
    row = lax.broadcasted_iota(jnp.int32, (BLK, 2 * BLK), 0)
    col = lax.broadcasted_iota(jnp.int32, (BLK, 2 * BLK), 1)
    causal = col <= row + BLK
    for g in range(PER):
        wide = jnp.broadcast_to(base_ref[g : g + 1, :], (BLK, 2 * BLK))
        rolled = pltpu.roll(wide, 0, 1, stride=1, stride_axis=0)
        out_ref[g * BLK : (g + 1) * BLK, :] = jnp.where(causal, rolled, 0.0).astype(bf16)


def toeplitz(kernel_taps):
    filters = kernel_taps.shape[0]
    base = jnp.roll(kernel_taps[:, ::-1], BLK + 1, axis=1)
    return pl.pallas_call(
        toeplitz_kernel,
        grid=(filters // PER,),
        in_specs=[pl.BlockSpec((PER, 2 * BLK), lambda i: (i, 0))],
        out_specs=pl.BlockSpec((PER * BLK, 2 * BLK), lambda i: (i, 0)),
        out_shape=jax.ShapeDtypeStruct((filters * BLK, 2 * BLK), bf16),
        compiler_params=params(),
        cost_estimate=cost(0, filters * BLK * 2 * BLK * 4),
        name="toeplitz",
    )(base)


def pick(result):
    lane = lax.broadcasted_iota(jnp.int32, (BLK, 2 * LANES), 1) % LANES // GROUP
    total = result[:BLK]
    for g in range(1, PER):
        total = jnp.where(lane == g, result[g * BLK : (g + 1) * BLK], total)
    return total


def two_blocks(table, before, first, second):
    wide = jnp.concatenate(
        [jnp.concatenate([before, first], axis=0), jnp.concatenate([first, second], axis=0)], axis=1
    )
    result = pick(jnp.dot(table, wide, preferred_element_type=f32))
    return result[:, :LANES], result[:, LANES:]


def fir(values, taps, start, length):
    total = taps[0:1] * values[start : start + length]
    for lagged in range(1, SHORT):
        total = total + taps[lagged : lagged + 1] * values[start - lagged : start - lagged + length]
    return total


def medium_kernel(x_ref, taps_ref, table_ref, out_ref):
    rows = x_ref.shape[1]
    own = rows - BLK - RIM
    feats = [x_ref[i].astype(f32) for i in range(3)]
    q = fir(feats[0], taps_ref[0], BLK + RIM, own)
    k = fir(feats[1], taps_ref[1], RIM, own + BLK)
    v = fir(feats[2], taps_ref[2], RIM, own + BLK)
    product = (k * v).astype(bf16)
    table = table_ref[...]
    for n in range(0, own // BLK, 2):
        part = [product[(n + j) * BLK : (n + j + 1) * BLK] for j in range(3)]
        y0, y1 = two_blocks(table, *part)
        out_ref[n * BLK : (n + 1) * BLK] = (q[n * BLK : (n + 1) * BLK] * y0).astype(bf16)
        out_ref[(n + 1) * BLK : (n + 2) * BLK] = (q[(n + 1) * BLK : (n + 2) * BLK] * y1).astype(bf16)


def medium(extended, taps, table):
    _, rows, channels = extended.shape
    own = rows - BLK - RIM
    return pl.pallas_call(
        medium_kernel,
        grid=(channels // LANES,),
        in_specs=[
            pl.BlockSpec((3, rows, LANES), lambda i: (0, 0, i)),
            pl.BlockSpec((3, SHORT, LANES), lambda i: (0, 0, i)),
            pl.BlockSpec((PER * BLK, 2 * BLK), lambda i: (i, 0)),
        ],
        out_specs=pl.BlockSpec((own, LANES), lambda i: (0, i)),
        out_shape=jax.ShapeDtypeStruct((own, channels), bf16),
        compiler_params=params(),
        cost_estimate=cost(channels // LANES * 2 * 1024 * 256 * 256, 16 * 2**20),
        name="medium",
    )(extended, taps, table)


def product_kernel(segs, k_ref, v_ref, taps_ref, high_ref, low_ref, product_ref, state_ref):
    rows = k_ref.shape[1] - RIM
    seg = rows // segs
    k = fir(k_ref[0].astype(f32), taps_ref[1], RIM, rows)
    v = fir(v_ref[0].astype(f32), taps_ref[2], RIM, rows)
    product = (k * v).astype(bf16)
    product_ref[0] = product
    lane = lax.broadcasted_iota(jnp.int32, (ORDER, LANES), 1) // GROUP
    for s in range(segs):
        part = product[s * seg : (s + 1) * seg]
        sums = jnp.dot(high_ref[...], part, preferred_element_type=f32) + jnp.dot(
            low_ref[...], part, preferred_element_type=f32
        )
        total = sums[:ORDER]
        for g in range(1, PER):
            total = jnp.where(lane == g, sums[g * ORDER : (g + 1) * ORDER], total)
        state_ref[0, s] = total


def local_kernel(segs, q_ref, taps_ref, product_ref, table_ref, q_out, y_out):
    rows = q_ref.shape[1] - RIM
    seg = rows // segs
    q_out[0] = fir(q_ref[0].astype(f32), taps_ref[0], RIM, rows)
    zeros = jnp.zeros((BLK, LANES), bf16)
    table = table_ref[...]
    for s in range(segs):
        first = product_ref[0, s * seg : s * seg + BLK]
        second = product_ref[0, s * seg + BLK : (s + 1) * seg]
        y0, y1 = two_blocks(table, zeros, first, second)
        y_out[0, s * seg : s * seg + BLK] = y0
        y_out[0, s * seg + BLK : (s + 1) * seg] = y1


def finish_kernel(segs, q_ref, y_ref, state_ref, high_ref, low_ref, out_ref):
    seg = q_ref.shape[1] // segs
    row = lax.broadcasted_iota(jnp.int32, (LANES, LANES), 0) // ORDER
    lane = lax.broadcasted_iota(jnp.int32, (LANES, LANES), 1) // GROUP
    for s in range(segs):
        state = jnp.concatenate([state_ref[0, s]] * PER, axis=0)
        state = jnp.where(row == lane, state, 0.0)
        state_high = state.astype(bf16)
        state_low = (state - state_high.astype(f32)).astype(bf16)
        at = slice(s * seg, (s + 1) * seg)
        y = y_ref[0, at]
        y = y + jnp.dot(high_ref[...], state_high, preferred_element_type=f32)
        y = y + jnp.dot(high_ref[...], state_low, preferred_element_type=f32)
        y = y + jnp.dot(low_ref[...], state_high, preferred_element_type=f32)
        out_ref[0, at] = (q_ref[0, at] * y.astype(bf16).astype(f32)).astype(bf16)


def long_product(projected, taps, high, low, segs):
    groups, rows, channels = projected.shape
    channels //= 3
    blocks = channels // LANES
    own = rows - RIM
    seg = own // segs
    return pl.pallas_call(
        functools.partial(product_kernel, segs),
        grid=(blocks, groups),
        in_specs=[
            pl.BlockSpec((1, rows, LANES), lambda i, x: (x, 0, blocks + i)),
            pl.BlockSpec((1, rows, LANES), lambda i, x: (x, 0, 2 * blocks + i)),
            pl.BlockSpec((3, SHORT, LANES), lambda i, x: (0, 0, i)),
            pl.BlockSpec((PER * ORDER, seg), lambda i, x: (i, 0)),
            pl.BlockSpec((PER * ORDER, seg), lambda i, x: (i, 0)),
        ],
        out_specs=[
            pl.BlockSpec((1, own, LANES), lambda i, x: (x, 0, i)),
            pl.BlockSpec((1, segs, ORDER, LANES), lambda i, x: (x, 0, 0, i)),
        ],
        out_shape=[
            jax.ShapeDtypeStruct((groups, own, channels), bf16),
            jax.ShapeDtypeStruct((groups, segs, ORDER, channels), f32),
        ],
        compiler_params=params(),
        cost_estimate=cost(2**28, 8 * 2**20),
        name="product",
    )(projected, projected, taps, high, low)


def long_local(projected, taps, product, table, segs):
    groups, rows, channels = projected.shape
    channels //= 3
    own = rows - RIM
    whole = pl.BlockSpec((1, own, LANES), lambda i, x: (x, 0, i))
    return pl.pallas_call(
        functools.partial(local_kernel, segs),
        grid=(channels // LANES, groups),
        in_specs=[
            pl.BlockSpec((1, rows, LANES), lambda i, x: (x, 0, i)),
            pl.BlockSpec((3, SHORT, LANES), lambda i, x: (0, 0, i)),
            whole,
            pl.BlockSpec((PER * BLK, 2 * BLK), lambda i, x: (i, 0)),
        ],
        out_specs=[whole, whole],
        out_shape=[jax.ShapeDtypeStruct((groups, own, channels), f32)] * 2,
        compiler_params=params(),
        cost_estimate=cost(2**31, 16 * 2**20),
        name="local",
    )(projected, taps, product, table)


def long_finish(q, y, state, high, low, segs):
    groups, own, channels = q.shape
    seg = own // segs
    whole = pl.BlockSpec((1, own, LANES), lambda i, x: (x, 0, i))
    decay = pl.BlockSpec((seg, PER * ORDER), lambda i, x: (0, i))
    return pl.pallas_call(
        functools.partial(finish_kernel, segs),
        grid=(channels // LANES, groups),
        in_specs=[
            whole,
            whole,
            pl.BlockSpec((1, segs, ORDER, LANES), lambda i, x: (x, 0, 0, i)),
            decay,
            decay,
        ],
        out_specs=whole,
        out_shape=jax.ShapeDtypeStruct((groups, own, channels), bf16),
        compiler_params=params(),
        cost_estimate=cost(2**28, 8 * 2**20),
        name="finish",
    )(q, y, state, high, low)


def split_high_low(value):
    high = lax.reduce_precision(value, 8, 7)
    return high.astype(bf16), (value - high).astype(bf16)


def shift_seq(value, steps):
    count = lax.axis_size("seq")
    return lax.ppermute(value, "seq", [(s, s + steps) for s in range(count - steps)])


def pair_stack(mine, other, index):
    first = index == 0
    return jnp.stack([jnp.where(first, mine, other), jnp.where(first, other, mine)])


def ring_order(chips):
    if chips % 2:
        return list(range(chips))
    return list(range(0, chips, 2)) + list(range(chips - 1, 0, -2))


def ring_gather(up, down, cores, after=None):
    count = lax.axis_size("seq")
    chips = count // cores
    order = ring_order(chips)
    spot = [order.index(chip) for chip in range(chips)]
    chip = lax.axis_index("seq") // cores
    place = jnp.asarray(spot, jnp.int32)[chip]
    lookup = jnp.asarray(order, jnp.int32)

    def perm(step):
        return [
            (order[a] * cores + c, order[(a + step) % chips] * cores + c)
            for a in range(chips)
            for c in range(cores)
        ]

    def put(store, piece, owner):
        return lax.dynamic_update_slice_in_dim(store, piece[None], owner, 0)

    both = [jnp.zeros((chips,) + up.shape, up.dtype), jnp.zeros((chips,) + down.shape, down.dtype)]
    both = [put(both[0], up, chip), put(both[1], down, chip)]
    for step in range(1, chips):
        up = lax.ppermute(up, "seq", perm(1))
        down = lax.ppermute(down, "seq", perm(-1))
        both[0] = put(both[0], up, lookup[(place - step) % chips])
        both[1] = put(both[1], down, lookup[(place + step) % chips])
    return both, up, down


def body(
    stream_in,
    mr_features,
    mr_short,
    medium_taps,
    mr_out_weight,
    li_gain,
    li_in_weight,
    li_short,
    li_rates,
    li_residues,
):
    rows = stream_in.shape[0]
    width = stream_in.shape[1]
    channels = mr_features.shape[2]
    tensors = lax.axis_size("tensor")
    cores = 2 if tensors == 1 and lax.axis_size("seq") % 4 == 0 else 1
    wide = 2 if cores == 2 and lax.axis_size("parts") == 2 else 1
    share = cores * wide
    count = lax.axis_size("seq")
    chips = count // cores
    seq_rank = lax.axis_index("seq")
    core = seq_rank % cores
    side = lax.axis_index("parts") if wide == 2 else 0
    tensor_rank = lax.axis_index("tensor")
    swap_pairs = [(s, s ^ 1) for s in range(count)]

    def swap_core(value):
        return lax.ppermute(value, "seq", swap_pairs)

    def swap_side(value):
        return lax.ppermute(value, "parts", [(0, 1), (1, 0)])

    part = channels // share
    quarter = side * cores + core
    filters = part // GROUP
    first_filter = tensor_rank * (channels // GROUP) + quarter * filters

    rim = shift_seq(jnp.transpose(mr_features[rows - BLK - RIM :], (1, 0, 2)), 1)
    extended = jnp.concatenate([rim, jnp.transpose(mr_features, (1, 0, 2))], axis=1)

    if cores == 2:
        half = width // 2
        out_stacks, last_up, last_down = ring_gather(
            mr_out_weight[: channels // 2], mr_out_weight[channels // 2 :], cores
        )
        weight = li_in_weight.reshape(-1, 3, share, part)
        mine = lax.dynamic_index_in_dim(weight, side * cores + core, 2, keepdims=False)
        theirs = lax.dynamic_index_in_dim(weight, side * cores + 1 - core, 2, keepdims=False)
        mine = mine.reshape(-1, 3 * part)
        other = swap_core(theirs.reshape(-1, 3 * part))
        halves = pair_stack(mine, other, core)
        up, down, last_up, last_down = lax.optimization_barrier(
            (halves[0], halves[1], last_up, last_down)
        )
        in_stacks, _, _ = ring_gather(up, down, cores)
        in_weight = jnp.stack(in_stacks, axis=1).reshape(width, 3 * part)
    else:
        out_weight = lax.all_gather(mr_out_weight, "seq", axis=1, tiled=True)
        in_weight = lax.all_gather(li_in_weight, "seq", axis=0, tiled=True).reshape(width, -1)

    local_taps = lax.dynamic_slice_in_dim(
        medium_taps, tensor_rank * (channels // GROUP), channels // GROUP, 1
    )
    medium_table = toeplitz(jnp.pad(local_taps.T, ((0, 0), (0, 2 * BLK - MEDIUM))))
    rates = lax.dynamic_slice_in_dim(li_rates, first_filter, filters, 0)
    residues = lax.dynamic_slice_in_dim(li_residues, first_filter, filters, 0)
    scaled = residues * jnp.sqrt(2.0 * rates / ORDER)
    steps = jnp.arange(rows, dtype=f32)
    spread = scaled.reshape(1, -1) * jnp.exp(-rates.reshape(1, -1) * steps[:, None])
    long_table = toeplitz(jnp.sum(spread.reshape(rows, filters, ORDER), axis=-1).T)
    spread_high, spread_low = split_high_low(spread)
    tail = jnp.exp(-rates.reshape(-1, 1) * (rows - steps)[None, :])
    tail_high, tail_low = split_high_low(tail)
    by_channel = jnp.repeat(rates.T, GROUP, axis=1)
    seg_decay = jnp.exp(-by_channel * rows)
    gap_decays = [jnp.exp(-by_channel * (rows * cores * gap)) for gap in range(chips - 1)]
    short_part = lax.dynamic_slice_in_dim(li_short, quarter * part, part, 2)
    short_part = jnp.transpose(short_part, (1, 0, 2))

    gated = medium(extended, jnp.transpose(mr_short, (1, 0, 2)), medium_table)

    if cores == 2:
        both = pair_stack(gated, swap_core(gated), core).reshape(cores * rows, channels)
        update = sum(
            jnp.einsum(
                "rk,jkn->jrn",
                both[:, i * channels // 2 : (i + 1) * channels // 2],
                out_stacks[i],
                preferred_element_type=f32,
            )
            for i in range(2)
        )
        update = update.reshape(chips, cores, rows, -1)
        mine = lax.dynamic_index_in_dim(update, core, 1, keepdims=False)
        theirs = lax.dynamic_index_in_dim(update, 1 - core, 1, keepdims=False)
        update = pair_stack(mine, swap_core(theirs), core)
        summed = jnp.transpose(update, (2, 1, 0, 3)).reshape(rows, width)
    else:
        summed = lax.psum(jnp.dot(gated, out_weight, preferred_element_type=f32), "tensor")
    stream = (stream_in.astype(f32) + summed).astype(bf16)
    widened = stream.astype(f32)
    mean_square = jnp.mean(widened * widened, axis=-1, keepdims=True)
    normed = (widened * lax.rsqrt(mean_square + 1e-06) * li_gain).astype(bf16)

    rows_all = normed[None]
    if wide == 2:
        rows_all = pair_stack(normed, swap_side(normed), side)
    if cores == 2:
        rows_all = pair_stack(rows_all, swap_core(rows_all), core)
        rows_all = jnp.transpose(rows_all, (1, 0, 2, 3)).reshape(wide, cores * rows, width)
    ahead = shift_seq(rows_all[:, cores * rows - RIM :], cores)
    rows_all = jnp.concatenate([ahead, rows_all], axis=1)
    projected = jnp.dot(
        rows_all.reshape(-1, width), in_weight, preferred_element_type=f32
    ).astype(bf16)
    projected = projected.reshape(wide, RIM + cores * rows, 3 * part)

    product, added = long_product(projected, short_part, tail_high, tail_low, cores)
    state = added[:, 0]
    for seg in range(1, cores):
        state = state * seg_decay + added[:, seg]
    start = 0.0
    for gap in range(1, chips):
        start = start + gap_decays[gap - 1] * shift_seq(state, gap * cores)
    starts = [start]
    for seg in range(1, cores):
        starts.append(starts[-1] * seg_decay + added[:, seg - 1])
    q, y = long_local(projected, short_part, product, long_table, cores)
    gated_li = long_finish(q, y, jnp.stack(starts, axis=1), spread_high, spread_low, cores)

    result = gated_li
    if wide == 2:
        mine = lax.dynamic_index_in_dim(result, side, 0, keepdims=False)
        theirs = lax.dynamic_index_in_dim(result, 1 - side, 0, keepdims=False)
        result = pair_stack(mine, swap_side(theirs), side)
    if cores == 2:
        result = result.reshape(wide, cores, rows, part)
        mine = lax.dynamic_index_in_dim(result, core, 1, keepdims=False)
        theirs = lax.dynamic_index_in_dim(result, 1 - core, 1, keepdims=False)
        result = pair_stack(mine, swap_core(theirs), core)
        result = jnp.transpose(result, (2, 1, 0, 3)).reshape(rows, channels)
    else:
        result = result.reshape(rows, channels)
    return (stream, result)


def solution(mesh):
    placed = (
        P(("parts", "seq"), None),
        P(("parts", "seq"), None, "tensor"),
        P(None, None, "tensor"),
        P(),
        P("tensor", "seq"),
        P(),
        P("seq", None, "tensor"),
        P(None, None, "tensor"),
        P(),
        P(),
    )
    return jax.shard_map(
        body,
        mesh=mesh,
        in_specs=placed,
        out_specs=(P(("parts", "seq"), None), P(("parts", "seq"), "tensor")),
        check_vma=False,
    )
```

time: 428 us -> 366 us (0.86)
  local copies, waits for them, and re-layouts: 190 us -> 124 us
  starting transfers between devices: 9.95 us -> 74.3 us
  other arithmetic: 90.1 us -> 30 us
  matrix products: 50.6 us -> 12.6 us
  Pallas kernels: 0 us -> 32.3 us
  blocking collectives: 30.6 us -> 0 us
  between operations: 14.5 us -> 37.4 us
  waiting for transfers between devices: 41.2 us -> 51.6 us
    gather x4 -> x0, local copies, waits for them, and re-layouts: 135 us -> none  [the longest x2 74.6 us: medium_filter(): filter_taps.T[:, jnp.clip(lag_table, 0, MEDIUM - 1)]]
    ppermute x2 -> x44, starting transfers between devices: 5.7 us -> 74.3 us  [the longest x14 26.5 us: ring_gather(): up = lax.ppermute(up, 'seq', perm(1))]
    add x3 -> x1, other arithmetic: 59.6 us -> 0.68 us  [body(): state = state * seg_decay + added[:, seg]]
    ppermute x2 -> x44, waiting for transfers between devices: 0.01 us -> 51.6 us  [the longest x14 31.7 us: ring_gather(): up = lax.ppermute(up, 'seq', perm(1))]
    all_gather x2 -> x0, waiting for transfers between devices: 40.5 us -> none  [the longest x1 40.5 us: body(): shard_rows = lax.all_gather(li_in_weight, 'seq', axis=0, tiled=True)]
    dot_general x7 -> x3, matrix products: 50.6 us -> 12.6 us  [the longest x1 7.13 us: body(): jnp.dot(rows_all.reshape(-1, width), in_weight, preferred_element_type=f32)]
    pallas_call x0 -> x6, Pallas kernels: none -> 32.3 us  [the longest x1 12.8 us: medium(): pl.pallas_call(medium_kernel, grid=(channels // LANES,), in_specs=[pl.Blo...]
    all_to_all x1 -> x0, blocking collectives: 30.6 us -> none  [body(): lax.all_to_all(response_local.reshape(length, slice_width).astype(jnp.bfl...]
  transfers between devices with their start and end apart: 5 -> 44, of which waited for: 1 -> 12; matrix products, arithmetic and copies ran while one was open for 57% -> 34% of each run, Pallas kernels for 0% -> 6%
where the time goes in v1:
time: 366 us; the launch traced here: 363 us
  local copies, waits for them, and re-layouts  124 us (34%)
  starting transfers between devices  74.3 us (20%)
  waiting for transfers between devices  51.6 us (14%)
  between operations  37.4 us (10%)
  Pallas kernels  32.3 us (9%)
  other arithmetic  30 us (8%)
  matrix products  12.6 us (3%)
    ppermute x14, waiting for transfers between devices, ring_gather(): up = lax.ppermute(up, 'seq', perm(1))  31.7 us
    unnamed x107, local copies, waits for them, and re-layouts  28.9 us
    ppermute x14, starting transfers between devices, ring_gather(): up = lax.ppermute(up, 'seq', perm(1))  26.5 us
    another operation x18, local copies, waits for them, and re-layouts, body(): in_weight = jnp.stack(in_stacks, axis=1).reshape(width, 3 * part)  24.8 us
    ppermute x9, starting transfers between devices, shift_seq(): lax.ppermute(value, 'seq', [(s, s + steps) for s in range(count - steps)])  23.4 us
    dynamic_update_slice x31, local copies, waits for them, and re-layouts, put(): return lax.dynamic_update_slice_in_dim(store, piece[None], owner, 0)  20.7 us
    pallas_call x1, Pallas kernels, medium(): pl.pallas_call(medium_kernel, grid=(channels // LANES,), in_specs=[pl.Blo...  12.8 us
    broadcast_in_dim x16, local copies, waits for them, and re-layouts, put(): return lax.dynamic_update_slice_in_dim(store, piece[None], owner, 0)  12.7 us
  transfers between devices with their start and end apart: 44, of which 12 were waited for; matrix products, arithmetic and copies ran while one was open for 34% of the time, Pallas kernels for 6%

profile of v1, /device:TPU:0, one launch (start us, length us, event | category | flops | bytes accessed | tf_op | source)
XLA Modules:
  0.0 362.7 jit_solution(7321472451426599015)
XLA Ops:
  0.6 2.1 fusion.18
  2.8 3.0 collective-permute-start.9
  5.7 2.9 slice_bitcast_fusion
  8.6 2.7 collective-permute-start.7
  13.0 2.3 collective-permute-start.20
  18.0 1.6 broadcast.158.clone.1
  21.5 1.6 collective-permute-start.1
  24.2 5.4 %collective-permute-done.10 = bf16[1024,128]{1,0:T(8,128)(2,1)} collective-permute-done((bf16[1024,128]{1,0:T(8,128)(2,1)}, bf16[1024,128]{1,0:T(8,128)(2,1)}, u32[]{:S(2)}, u32[]{:S(2)}) %collective-permute-start.10) | collective-permute-done | bytes 262176 | tf_op jit(solution)/shard_map/ppermute | solution.py:282
  29.6 1.5 collective-permute-start.11
  60.1 3.5 toeplitz.2.table_ref
  63.6 3.3 copy-done.2
  66.9 2.3 copy.118
  84.4 1.5 collective-permute-start.12
  92.7 7.8 %collective-permute-start.4 = (bf16[1024,128]{1,0:T(8,128)(2,1)}, bf16[1024,128]{1,0:T(8,128)(2,1)}, u32[]{:S(2)}, u32[]{:S(2)}) collective-permute-start(bf16[1024,128]{1,0:T(8,128)(2,1)} %collective-permute-done.3), channel_id=1, source_target_pairs={{0,4},{1,5},{4,8},{5,9},{8,12},{9,13},{12,14},{13,15},{14,10},{15,... | collective-permute-start | bytes 786440 | tf_op jit(solution)/shard_map/ppermute | solution.py:281
  100.5 3.2 pad_maximum_fusion.1.x_ref
  103.8 3.4 copy-done.3
  107.1 12.8 %medium.1 = bf16[256,2048]{1,0:T(8,128)(2,1)S(1)} custom-call(bf16[3,400,2048]{2,1,0:T(8,128)(2,1)S(1)} %pad_maximum_fusion.1.x_ref, f32[3,7,2048]{2,1,0:T(8,128)S(1)} %bitcast.186, bf16[16384,256]{1,0:T(8,128)(2,1)S(1)} %copy-done.3), custom_call_target="tpu_custom_call" | custom-call | flops 2147483648 | bytes 16777216 | tf_op jit(solution)/shard_map/medium/pallas_call | solution.py:97
  120.0 9.1 %collective-permute-start.8 = (bf16[256,2048]{1,0:T(8,128)(2,1)S(1)}, bf16[256,2048]{1,0:T(8,128)(2,1)}, u32[]{:S(2)}, u32[]{:S(2)}) collective-permute-start(bf16[256,2048]{1,0:T(8,128)(2,1)S(1)} %medium.1), channel_id=1, source_target_pairs={{0,1},{1,0},{2,3},{3,2},{4,5},{5,4},{6,7},{7,6},{8,9},{9,8},{10,11... | collective-permute-start | bytes 3145736 | tf_op jit(solution)/shard_map/ppermute | solution.py:316
  131.3 1.8 collective-permute-start.5
  139.8 2.1 collective-permute-start.6
  144.3 3.5 collective-permute-done.15
  153.8 4.2 %add_bitcast_fusion = f32[8,512,128]{1,2,0:T(8,128)} fusion(f32[8,128,512]{2,1,0:T(8,128)S(1)} %fusion.4, bf16[8,1024,128]{1,2,0:T(8,128)(2,1)} %constant_dynamic-update-slice_fusion.24, bf16[512,2048]{1,0:T(8,128)(2,1)S(1)} %bitcast.199), kind=kOutput, calls=%fused_computation.17 | convolution fusion | flops 1074266112 | bytes 7340032 | tf_op jit(solution)/shard_map/rk,jkn->jrn/dot_general | solution.py:373
  158.0 2.6 reshape.263
  160.6 3.6 %constant_dynamic-slice_fusion.5 = (f32[8,1,256,128]{2,1,3,0:T(1,128)}, f32[8,1,256,128]{2,1,3,0:T(1,128)}) fusion(f32[8,2,256,128]{2,1,3,0:T(2,128)S(1)} %reshape.263, s32[]{:T(128)S(6)} %select_n.463, s32[]{:T(128)S(6)} %select_n.464), kind=kLoop, calls=%fused_computation.85 | loop fusion | bytes 4194312 | tf_op jit(solution)/shard_map/jit(dynamic_index_in_dim)/dynamic_slice | solution.py:382
  164.2 3.6 copy.168
  168.8 1.9 bitcast_select_fusion.4
  170.7 1.8 collective-permute-start.21
  174.0 2.0 copy.149
  175.9 1.9 stack.114.clone
  180.6 1.5 maximum_bitcast_fusion.1
  182.2 1.9 copy.138
  184.1 1.9 fusion
  186.4 1.5 collective-permute-start.17
  187.9 2.0 stack.114.clone.1
  193.0 2.0 collective-permute-start.22
  196.6 7.5 %collective-permute-done.22 = bf16[128,1536]{0,1:T(8,128)(2,1)S(1)} collective-permute-done((bf16[128,1536]{0,1:T(8,128)(2,1)}, bf16[128,1536]{0,1:T(8,128)(2,1)S(1)}, u32[]{:S(2)}, u32[]{:S(2)}) %collective-permute-start.22) | collective-permute-done | bytes 393248 | tf_op jit(solution)/shard_map/ppermute | solution.py:281
  207.2 1.8 collective-permute-start.23
  210.8 6.8 %collective-permute-done.23 = bf16[128,1536]{0,1:T(8,128)(2,1)} collective-permute-done((bf16[128,1536]{0,1:T(8,128)(2,1)}, bf16[128,1536]{0,1:T(8,128)(2,1)}, u32[]{:S(2)}, u32[]{:S(2)}) %collective-permute-start.23) | collective-permute-done | bytes 393248 | tf_op jit(solution)/shard_map/ppermute | solution.py:281
  217.6 1.9 copy.144
  219.5 1.9 copy.152
  221.5 1.6 collective-permute-start.24
  223.5 1.8 select_bitcast_fusion.3
  225.3 1.5 pad_maximum_fusion.4
  228.4 2.4 collective-permute-done.24
  233.9 1.5 collective-permute-start.25
  237.6 5.7 %collective-permute-done.25 = bf16[128,1536]{0,1:T(8,128)(2,1)S(1)} collective-permute-done((bf16[128,1536]{0,1:T(8,128)(2,1)}, bf16[128,1536]{0,1:T(8,128)(2,1)S(1)}, u32[]{:S(2)}, u32[]{:S(2)}) %collective-permute-start.25) | collective-permute-done | bytes 393248 | tf_op jit(solution)/shard_map/ppermute | solution.py:281
  246.4 1.6 collective-permute-start.26
  250.0 4.9 %collective-permute-done.26 = bf16[128,1536]{0,1:T(8,128)(2,1)S(1)} collective-permute-done((bf16[128,1536]{0,1:T(8,128)(2,1)}, bf16[128,1536]{0,1:T(8,128)(2,1)S(1)}, u32[]{:S(2)}, u32[]{:S(2)}) %collective-permute-start.26) | collective-permute-done | bytes 393248 | tf_op jit(solution)/shard_map/ppermute | solution.py:281
  258.0 1.8 collective-permute-start.27
  261.7 4.4 %collective-permute-done.27 = bf16[128,1536]{0,1:T(8,128)(2,1)S(1)} collective-permute-done((bf16[128,1536]{0,1:T(8,128)(2,1)}, bf16[128,1536]{0,1:T(8,128)(2,1)S(1)}, u32[]{:S(2)}, u32[]{:S(2)}) %collective-permute-start.27) | collective-permute-done | bytes 393248 | tf_op jit(solution)/shard_map/ppermute | solution.py:281
  270.1 1.9 select_bitcast_fusion.1
  272.0 2.4 maximum_bitcast_fusion
  274.4 6.3 %copy.139 = bf16[2,2,256,2048]{3,2,1,0:T(8,128)(2,1)} copy(bf16[2,2,256,2048]{2,3,0,1:T(8,128)(2,1)} %maximum_bitcast_fusion) | data formatting | bytes 8388608 | tf_op jit(solution)/shard_map/transpose | solution.py:398
  281.6 3.2 collective-permute-start.19
  284.9 3.6 pad_maximum_fusion
  289.5 7.1 %convolution_convert_fusion = bf16[1056,1536]{1,0:T(8,128)(2,1)S(1)} fusion(bf16[1056,2048]{1,0:T(8,128)(2,1)S(1)} %bitcast.195, bf16[2048,1536]{1,0:T(8,128)(2,1)S(1)} %bitcast.190), kind=kOutput, calls=%fused_computation | convolution fusion | flops 6645399552 | bytes 13860864 | tf_op jit(solution)/shard_map/dot_general | solution.py:401
  296.7 6.3 %product.1 = (bf16[2,512,512]{2,1,0:T(8,128)(2,1)S(1)}, f32[2,2,16,512]{3,2,1,0:T(8,128)S(1)}) custom-call(bf16[2,528,1536]{2,1,0:T(8,128)(2,1)S(1)} %bitcast.183, bf16[2,528,1536]{2,1,0:T(8,128)(2,1)S(1)} %bitcast.184, f32[3,7,512]{2,1,0:T(8,128)S(1)} %dynamic-slice_bitcast_fusion.1.taps_ref, bf16[512,256]{1,0:T(8,128)(2,1)S(1)} %copy-done.6, ...), custom_call_target="tpu_custom_call" | custom-call | flops 268435456 | bytes 8388608 | tf_op jit(solution)/shard_map/product/pallas_call | solution.py:169
  304.6 7.1 %collective-permute-start.41 = (f32[2,16,512]{2,1,0:T(8,128)}, f32[2,16,512]{2,1,0:T(8,128)}, u32[]{:S(2)}, u32[]{:S(2)}) collective-permute-start(f32[2,16,512]{2,1,0:T(8,128)} %fusion.13), channel_id=1, source_target_pairs={{0,14},{1,15},{16,30},{17,31}} | collective-permute-start | bytes 196616 | tf_op jit(solution)/shard_map/ppermute | solution.py:245
  311.7 1.9 collective-permute-start.40
  331.6 3.4 collective-permute-start.35
  335.0 1.6 copy-done.5
  337.9 5.7 %local.1 = (f32[2,512,512]{2,1,0:T(8,128)S(1)}, f32[2,512,512]{2,1,0:T(8,128)S(1)}) custom-call(bf16[2,528,1536]{2,1,0:T(8,128)(2,1)S(1)} %bitcast.185, f32[3,7,512]{2,1,0:T(8,128)S(1)} %dynamic-slice_bitcast_fusion.1.taps_ref, bf16[2,512,512]{2,1,0:T(8,128)(2,1)S(1)} %copy-done.13, bf16[4096,256]{1,0:T(8,128)(2,1)S(1)} %copy-done.5), custom_call_target="tpu_custom_call" | custom-call | flops 2147483648 | bytes 16777216 | tf_op jit(solution)/shard_map/local/pallas_call | solution.py:198
  344.7 3.2 finish.1
  348.6 8.8 %collective-permute-done.42 = bf16[512,512]{1,0:T(8,128)(2,1)} collective-permute-done((bf16[512,512]{1,0:T(8,128)(2,1)S(1)}, bf16[512,512]{1,0:T(8,128)(2,1)}, u32[]{:S(2)}, u32[]{:S(2)}) %collective-permute-start.42) | collective-permute-done | bytes 524320 | tf_op jit(solution)/shard_map/ppermute | solution.py:319
  (273 shorter events, 106.0 us)
Async XLA Ops:
  0.6 167.2 %copy-start = (f32[7,3,2048]{2,0,1:T(8,128)S(1)}, f32[7,3,2048]{2,0,1:T(8,128)}, u32[]{:S(2)}) copy-start(f32[7,3,2048]{2,0,1:T(8,128)} %param.21) | copy-start | bytes 516100
  2.8 8.5 %copy-start.20 = (bf16[128,3,2048]{2,0,1:T(8,128)(2,1)S(1)}, bf16[128,3,2048]{2,0,1:T(8,128)(2,1)}, u32[]{:S(2)}) copy-start(bf16[128,3,2048]{2,0,1:T(8,128)(2,1)} %param.20) | copy-start | bytes 4718596
  2.8 18.3 %collective-permute-start.9 = (bf16[1024,128]{1,0:T(8,128)(2,1)}, bf16[1024,128]{1,0:T(8,128)(2,1)}, u32[]{:S(2)}, u32[]{:S(2)}) collective-permute-start(bf16[1024,128]{1,0:T(8,128)(2,1)} %get-tuple-element.45), channel_id=1, source_target_pairs={{0,2},{1,3},{4,0},{5,1},{8,4},{9,5},{12,8},{13,9},{14,12},{15,13},... | collective-permute-start | bytes 786440 | tf_op jit(solution)/shard_map/ppermute | solution.py:282
  8.6 91.9 %collective-permute-start.7 = (bf16[3,144,2048]{2,1,0:T(8,128)(2,1)}, bf16[3,144,2048]{2,1,0:T(8,128)(2,1)}, u32[]{:S(2)}, u32[]{:S(2)}) collective-permute-start(bf16[3,144,2048]{2,1,0:T(8,128)(2,1)} %slice_bitcast_fusion), channel_id=1, source_target_pairs={{0,1},{1,2},{2,3},{3,4},{4,5},{5,6},{6,7},{7,8},{8,9},{9,10},{10,1... | collective-permute-start | bytes 5308424 | tf_op jit(solution)/shard_map/ppermute | solution.py:245
  11.3 10.3 %collective-permute-start = (bf16[1024,128]{1,0:T(8,128)(2,1)}, bf16[1024,128]{1,0:T(8,128)(2,1)}, u32[]{:S(2)}, u32[]{:S(2)}) collective-permute-start(bf16[1024,128]{1,0:T(8,128)(2,1)} %get-tuple-element.42), channel_id=1, source_target_pairs={{0,4},{1,5},{4,8},{5,9},{8,12},{9,13},{12,14},{13,15},{14,10},{15,... | collective-permute-start | bytes 786440 | tf_op jit(solution)/shard_map/ppermute | solution.py:281
  13.0 155.7 %collective-permute-start.20 = (bf16[128,1536]{0,1:T(8,128)(2,1)}, bf16[128,1536]{0,1:T(8,128)(2,1)}, u32[]{:S(2)}, u32[]{:S(2)}) collective-permute-start(bf16[128,1536]{0,1:T(8,128)(2,1)} %bitcast.69), channel_id=1, source_target_pairs={{0,1},{1,0},{2,3},{3,2},{4,5},{5,4},{6,7},{7,6},{8,9},{9,8},{10,11... | collective-permute-start | bytes 1179656 | tf_op jit(solution)/shard_map/ppermute | solution.py:316
  17.7 13.9 %copy-start.47 = (s32[8]{0:T(128)S(1)}, s32[8]{0:T(128)}, u32[]{:S(2)}) copy-start(s32[8]{0:T(128)} %constant.307.clone) | copy-start | bytes 100
  17.8 23.8 %copy-start.40 = (s32[8]{0:T(128)S(1)}, s32[8]{0:T(128)}, u32[]{:S(2)}) copy-start(s32[8]{0:T(128)} %constant.308.clone) | copy-start | bytes 100
  21.0 8.6 %collective-permute-start.10 = (bf16[1024,128]{1,0:T(8,128)(2,1)}, bf16[1024,128]{1,0:T(8,128)(2,1)}, u32[]{:S(2)}, u32[]{:S(2)}) collective-permute-start(bf16[1024,128]{1,0:T(8,128)(2,1)} %collective-permute-done.9), channel_id=1, source_target_pairs={{0,2},{1,3},{4,0},{5,1},{8,4},{9,5},{12,8},{13,9},{14,12},{15,13},... | collective-permute-start | bytes 786440 | tf_op jit(solution)/shard_map/ppermute | solution.py:282
  21.5 9.6 %collective-permute-start.1 = (bf16[1024,128]{1,0:T(8,128)(2,1)}, bf16[1024,128]{1,0:T(8,128)(2,1)}, u32[]{:S(2)}, u32[]{:S(2)}) collective-permute-start(bf16[1024,128]{1,0:T(8,128)(2,1)} %collective-permute-done), channel_id=1, source_target_pairs={{0,4},{1,5},{4,8},{5,9},{8,12},{9,13},{12,14},{13,15},{14,10},{15,... | collective-permute-start | bytes 786440 | tf_op jit(solution)/shard_map/ppermute | solution.py:281
  29.6 54.8 %collective-permute-start.11 = (bf16[1024,128]{1,0:T(8,128)(2,1)}, bf16[1024,128]{1,0:T(8,128)(2,1)}, u32[]{:S(2)}, u32[]{:S(2)}) collective-permute-start(bf16[1024,128]{1,0:T(8,128)(2,1)} %collective-permute-done.10), channel_id=1, source_target_pairs={{0,2},{1,3},{4,0},{5,1},{8,4},{9,5},{12,8},{13,9},{14,12},{15,13},... | collective-permute-start | bytes 786440 | tf_op jit(solution)/shard_map/ppermute | solution.py:282
  31.1 54.9 %collective-permute-start.2 = (bf16[1024,128]{1,0:T(8,128)(2,1)}, bf16[1024,128]{1,0:T(8,128)(2,1)}, u32[]{:S(2)}, u32[]{:S(2)}) collective-permute-start(bf16[1024,128]{1,0:T(8,128)(2,1)} %collective-permute-done.1), channel_id=1, source_target_pairs={{0,4},{1,5},{4,8},{5,9},{8,12},{9,13},{12,14},{13,15},{14,10},{15,... | collective-permute-start | bytes 786440 | tf_op jit(solution)/shard_map/ppermute | solution.py:281
  84.4 6.7 %collective-permute-start.12 = (bf16[1024,128]{1,0:T(8,128)(2,1)}, bf16[1024,128]{1,0:T(8,128)(2,1)}, u32[]{:S(2)}, u32[]{:S(2)}) collective-permute-start(bf16[1024,128]{1,0:T(8,128)(2,1)} %collective-permute-done.11), channel_id=1, source_target_pairs={{0,2},{1,3},{4,0},{5,1},{8,4},{9,5},{12,8},{13,9},{14,12},{15,13},... | collective-permute-start | bytes 786440 | tf_op jit(solution)/shard_map/ppermute | solution.py:282
  86.0 6.7 %collective-permute-start.3 = (bf16[1024,128]{1,0:T(8,128)(2,1)}, bf16[1024,128]{1,0:T(8,128)(2,1)}, u32[]{:S(2)}, u32[]{:S(2)}) collective-permute-start(bf16[1024,128]{1,0:T(8,128)(2,1)} %collective-permute-done.2), channel_id=1, source_target_pairs={{0,4},{1,5},{4,8},{5,9},{8,12},{9,13},{12,14},{13,15},{14,10},{15,... | collective-permute-start | bytes 786440 | tf_op jit(solution)/shard_map/ppermute | solution.py:281
  90.6 9.9 %copy-start.18 = (bf16[8,1024,128]{1,2,0:T(8,128)(2,1)}, bf16[8,1024,128]{1,2,0:T(8,128)(2,1)S(1)}, u32[]{:S(2)}) copy-start(bf16[8,1024,128]{1,2,0:T(8,128)(2,1)S(1)} %constant_dynamic-update-slice_fusion.20) | copy-start | bytes 6291460
  91.2 39.8 %collective-permute-start.13 = (bf16[1024,128]{1,0:T(8,128)(2,1)}, bf16[1024,128]{1,0:T(8,128)(2,1)}, u32[]{:S(2)}, u32[]{:S(2)}) collective-permute-start(bf16[1024,128]{1,0:T(8,128)(2,1)} %collective-permute-done.12), channel_id=1, source_target_pairs={{0,2},{1,3},{4,0},{5,1},{8,4},{9,5},{12,8},{13,9},{14,12},{15,13},... | collective-permute-start | bytes 786440 | tf_op jit(solution)/shard_map/ppermute | solution.py:282
  92.7 38.6 %collective-permute-start.4 = (bf16[1024,128]{1,0:T(8,128)(2,1)}, bf16[1024,128]{1,0:T(8,128)(2,1)}, u32[]{:S(2)}, u32[]{:S(2)}) collective-permute-start(bf16[1024,128]{1,0:T(8,128)(2,1)} %collective-permute-done.3), channel_id=1, source_target_pairs={{0,4},{1,5},{4,8},{5,9},{8,12},{9,13},{12,14},{13,15},{14,10},{15,... | collective-permute-start | bytes 786440 | tf_op jit(solution)/shard_map/ppermute | solution.py:281
  120.0 29.6 %collective-permute-start.8 = (bf16[256,2048]{1,0:T(8,128)(2,1)S(1)}, bf16[256,2048]{1,0:T(8,128)(2,1)}, u32[]{:S(2)}, u32[]{:S(2)}) collective-permute-start(bf16[256,2048]{1,0:T(8,128)(2,1)S(1)} %medium.1), channel_id=1, source_target_pairs={{0,1},{1,0},{2,3},{3,2},{4,5},{5,4},{6,7},{7,6},{8,9},{9,8},{10,11... | collective-permute-start | bytes 3145736 | tf_op jit(solution)/shard_map/ppermute | solution.py:316
  130.9 8.8 %collective-permute-start.14 = (bf16[1024,128]{1,0:T(8,128)(2,1)}, bf16[1024,128]{1,0:T(8,128)(2,1)S(1)}, u32[]{:S(2)}, u32[]{:S(2)}) collective-permute-start(bf16[1024,128]{1,0:T(8,128)(2,1)} %collective-permute-done.13), channel_id=1, source_target_pairs={{0,2},{1,3},{4,0},{5,1},{8,4},{9,5},{12,8},{13,9},{14,12},{15,13},... | collective-permute-start | bytes 786440 | tf_op jit(solution)/shard_map/ppermute | solution.py:282
  131.3 8.5 %collective-permute-start.5 = (bf16[1024,128]{1,0:T(8,128)(2,1)}, bf16[1024,128]{1,0:T(8,128)(2,1)S(1)}, u32[]{:S(2)}, u32[]{:S(2)}) collective-permute-start(bf16[1024,128]{1,0:T(8,128)(2,1)} %collective-permute-done.4), channel_id=1, source_target_pairs={{0,4},{1,5},{4,8},{5,9},{8,12},{9,13},{12,14},{13,15},{14,10},{15,... | collective-permute-start | bytes 786440 | tf_op jit(solution)/shard_map/ppermute | solution.py:281
  139.8 8.0 %collective-permute-start.15 = (bf16[1024,128]{1,0:T(8,128)(2,1)S(1)}, bf16[1024,128]{1,0:T(8,128)(2,1)S(1)}, u32[]{:S(2)}, u32[]{:S(2)}) collective-permute-start(bf16[1024,128]{1,0:T(8,128)(2,1)S(1)} %collective-permute-done.14), channel_id=1, source_target_pairs={{0,2},{1,3},{4,0},{5,1},{8,4},{9,5},{12,8},{13,9},{14,12},{15,13},... | collective-permute-start | bytes 786440 | tf_op jit(solution)/shard_map/ppermute | solution.py:282
  139.8 8.2 %collective-permute-start.6 = (bf16[1024,128]{1,0:T(8,128)(2,1)S(1)}, bf16[1024,128]{1,0:T(8,128)(2,1)S(1)}, u32[]{:S(2)}, u32[]{:S(2)}) collective-permute-start(bf16[1024,128]{1,0:T(8,128)(2,1)S(1)} %collective-permute-done.5), channel_id=1, source_target_pairs={{0,4},{1,5},{4,8},{5,9},{8,12},{9,13},{12,14},{13,15},{14,10},{15,... | collective-permute-start | bytes 786440 | tf_op jit(solution)/shard_map/ppermute | solution.py:281
  167.8 11.5 %collective-permute-start.16 = (f32[8,256,128]{2,1,0:T(8,128)}, f32[8,256,128]{2,1,0:T(8,128)}, u32[]{:S(2)}, u32[]{:S(2)}) collective-permute-start(f32[8,256,128]{2,1,0:T(8,128)} %bitcast.55), channel_id=1, source_target_pairs={{0,1},{1,0},{2,3},{3,2},{4,5},{5,4},{6,7},{7,6},{8,9},{9,8},{10,11... | collective-permute-start | bytes 3145736 | tf_op jit(solution)/shard_map/ppermute | solution.py:316
  170.7 20.0 %collective-permute-start.21 = (bf16[128,1536]{0,1:T(8,128)(2,1)}, bf16[128,1536]{0,1:T(8,128)(2,1)}, u32[]{:S(2)}, u32[]{:S(2)}) collective-permute-start(bf16[128,1536]{0,1:T(8,128)(2,1)} %get-tuple-element.8), channel_id=1, source_target_pairs={{0,4},{1,5},{4,8},{5,9},{8,12},{9,13},{12,14},{13,15},{14,10},{15,... | collective-permute-start | bytes 1179656 | tf_op jit(solution)/shard_map/ppermute | solution.py:281
  173.7 18.1 %collective-permute-start.28 = (bf16[128,1536]{0,1:T(8,128)(2,1)}, bf16[128,1536]{0,1:T(8,128)(2,1)}, u32[]{:S(2)}, u32[]{:S(2)}) collective-permute-start(bf16[128,1536]{0,1:T(8,128)(2,1)} %get-tuple-element.9), channel_id=1, source_target_pairs={{0,2},{1,3},{4,0},{5,1},{8,4},{9,5},{12,8},{13,9},{14,12},{15,13},... | collective-permute-start | bytes 1179656 | tf_op jit(solution)/shard_map/ppermute | solution.py:282
  186.0 37.5 %copy-start.15 = (bf16[256,2048]{0,1:T(8,128)(2,1)}, bf16[256,2048]{0,1:T(8,128)(2,1)S(1)}, u32[]{:S(2)}) copy-start(bf16[256,2048]{0,1:T(8,128)(2,1)S(1)} %get-tuple-element.23) | copy-start | bytes 3145732
  186.4 37.1 %collective-permute-start.17 = (bf16[256,2048]{0,1:T(8,128)(2,1)S(1)}, bf16[256,2048]{0,1:T(8,128)(2,1)}, u32[]{:S(2)}, u32[]{:S(2)}) collective-permute-start(bf16[256,2048]{0,1:T(8,128)(2,1)S(1)} %fusion.2), channel_id=1, source_target_pairs={{0,16},{16,0},{1,17},{17,1},{2,18},{18,2},{3,19},{19,3},{4,20},{20... | collective-permute-start | bytes 3145736 | tf_op jit(solution)/shard_map/ppermute | solution.py:319
  193.0 11.1 %collective-permute-start.22 = (bf16[128,1536]{0,1:T(8,128)(2,1)}, bf16[128,1536]{0,1:T(8,128)(2,1)S(1)}, u32[]{:S(2)}, u32[]{:S(2)}) collective-permute-start(bf16[128,1536]{0,1:T(8,128)(2,1)} %collective-permute-done.21), channel_id=1, source_target_pairs={{0,4},{1,5},{4,8},{5,9},{8,12},{9,13},{12,14},{13,15},{14,10},{15,... | collective-permute-start | bytes 1179656 | tf_op jit(solution)/shard_map/ppermute | solution.py:281
  195.0 11.1 %collective-permute-start.29 = (bf16[128,1536]{0,1:T(8,128)(2,1)}, bf16[128,1536]{0,1:T(8,128)(2,1)}, u32[]{:S(2)}, u32[]{:S(2)}) collective-permute-start(bf16[128,1536]{0,1:T(8,128)(2,1)} %collective-permute-done.28), channel_id=1, source_target_pairs={{0,2},{1,3},{4,0},{5,1},{8,4},{9,5},{12,8},{13,9},{14,12},{15,13},... | collective-permute-start | bytes 1179656 | tf_op jit(solution)/shard_map/ppermute | solution.py:282
  207.2 10.4 %collective-permute-start.23 = (bf16[128,1536]{0,1:T(8,128)(2,1)}, bf16[128,1536]{0,1:T(8,128)(2,1)}, u32[]{:S(2)}, u32[]{:S(2)}) collective-permute-start(bf16[128,1536]{0,1:T(8,128)(2,1)} %copy-done.26), channel_id=1, source_target_pairs={{0,4},{1,5},{4,8},{5,9},{8,12},{9,13},{12,14},{13,15},{14,10},{15,... | collective-permute-start | bytes 1179656 | tf_op jit(solution)/shard_map/ppermute | solution.py:281
  209.0 10.5 %collective-permute-start.30 = (bf16[128,1536]{0,1:T(8,128)(2,1)}, bf16[128,1536]{0,1:T(8,128)(2,1)}, u32[]{:S(2)}, u32[]{:S(2)}) collective-permute-start(bf16[128,1536]{0,1:T(8,128)(2,1)} %collective-permute-done.29), channel_id=1, source_target_pairs={{0,2},{1,3},{4,0},{5,1},{8,4},{9,5},{12,8},{13,9},{14,12},{15,13},... | collective-permute-start | bytes 1179656 | tf_op jit(solution)/shard_map/ppermute | solution.py:282
  221.5 9.3 %collective-permute-start.24 = (bf16[128,1536]{0,1:T(8,128)(2,1)}, bf16[128,1536]{0,1:T(8,128)(2,1)S(1)}, u32[]{:S(2)}, u32[]{:S(2)}) collective-permute-start(bf16[128,1536]{0,1:T(8,128)(2,1)} %collective-permute-done.23), channel_id=1, source_target_pairs={{0,4},{1,5},{4,8},{5,9},{8,12},{9,13},{12,14},{13,15},{14,10},{15,... | collective-permute-start | bytes 1179656 | tf_op jit(solution)/shard_map/ppermute | solution.py:281
  223.1 9.7 %collective-permute-start.31 = (bf16[128,1536]{0,1:T(8,128)(2,1)}, bf16[128,1536]{0,1:T(8,128)(2,1)}, u32[]{:S(2)}, u32[]{:S(2)}) collective-permute-start(bf16[128,1536]{0,1:T(8,128)(2,1)} %collective-permute-done.30), channel_id=1, source_target_pairs={{0,2},{1,3},{4,0},{5,1},{8,4},{9,5},{12,8},{13,9},{14,12},{15,13},... | collective-permute-start | bytes 1179656 | tf_op jit(solution)/shard_map/ppermute | solution.py:282
  226.8 43.3 %collective-permute-start.18 = (bf16[2,256,2048]{1,2,0:T(8,128)(2,1)}, bf16[2,256,2048]{1,2,0:T(8,128)(2,1)}, u32[]{:S(2)}, u32[]{:S(2)}) collective-permute-start(bf16[2,256,2048]{1,2,0:T(8,128)(2,1)} %pad_maximum_fusion.4), channel_id=1, source_target_pairs={{0,1},{1,0},{2,3},{3,2},{4,5},{5,4},{6,7},{7,6},{8,9},{9,8},{10,11... | collective-permute-start | bytes 6291464 | tf_op jit(solution)/shard_map/ppermute | solution.py:316
  233.9 9.4 %collective-permute-start.25 = (bf16[128,1536]{0,1:T(8,128)(2,1)}, bf16[128,1536]{0,1:T(8,128)(2,1)S(1)}, u32[]{:S(2)}, u32[]{:S(2)}) collective-permute-start(bf16[128,1536]{0,1:T(8,128)(2,1)} %copy-done.25), channel_id=1, source_target_pairs={{0,4},{1,5},{4,8},{5,9},{8,12},{9,13},{12,14},{13,15},{14,10},{15,... | collective-permute-start | bytes 1179656 | tf_op jit(solution)/shard_map/ppermute | solution.py:281
  235.4 9.8 %collective-permute-start.32 = (bf16[128,1536]{0,1:T(8,128)(2,1)}, bf16[128,1536]{0,1:T(8,128)(2,1)}, u32[]{:S(2)}, u32[]{:S(2)}) collective-permute-start(bf16[128,1536]{0,1:T(8,128)(2,1)} %collective-permute-done.31), channel_id=1, source_target_pairs={{0,2},{1,3},{4,0},{5,1},{8,4},{9,5},{12,8},{13,9},{14,12},{15,13},... | collective-permute-start | bytes 1179656 | tf_op jit(solution)/shard_map/ppermute | solution.py:282
  246.4 8.5 %collective-permute-start.26 = (bf16[128,1536]{0,1:T(8,128)(2,1)}, bf16[128,1536]{0,1:T(8,128)(2,1)S(1)}, u32[]{:S(2)}, u32[]{:S(2)}) collective-permute-start(bf16[128,1536]{0,1:T(8,128)(2,1)} %copy-done.27), channel_id=1, source_target_pairs={{0,4},{1,5},{4,8},{5,9},{8,12},{9,13},{12,14},{13,15},{14,10},{15,... | collective-permute-start | bytes 1179656 | tf_op jit(solution)/shard_map/ppermute | solution.py:281
  248.0 8.8 %collective-permute-start.33 = (bf16[128,1536]{0,1:T(8,128)(2,1)}, bf16[128,1536]{0,1:T(8,128)(2,1)}, u32[]{:S(2)}, u32[]{:S(2)}) collective-permute-start(bf16[128,1536]{0,1:T(8,128)(2,1)} %collective-permute-done.32), channel_id=1, source_target_pairs={{0,2},{1,3},{4,0},{5,1},{8,4},{9,5},{12,8},{13,9},{14,12},{15,13},... | collective-permute-start | bytes 1179656 | tf_op jit(solution)/shard_map/ppermute | solution.py:282
  258.0 8.0 %collective-permute-start.27 = (bf16[128,1536]{0,1:T(8,128)(2,1)}, bf16[128,1536]{0,1:T(8,128)(2,1)S(1)}, u32[]{:S(2)}, u32[]{:S(2)}) collective-permute-start(bf16[128,1536]{0,1:T(8,128)(2,1)} %copy-done.28), channel_id=1, source_target_pairs={{0,4},{1,5},{4,8},{5,9},{8,12},{9,13},{12,14},{13,15},{14,10},{15,... | collective-permute-start | bytes 1179656 | tf_op jit(solution)/shard_map/ppermute | solution.py:281
  259.8 8.2 %collective-permute-start.34 = (bf16[128,1536]{0,1:T(8,128)(2,1)}, bf16[128,1536]{0,1:T(8,128)(2,1)}, u32[]{:S(2)}, u32[]{:S(2)}) collective-permute-start(bf16[128,1536]{0,1:T(8,128)(2,1)} %collective-permute-done.33), channel_id=1, source_target_pairs={{0,2},{1,3},{4,0},{5,1},{8,4},{9,5},{12,8},{13,9},{14,12},{15,13},... | collective-permute-start | bytes 1179656 | tf_op jit(solution)/shard_map/ppermute | solution.py:282
  281.6 6.8 %collective-permute-start.19 = (bf16[2,16,2048]{2,1,0:T(8,128)(2,1)S(1)}, bf16[2,16,2048]{2,1,0:T(8,128)(2,1)S(1)}, u32[]{:S(2)}, u32[]{:S(2)}) collective-permute-start(bf16[2,16,2048]{2,1,0:T(8,128)(2,1)S(1)} %slice.65), channel_id=1, source_target_pairs={{0,2},{1,3},{2,4},{3,5},{4,6},{5,7},{6,8},{7,9},{8,10},{9,11},{10,... | collective-permute-start | bytes 393224 | tf_op jit(solution)/shard_map/ppermute | solution.py:245
  289.5 7.1 %copy-start.6 = (bf16[512,256]{1,0:T(8,128)(2,1)S(1)}, bf16[512,256]{1,0:T(8,128)(2,1)}, u32[]{:S(2)}) copy-start(bf16[512,256]{1,0:T(8,128)(2,1)} %get-tuple-element.57.high_ref) | copy-start | bytes 786436
  296.7 7.3 %copy-start.30 = (f32[16,512]{1,0:T(8,128)S(1)}, f32[16,512]{1,0:T(8,128)}, u32[]{:S(2)}) copy-start(f32[16,512]{1,0:T(8,128)} %exp.128) | copy-start | bytes 98308
  296.7 16.9 %copy-start.39 = (f32[32,129]{1,0:T(8,128)S(1)}, f32[32,129]{1,0:T(8,128)}, u32[]{:S(2)}) copy-start(f32[32,129]{1,0:T(8,128)} %slice.87) | copy-start | bytes 49540
  296.7 16.9 %copy-start.41 = (f32[32,127]{1,0:T(8,128)S(1)}, f32[32,127]{1,0:T(8,128)}, u32[]{:S(2)}) copy-start(f32[32,127]{1,0:T(8,128)} %slice.60) | copy-start | bytes 48772
  303.9 10.6 %copy-start.9 = (f32[2,2,16,512]{3,2,1,0:T(8,128)}, f32[2,2,16,512]{3,2,1,0:T(8,128)S(1)}, u32[]{:S(2)}) copy-start(f32[2,2,16,512]{3,2,1,0:T(8,128)S(1)} %get-tuple-element.13) | copy-start | bytes 393220
  303.9 12.0 %copy-start.44 = (f32[16,32]{1,0:T(8,128)S(1)}, f32[16,32]{1,0:T(8,128)}, u32[]{:S(2)}) copy-start(f32[16,32]{1,0:T(8,128)} %get-tuple-element.52) | copy-start | bytes 6148
  304.6 25.6 %collective-permute-start.41 = (f32[2,16,512]{2,1,0:T(8,128)}, f32[2,16,512]{2,1,0:T(8,128)}, u32[]{:S(2)}, u32[]{:S(2)}) collective-permute-start(f32[2,16,512]{2,1,0:T(8,128)} %fusion.13), channel_id=1, source_target_pairs={{0,14},{1,15},{16,30},{17,31}} | collective-permute-start | bytes 196616 | tf_op jit(solution)/shard_map/ppermute | solution.py:245
  311.7 19.9 %collective-permute-start.40 = (f32[2,16,512]{2,1,0:T(8,128)}, f32[2,16,512]{2,1,0:T(8,128)}, u32[]{:S(2)}, u32[]{:S(2)}) collective-permute-start(f32[2,16,512]{2,1,0:T(8,128)} %fusion.13), channel_id=1, source_target_pairs={{0,12},{1,13},{2,14},{3,15},{16,28},{17,29},{18,30},{19,31}} | collective-permute-start | bytes 196616 | tf_op jit(solution)/shard_map/ppermute | solution.py:245
  326.4 17.3 %collective-permute-start.39 = (f32[2,16,512]{2,1,0:T(8,128)}, f32[2,16,512]{2,1,0:T(8,128)S(1)}, u32[]{:S(2)}, u32[]{:S(2)}) collective-permute-start(f32[2,16,512]{2,1,0:T(8,128)} %fusion.13), channel_id=1, source_target_pairs={{0,10},{1,11},{2,12},{3,13},{4,14},{5,15},{16,26},{17,27},{18,28},... | collective-permute-start | bytes 196616 | tf_op jit(solution)/shard_map/ppermute | solution.py:245
  327.7 16.0 %collective-permute-start.38 = (f32[2,16,512]{2,1,0:T(8,128)}, f32[2,16,512]{2,1,0:T(8,128)S(1)}, u32[]{:S(2)}, u32[]{:S(2)}) collective-permute-start(f32[2,16,512]{2,1,0:T(8,128)} %fusion.13), channel_id=1, source_target_pairs={{0,8},{1,9},{2,10},{3,11},{4,12},{5,13},{6,14},{7,15},{16,24},{17,... | collective-permute-start | bytes 196616 | tf_op jit(solution)/shard_map/ppermute | solution.py:245
  329.0 14.7 %collective-permute-start.37 = (f32[2,16,512]{2,1,0:T(8,128)}, f32[2,16,512]{2,1,0:T(8,128)S(1)}, u32[]{:S(2)}, u32[]{:S(2)}) collective-permute-start(f32[2,16,512]{2,1,0:T(8,128)} %fusion.13), channel_id=1, source_target_pairs={{0,6},{1,7},{2,8},{3,9},{4,10},{5,11},{6,12},{7,13},{8,14},{9,15},... | collective-permute-start | bytes 196616 | tf_op jit(solution)/shard_map/ppermute | solution.py:245
  330.3 13.4 %collective-permute-start.36 = (f32[2,16,512]{2,1,0:T(8,128)}, f32[2,16,512]{2,1,0:T(8,128)S(1)}, u32[]{:S(2)}, u32[]{:S(2)}) collective-permute-start(f32[2,16,512]{2,1,0:T(8,128)} %fusion.13), channel_id=1, source_target_pairs={{0,4},{1,5},{2,6},{3,7},{4,8},{5,9},{6,10},{7,11},{8,12},{9,13},{1... | collective-permute-start | bytes 196616 | tf_op jit(solution)/shard_map/ppermute | solution.py:245
  331.6 12.1 %collective-permute-start.35 = (f32[2,16,512]{2,1,0:T(8,128)}, f32[2,16,512]{2,1,0:T(8,128)S(1)}, u32[]{:S(2)}, u32[]{:S(2)}) collective-permute-start(f32[2,16,512]{2,1,0:T(8,128)} %fusion.13), channel_id=1, source_target_pairs={{0,2},{1,3},{2,4},{3,5},{4,6},{5,7},{6,8},{7,9},{8,10},{9,11},{10,... | collective-permute-start | bytes 196616 | tf_op jit(solution)/shard_map/ppermute | solution.py:245
  337.9 5.9 %copy-start.34 = (f32[16,512]{1,0:T(8,128)S(1)}, f32[16,512]{1,0:T(8,128)}, u32[]{:S(2)}) copy-start(f32[16,512]{1,0:T(8,128)} %exp.140) | copy-start | bytes 98308
  337.9 5.9 %copy-start.35 = (f32[16,512]{1,0:T(8,128)S(1)}, f32[16,512]{1,0:T(8,128)}, u32[]{:S(2)}) copy-start(f32[16,512]{1,0:T(8,128)} %exp.137) | copy-start | bytes 98308
  337.9 5.9 %copy-start.36 = (f32[16,512]{1,0:T(8,128)S(1)}, f32[16,512]{1,0:T(8,128)}, u32[]{:S(2)}) copy-start(f32[16,512]{1,0:T(8,128)} %exp.134) | copy-start | bytes 98308
  337.9 5.9 %copy-start.37 = (f32[16,512]{1,0:T(8,128)S(1)}, f32[16,512]{1,0:T(8,128)}, u32[]{:S(2)}) copy-start(f32[16,512]{1,0:T(8,128)} %exp.131) | copy-start | bytes 98308
  337.9 5.9 %copy-start.38 = (f32[16,512]{1,0:T(8,128)S(1)}, f32[16,512]{1,0:T(8,128)}, u32[]{:S(2)}) copy-start(f32[16,512]{1,0:T(8,128)} %exp.125) | copy-start | bytes 98308
  337.9 6.8 %copy-start.7 = (bf16[256,512]{1,0:T(8,128)(2,1)S(1)}, bf16[256,512]{1,0:T(8,128)(2,1)}, u32[]{:S(2)}) copy-start(bf16[256,512]{1,0:T(8,128)(2,1)} %get-tuple-element.54.low_ref) | copy-start | bytes 786436
  337.9 6.8 %copy-start.8 = (bf16[256,512]{1,0:T(8,128)(2,1)S(1)}, bf16[256,512]{1,0:T(8,128)(2,1)}, u32[]{:S(2)}) copy-start(bf16[256,512]{1,0:T(8,128)(2,1)} %get-tuple-element.55.high_ref) | copy-start | bytes 786436
  348.0 10.6 %copy-start.16 = (bf16[256,2048]{0,1:T(8,128)(2,1)S(1)}, bf16[256,2048]{0,1:T(8,128)(2,1)}, u32[]{:S(2)}) copy-start(bf16[256,2048]{0,1:T(8,128)(2,1)} %copy-done.15) | copy-start | bytes 3145732
  348.0 9.4 %collective-permute-start.42 = (bf16[512,512]{1,0:T(8,128)(2,1)S(1)}, bf16[512,512]{1,0:T(8,128)(2,1)}, u32[]{:S(2)}, u32[]{:S(2)}) collective-permute-start(bf16[512,512]{1,0:T(8,128)(2,1)S(1)} %dynamic-slice_bitcast_fusion), channel_id=1, source_target_pairs={{0,16},{16,0},{1,17},{17,1},{2,18},{18,2},{3,19},{19,3},{4,20},{20... | collective-permute-start | bytes 1572872 | tf_op jit(solution)/shard_map/ppermute | solution.py:319
  358.5 2.0 collective-permute-start.43
  (28 other events, 80.4 us)

commit v2 on v1

--- a/solution.py
+++ b/solution.py
@@ -75,13 +75,16 @@
     return total
 
 
-def medium_kernel(x_ref, taps_ref, table_ref, out_ref):
-    rows = x_ref.shape[1]
-    own = rows - BLK - RIM
-    feats = [x_ref[i].astype(f32) for i in range(3)]
-    q = fir(feats[0], taps_ref[0], BLK + RIM, own)
-    k = fir(feats[1], taps_ref[1], RIM, own + BLK)
-    v = fir(feats[2], taps_ref[2], RIM, own + BLK)
+def medium_kernel(x_ref, rim_ref, taps_ref, table_ref, out_ref):
+    own = x_ref.shape[1]
+    ahead = BLK + RIM
+
+    def joined(at, length, i):
+        return jnp.concatenate([rim_ref[at : at + length], x_ref[i]], axis=0).astype(f32)
+
+    q = fir(joined(2 * ahead, RIM, 0), taps_ref[0], RIM, own)
+    k = fir(joined(0, ahead, 1), taps_ref[1], RIM, own + BLK)
+    v = fir(joined(ahead, ahead, 2), taps_ref[2], RIM, own + BLK)
     product = (k * v).astype(bf16)
     table = table_ref[...]
     for n in range(0, own // BLK, 2):
@@ -91,14 +94,14 @@
         out_ref[(n + 1) * BLK : (n + 2) * BLK] = (q[(n + 1) * BLK : (n + 2) * BLK] * y1).astype(bf16)
 
 
-def medium(extended, taps, table):
-    _, rows, channels = extended.shape
-    own = rows - BLK - RIM
+def medium(features, rim, taps, table):
+    _, own, channels = features.shape
     return pl.pallas_call(
         medium_kernel,
         grid=(channels // LANES,),
         in_specs=[
-            pl.BlockSpec((3, rows, LANES), lambda i: (0, 0, i)),
+            pl.BlockSpec((3, own, LANES), lambda i: (0, 0, i)),
+            pl.BlockSpec((rim.shape[0], LANES), lambda i: (0, i)),
             pl.BlockSpec((3, SHORT, LANES), lambda i: (0, 0, i)),
             pl.BlockSpec((PER * BLK, 2 * BLK), lambda i: (i, 0)),
         ],
@@ -107,7 +110,124 @@
         compiler_params=params(),
         cost_estimate=cost(channels // LANES * 2 * 1024 * 256 * 256, 16 * 2**20),
         name="medium",
-    )(extended, taps, table)
+    )(features, rim, taps, table)
+
+
+def out_kernel(a_ref, b_ref, *refs):
+    pieces, (mine, theirs) = refs[:-2], refs[-2:]
+    for n in range(0, len(pieces), 2):
+        weight = jnp.concatenate([pieces[n][...], pieces[n + 1][...]], axis=1)
+        for source, target in ((a_ref, mine), (b_ref, theirs)):
+            result = jnp.dot(source[...], weight, preferred_element_type=f32)
+            half = result.shape[1] // 2
+            target[n] = result[:, :half]
+            target[n + 1] = result[:, half:]
+
+
+def out_projection(gated, other, pieces):
+    rows = gated.shape[0]
+    shape = jax.ShapeDtypeStruct((len(pieces), rows, pieces[0].shape[1]), f32)
+    return pl.pallas_call(
+        out_kernel,
+        out_shape=[shape, shape],
+        compiler_params=params(),
+        cost_estimate=cost(2**31, 9 * 2**20),
+        name="out_projection",
+    )(gated, other, *pieces)
+
+
+def stream_kernel(where_ref, mine_ref, recv_ref, in_ref, gain_ref, stream_ref, normed_ref):
+    chips, rows, piece = mine_ref.shape
+    chip, core = where_ref[0], where_ref[1]
+    total = jnp.zeros((rows, 1), f32)
+    kept = []
+    for j in range(chips):
+        columns = pl.ds(pl.multiple_of((chip + j) % chips * 2 * piece, 2 * piece), 2 * piece)
+        mine, recv = mine_ref[j], recv_ref[j]
+        first = jnp.where(core == 0, mine, recv)
+        second = jnp.where(core == 0, recv, mine)
+        update = jnp.concatenate([first, second], axis=1)
+        value = (in_ref[:, columns].astype(f32) + update).astype(bf16)
+        stream_ref[:, columns] = value
+        value = value.astype(f32)
+        total = total + jnp.sum(value * value, axis=1, keepdims=True)
+        kept.append((columns, value))
+    scale = lax.rsqrt(total / (chips * 2 * piece) + 1e-06)
+    for j in range(chips):
+        columns, value = kept[j]
+        normed_ref[j] = (value * scale * gain_ref[:, columns]).astype(bf16)
+
+
+def stream_norm(where, mine, recv, stream_in, gain):
+    chips, rows, piece = mine.shape
+    width = stream_in.shape[1]
+    step = 64
+    pieces = pl.BlockSpec((chips, step, piece), lambda i: (0, i, 0))
+    whole = pl.BlockSpec((step, width), lambda i: (i, 0))
+    return pl.pallas_call(
+        stream_kernel,
+        grid=(rows // step,),
+        in_specs=[
+            pl.BlockSpec(memory_space=pltpu.SMEM),
+            pieces,
+            pieces,
+            whole,
+            pl.BlockSpec((1, width), lambda i: (0, 0)),
+        ],
+        out_specs=[whole, pl.BlockSpec((chips, step, 2 * piece), lambda i: (0, i, 0))],
+        out_shape=[
+            jax.ShapeDtypeStruct((rows, width), bf16),
+            jax.ShapeDtypeStruct((chips, rows, 2 * piece), bf16),
+        ],
+        compiler_params=params(),
+        cost_estimate=cost(2**22, 6 * 2**20),
+        name="stream_norm",
+    )(where, mine, recv, stream_in, gain)
+
+
+def in_kernel(wide, chips, where_ref, ahead_ref, *refs):
+    sources, pieces, out_ref = refs[: 2 * wide], refs[2 * wide : -1], refs[-1]
+    side, core, chip = where_ref[2], where_ref[1], where_ref[0]
+    rows = sources[0].shape[1]
+
+    def times(value):
+        total = jnp.dot(value(0), pieces[0][...], preferred_element_type=f32)
+        for j in range(1, chips):
+            total = total + jnp.dot(value(j), pieces[j][...], preferred_element_type=f32)
+        return total
+
+    for off_side in range(wide):
+        at = (side + off_side) % wide
+        front = times(lambda j: ahead_ref[off_side, j])
+        out_ref[at, :RIM] = jnp.where(chip > 0, front, 0.0).astype(bf16)
+        for off_core in range(2):
+            start = pl.multiple_of(RIM + (core + off_core) % 2 * rows, RIM)
+            result = times(lambda j: sources[off_side * 2 + off_core][j])
+            out_ref[at, pl.ds(start, rows)] = result.astype(bf16)
+
+
+def in_projection(where, ahead, sources, pieces):
+    wide = len(sources) // 2
+    chips, rows, depth = sources[0].shape
+    columns = pieces[0].shape[1]
+    step = 256
+    fixed = pl.BlockSpec((chips, rows, depth), lambda n: (0, 0, 0))
+    total = RIM + 2 * rows
+    return pl.pallas_call(
+        functools.partial(in_kernel, wide, chips),
+        grid=(columns // step,),
+        in_specs=[
+            pl.BlockSpec(memory_space=pltpu.SMEM),
+            pl.BlockSpec(ahead.shape, lambda n: (0, 0, 0, 0)),
+        ]
+        + [fixed] * len(sources)
+        + [pl.BlockSpec((depth, step), lambda n: (0, n))] * chips,
+        out_specs=pl.BlockSpec((wide, total, step), lambda n: (0, 0, n)),
+        out_shape=jax.ShapeDtypeStruct((wide, total, columns), bf16),
+        compiler_params=params(),
+        cost_estimate=cost(2 * wide * total * chips * depth * columns, 14 * 2**20),
+        name="in_projection",
+    )(where, ahead, *sources, *pieces)
 
 
 def product_kernel(segs, k_ref, v_ref, taps_ref, high_ref, low_ref, product_ref, state_ref):
@@ -250,39 +370,15 @@
     return jnp.stack([jnp.where(first, mine, other), jnp.where(first, other, mine)])
 
 
-def ring_order(chips):
-    if chips % 2:
-        return list(range(chips))
-    return list(range(0, chips, 2)) + list(range(chips - 1, 0, -2))
-
-
-def ring_gather(up, down, cores, after=None):
+def turn(value, steps, cores):
     count = lax.axis_size("seq")
-    chips = count // cores
-    order = ring_order(chips)
-    spot = [order.index(chip) for chip in range(chips)]
-    chip = lax.axis_index("seq") // cores
-    place = jnp.asarray(spot, jnp.int32)[chip]
-    lookup = jnp.asarray(order, jnp.int32)
-
-    def perm(step):
-        return [
-            (order[a] * cores + c, order[(a + step) % chips] * cores + c)
-            for a in range(chips)
-            for c in range(cores)
-        ]
-
-    def put(store, piece, owner):
-        return lax.dynamic_update_slice_in_dim(store, piece[None], owner, 0)
-
-    both = [jnp.zeros((chips,) + up.shape, up.dtype), jnp.zeros((chips,) + down.shape, down.dtype)]
-    both = [put(both[0], up, chip), put(both[1], down, chip)]
-    for step in range(1, chips):
-        up = lax.ppermute(up, "seq", perm(1))
-        down = lax.ppermute(down, "seq", perm(-1))
-        both[0] = put(both[0], up, lookup[(place - step) % chips])
-        both[1] = put(both[1], down, lookup[(place + step) % chips])
-    return both, up, down
+    return lax.ppermute(
+        value, "seq", [((s + steps * cores) % count, s) for s in range(count)]
+    )
+
+
+def spread_pieces(piece, chips, cores):
+    return [piece] + [turn(piece, step, cores) for step in range(1, chips)]
 
 
 def body(
@@ -323,25 +419,20 @@
     filters = part // GROUP
     first_filter = tensor_rank * (channels // GROUP) + quarter * filters
 
-    rim = shift_seq(jnp.transpose(mr_features[rows - BLK - RIM :], (1, 0, 2)), 1)
-    extended = jnp.concatenate([rim, jnp.transpose(mr_features, (1, 0, 2))], axis=1)
+    features = jnp.transpose(mr_features, (1, 0, 2))
+    rim = jnp.concatenate(
+        [features[1, rows - BLK - RIM :], features[2, rows - BLK - RIM :], features[0, rows - RIM :]]
+    )
+    rim = shift_seq(rim, 1)
 
     if cores == 2:
-        half = width // 2
-        out_stacks, last_up, last_down = ring_gather(
-            mr_out_weight[: channels // 2], mr_out_weight[channels // 2 :], cores
-        )
+        out_pieces = spread_pieces(mr_out_weight, chips, cores)
         weight = li_in_weight.reshape(-1, 3, share, part)
         mine = lax.dynamic_index_in_dim(weight, side * cores + core, 2, keepdims=False)
         theirs = lax.dynamic_index_in_dim(weight, side * cores + 1 - core, 2, keepdims=False)
         mine = mine.reshape(-1, 3 * part)
         other = swap_core(theirs.reshape(-1, 3 * part))
-        halves = pair_stack(mine, other, core)
-        up, down, last_up, last_down = lax.optimization_barrier(
-            (halves[0], halves[1], last_up, last_down)
-        )
-        in_stacks, _, _ = ring_gather(up, down, cores)
-        in_weight = jnp.stack(in_stacks, axis=1).reshape(width, 3 * part)
+        in_piece = pair_stack(mine, other, core).reshape(-1, 3 * part)
     else:
         out_weight = lax.all_gather(mr_out_weight, "seq", axis=1, tiled=True)
         in_weight = lax.all_gather(li_in_weight, "seq", axis=0, tiled=True).reshape(width, -1)
@@ -361,47 +452,45 @@
     tail_high, tail_low = split_high_low(tail)
     by_channel = jnp.repeat(rates.T, GROUP, axis=1)
     seg_decay = jnp.exp(-by_channel * rows)
-    gap_decays = [jnp.exp(-by_channel * (rows * cores * gap)) for gap in range(chips - 1)]
+    gaps = jnp.arange(1, chips)
+    gap_decays = jnp.where(
+        (seq_rank // cores >= gaps)[:, None, None],
+        jnp.exp(-by_channel * (rows * cores * (gaps - 1)).astype(f32)[:, None, None]),
+        0.0,
+    )
     short_part = lax.dynamic_slice_in_dim(li_short, quarter * part, part, 2)
     short_part = jnp.transpose(short_part, (1, 0, 2))
 
-    gated = medium(extended, jnp.transpose(mr_short, (1, 0, 2)), medium_table)
-
     if cores == 2:
-        both = pair_stack(gated, swap_core(gated), core).reshape(cores * rows, channels)
-        update = sum(
-            jnp.einsum(
-                "rk,jkn->jrn",
-                both[:, i * channels // 2 : (i + 1) * channels // 2],
-                out_stacks[i],
-                preferred_element_type=f32,
-            )
-            for i in range(2)
+        in_piece, medium_table = lax.optimization_barrier((in_piece, medium_table))
+        in_pieces = spread_pieces(in_piece, chips, cores)
+    gated = medium(features, rim, jnp.transpose(mr_short, (1, 0, 2)), medium_table)
+
+    if cores == 2:
+        where = jnp.stack([seq_rank // cores, core, jnp.asarray(side, jnp.int32)])
+        mine, theirs = out_projection(gated, swap_core(gated), out_pieces)
+        stream, normed = stream_norm(where, mine, swap_core(theirs), stream_in, li_gain[None])
+        sources = []
+        for own in [normed] + ([swap_side(normed)] if wide == 2 else []):
+            sources += [own, swap_core(own)]
+        ahead = jnp.stack(
+            [
+                jnp.where(core == 1, sources[i][:, rows - RIM :], sources[i + 1][:, rows - RIM :])
+                for i in range(0, len(sources), 2)
+            ]
         )
-        update = update.reshape(chips, cores, rows, -1)
-        mine = lax.dynamic_index_in_dim(update, core, 1, keepdims=False)
-        theirs = lax.dynamic_index_in_dim(update, 1 - core, 1, keepdims=False)
-        update = pair_stack(mine, swap_core(theirs), core)
-        summed = jnp.transpose(update, (2, 1, 0, 3)).reshape(rows, width)
+        ahead = jnp.roll(turn(ahead, -1, cores), -1, axis=1)
+        projected = in_projection(where, ahead, sources, in_pieces)
     else:
         summed = lax.psum(jnp.dot(gated, out_weight, preferred_element_type=f32), "tensor")
-    stream = (stream_in.astype(f32) + summed).astype(bf16)
-    widened = stream.astype(f32)
-    mean_square = jnp.mean(widened * widened, axis=-1, keepdims=True)
-    normed = (widened * lax.rsqrt(mean_square + 1e-06) * li_gain).astype(bf16)
-
-    rows_all = normed[None]
-    if wide == 2:
-        rows_all = pair_stack(normed, swap_side(normed), side)
-    if cores == 2:
-        rows_all = pair_stack(rows_all, swap_core(rows_all), core)
-        rows_all = jnp.transpose(rows_all, (1, 0, 2, 3)).reshape(wide, cores * rows, width)
-    ahead = shift_seq(rows_all[:, cores * rows - RIM :], cores)
-    rows_all = jnp.concatenate([ahead, rows_all], axis=1)
-    projected = jnp.dot(
-        rows_all.reshape(-1, width), in_weight, preferred_element_type=f32
-    ).astype(bf16)
-    projected = projected.reshape(wide, RIM + cores * rows, 3 * part)
+        stream = (stream_in.astype(f32) + summed).astype(bf16)
+        widened = stream.astype(f32)
+        mean_square = jnp.mean(widened * widened, axis=-1, keepdims=True)
+        normed = (widened * lax.rsqrt(mean_square + 1e-06) * li_gain).astype(bf16)
+        ahead = shift_seq(normed[rows - RIM :], 1)
+        projected = jnp.dot(
+            jnp.concatenate([ahead, normed]), in_weight, preferred_element_type=f32
+        ).astype(bf16)[None]
 
     product, added = long_product(projected, short_part, tail_high, tail_low, cores)
     state = added[:, 0]
@@ -409,7 +498,7 @@
         state = state * seg_decay + added[:, seg]
     start = 0.0
     for gap in range(1, chips):
-        start = start + gap_decays[gap - 1] * shift_seq(state, gap * cores)
+        start = start + gap_decays[gap - 1] * turn(state, -gap, cores)
     starts = [start]
     for seg in range(1, cores):
         starts.append(starts[-1] * seg_decay + added[:, seg - 1])

time: 366 us -> 372 us (1.016)
  waiting for transfers between devices: 51.6 us -> 152 us
  local copies, waits for them, and re-layouts: 124 us -> 26.5 us
  starting transfers between devices: 74.3 us -> 128 us
  between operations: 37.4 us -> 1.26 us
  other arithmetic: 30 us -> 9.41 us
  Pallas kernels: 32.3 us -> 52.8 us
  matrix products: 12.6 us -> 0 us
    ppermute x28 -> x22, starting transfers between devices: 37.2 us -> 113 us  [turn(): lax.ppermute(value, 'seq', [((s + steps * cores) % count, s) for s in ran...]
    ppermute x28 -> x22, waiting for transfers between devices: 42.4 us -> 113 us  [turn(): lax.ppermute(value, 'seq', [((s + steps * cores) % count, s) for s in ran...]
    ppermute x2, waiting for transfers between devices: 8.78 us -> 34.3 us  [swap_side(): return lax.ppermute(value, 'parts', [(0, 1), (1, 0)])]
    another operation x20 -> x1, local copies, waits for them, and re-layouts: 26.7 us -> 2.3 us  [pair_stack(): jnp.stack([jnp.where(first, mine, other), jnp.where(first, other, mine)])]
    dynamic_update_slice x31 -> x0, local copies, waits for them, and re-layouts: 20.7 us -> none  [put(): return lax.dynamic_update_slice_in_dim(store, piece[None], owner, 0)]
    ppermute x9 -> x1, starting transfers between devices: 23.4 us -> 3.41 us  [shift_seq(): lax.ppermute(value, 'seq', [(s, s + steps) for s in range(count - steps)])]
    pallas_call x0 -> x3, Pallas kernels: none -> 19.2 us  [the longest x1 11.5 us: in_projection(): pl.pallas_call(functools.partial(in_kernel, wide, chips), grid=(columns /...]
    broadcast_in_dim x16 -> x0, local copies, waits for them, and re-layouts: 12.7 us -> none  [put(): return lax.dynamic_update_slice_in_dim(store, piece[None], owner, 0)]
  transfers between devices with their start and end apart: 44 -> 31, of which waited for: 12 -> 10; matrix products, arithmetic and copies ran while one was open for 34% -> 4% of each run, Pallas kernels for 6% -> 7%
where the time goes in v2:
time: 372 us; the launch traced here: 371 us
  waiting for transfers between devices  152 us (41%)
  starting transfers between devices  128 us (34%)
  Pallas kernels  52.8 us (14%)
  local copies, waits for them, and re-layouts  26.5 us (7%)
  other arithmetic  9.41 us (3%)
    ppermute x22, waiting for transfers between devices, turn(): lax.ppermute(value, 'seq', [((s + steps * cores) % count, s) for s in ran...  113 us
    ppermute x22, starting transfers between devices, turn(): lax.ppermute(value, 'seq', [((s + steps * cores) % count, s) for s in ran...  113 us
    ppermute x2, waiting for transfers between devices, swap_side(): return lax.ppermute(value, 'parts', [(0, 1), (1, 0)])  34.3 us
    unnamed x75, local copies, waits for them, and re-layouts  19 us
    pallas_call x1, Pallas kernels, medium(): pl.pallas_call(medium_kernel, grid=(channels // LANES,), in_specs=[pl.Blo...  14.1 us
    pallas_call x1, Pallas kernels, in_projection(): pl.pallas_call(functools.partial(in_kernel, wide, chips), grid=(columns /...  11.5 us
    ppermute x6, starting transfers between devices, swap_core(): return lax.ppermute(value, 'seq', swap_pairs)  8.61 us
  transfers between devices with their start and end apart: 31, of which 10 were waited for; matrix products, arithmetic and copies ran while one was open for 4% of the time, Pallas kernels for 7%

profile of v2, /device:TPU:0, one launch (start us, length us, event | category | flops | bytes accessed | tf_op | source)
XLA Modules:
  0.0 370.7 jit_solution(1662526687885248331)
XLA Ops:
  0.7 1.5 slice_bitcast_fusion.1
  2.1 0.8 slice_bitcast_fusion.4
  3.0 1.1 pad_maximum_fusion
  4.1 3.4 collective-permute-start
  7.5 0.9 copy.44
  8.4 0.8 constant_dynamic-slice_fusion.1
  9.2 1.6 collective-permute-start.1
  10.8 2.9 collective-permute-start.3
  13.8 2.1 collective-permute-start.4
  16.3 3.5 toeplitz.2.table_ref
  19.8 3.3 copy-done.1
  23.1 1.2 bitcast_select_fusion.3
  24.4 0.9 pad_maximum_fusion.1
  25.3 2.3 copy.45
  27.6 3.4 copy-done.2
  31.0 14.1 %medium.1.a_ref = bf16[256,2048]{1,0:T(8,128)(2,1)S(1)} custom-call(bf16[3,256,2048]{2,1,0:T(8,128)(2,1)S(1)} %bitcast.85, bf16[304,2048]{1,0:T(8,128)(2,1)} %collective-permute-done.rim_ref, f32[3,7,2048]{2,1,0:T(8,128)S(1)} %bitcast.94, bf16[16384,256]{1,0:T(8,128)(2,1)S(1)} %copy-done.2), custom_call_target="tpu_custom_call" | custom-call | flops 2147483648 | bytes 16777216 | tf_op jit(solution)/shard_map/medium/pallas_call | solution.py:99
  45.1 6.9 %collective-permute-start.2 = (bf16[256,2048]{1,0:T(8,128)(2,1)S(1)}, bf16[256,2048]{1,0:T(8,128)(2,1)S(1)}, u32[]{:S(2)}, u32[]{:S(2)}) collective-permute-start(bf16[256,2048]{1,0:T(8,128)(2,1)S(1)} %medium.1.a_ref), channel_id=1, source_target_pairs={{0,1},{1,0},{2,3},{3,2},{4,5},{5,4},{6,7},{7,6},{8,9},{9,8},{10,11... | collective-permute-start | bytes 3145736 | tf_op jit(solution)/shard_map/ppermute | solution.py:412
  52.0 15.7 %collective-permute-start.6 = (bf16[2048,128]{1,0:T(8,128)(2,1)}, bf16[2048,128]{1,0:T(8,128)(2,1)S(1)}, u32[]{:S(2)}, u32[]{:S(2)}) collective-permute-start(bf16[2048,128]{1,0:T(8,128)(2,1)} %refs_0_.1), channel_id=1, source_target_pairs={{8,0},{9,1},{10,2},{11,3},{12,4},{13,5},{14,6},{15,7},{0,8},{1,9},... | collective-permute-start | bytes 1572872 | tf_op jit(solution)/shard_map/ppermute | solution.py:375
  67.7 1.6 collective-permute-start.8
  69.4 1.5 collective-permute-start.9
  70.9 43.3 %collective-permute-done.6.refs_4_ = bf16[2048,128]{1,0:T(8,128)(2,1)S(1)} collective-permute-done((bf16[2048,128]{1,0:T(8,128)(2,1)}, bf16[2048,128]{1,0:T(8,128)(2,1)S(1)}, u32[]{:S(2)}, u32[]{:S(2)}) %collective-permute-start.6) | collective-permute-done | bytes 524320 | tf_op jit(solution)/shard_map/ppermute | solution.py:375
  114.2 11.3 %collective-permute-done.7.refs_5_ = bf16[2048,128]{1,0:T(8,128)(2,1)S(1)} collective-permute-done((bf16[2048,128]{1,0:T(8,128)(2,1)}, bf16[2048,128]{1,0:T(8,128)(2,1)S(1)}, u32[]{:S(2)}, u32[]{:S(2)}) %collective-permute-start.7) | collective-permute-done | bytes 524320 | tf_op jit(solution)/shard_map/ppermute | solution.py:375
  125.5 4.8 %out_projection.1 = (f32[8,256,128]{2,1,0:T(8,128)S(1)}, f32[8,256,128]{2,1,0:T(8,128)}) custom-call(bf16[256,2048]{1,0:T(8,128)(2,1)S(1)} %medium.1.a_ref, bf16[256,2048]{1,0:T(8,128)(2,1)S(1)} %collective-permute-done.2.b_ref, bf16[2048,128]{1,0:T(8,128)(2,1)} %refs_0_.1, bf16[2048,128]{1,0:T(8,128)(2,1)} %collective-permute-done.3.refs_1_, ...), custom_call_target="tpu_custom_call" | custom-call | flops 2147483648 | bytes 9437184 | tf_op jit(solution)/shard_map/out_projection/pallas_call | solution.py:130
  130.4 2.8 collective-permute-done.10.recv_ref
  133.2 2.9 stream_norm.1
  136.0 1.5 collective-permute-start.12
  137.5 23.9 %collective-permute-done.12.refs_2_ = bf16[8,256,256]{2,1,0:T(8,128)(2,1)S(1)} collective-permute-done((bf16[8,256,256]{2,1,0:T(8,128)(2,1)}, bf16[8,256,256]{2,1,0:T(8,128)(2,1)S(1)}, u32[]{:S(2)}, u32[]{:S(2)}) %collective-permute-start.12) | collective-permute-done | bytes 1048608 | tf_op jit(solution)/shard_map/ppermute | solution.py:415
  162.4 0.7 slice_bitcast_fusion.11
  163.1 1.1 collective-permute-start.16
  164.2 0.9 fusion.8
  165.1 0.9 fusion.7
  165.9 0.7 pad_maximum_fusion.2
  166.6 0.9 collective-permute-start.14
  168.0 0.7 slice.152
  168.7 3.5 collective-permute-start.17
  172.6 10.7 %collective-permute-done.15.refs_5_ = bf16[256,1536]{1,0:T(8,128)(2,1)} collective-permute-done((bf16[256,1536]{1,0:T(8,128)(2,1)}, bf16[256,1536]{1,0:T(8,128)(2,1)}, u32[]{:S(2)}, u32[]{:S(2)}) %collective-permute-start.15) | collective-permute-done | bytes 786464 | tf_op jit(solution)/shard_map/ppermute | solution.py:375
  183.3 2.6 collective-permute-start.19
  185.9 12.4 %collective-permute-done.16.refs_6_ = bf16[256,1536]{1,0:T(8,128)(2,1)} collective-permute-done((bf16[256,1536]{1,0:T(8,128)(2,1)}, bf16[256,1536]{1,0:T(8,128)(2,1)}, u32[]{:S(2)}, u32[]{:S(2)}) %collective-permute-start.16) | collective-permute-done | bytes 786464 | tf_op jit(solution)/shard_map/ppermute | solution.py:375
  198.3 71.0 %collective-permute-start.20 = (bf16[256,1536]{1,0:T(8,128)(2,1)S(1)}, bf16[256,1536]{1,0:T(8,128)(2,1)S(1)}, u32[]{:S(2)}, u32[]{:S(2)}) collective-permute-start(bf16[256,1536]{1,0:T(8,128)(2,1)S(1)} %bitcast.91), channel_id=1, source_target_pairs={{12,0},{13,1},{14,2},{15,3},{0,4},{1,5},{2,6},{3,7},{4,8},{5,9},{6... | collective-permute-start | bytes 2359304 | tf_op jit(solution)/shard_map/ppermute | solution.py:375
  269.5 1.0 fusion.1
  270.5 31.7 %collective-permute-done.18.refs_8_ = bf16[256,1536]{1,0:T(8,128)(2,1)S(1)} collective-permute-done((bf16[256,1536]{1,0:T(8,128)(2,1)S(1)}, bf16[256,1536]{1,0:T(8,128)(2,1)S(1)}, u32[]{:S(2)}, u32[]{:S(2)}) %collective-permute-start.18) | collective-permute-done | bytes 786464 | tf_op jit(solution)/shard_map/ppermute | solution.py:375
  302.1 3.9 %collective-permute-done.19.refs_9_ = bf16[256,1536]{1,0:T(8,128)(2,1)S(1)} collective-permute-done((bf16[256,1536]{1,0:T(8,128)(2,1)S(1)}, bf16[256,1536]{1,0:T(8,128)(2,1)S(1)}, u32[]{:S(2)}, u32[]{:S(2)}) %collective-permute-start.19) | collective-permute-done | bytes 786464 | tf_op jit(solution)/shard_map/ppermute | solution.py:375
  306.1 1.1 copy-done.10
  307.2 1.2 copy-done.16
  308.5 1.2 copy-done.18
  309.7 11.5 %in_projection.1.k_ref.v_ref.q_ref = bf16[2,528,1536]{2,1,0:T(8,128)(2,1)S(1)} custom-call(s32[3]{0:T(128)S(1)} %pad_add_fusion.where_ref, bf16[2,8,16,256]{3,2,1,0:T(8,128)(2,1)S(1)} %pad_maximum_fusion.3.ahead_ref, bf16[8,256,256]{2,1,0:T(8,128)(2,1)} %get-tuple-element.16.refs_0_, bf16[8,256,256]{2,1,0:T(8,128)(2,1)S(1)} %copy-done.18, ...), custom_call_target="tpu_custom_call" | custom-call | flops 6643777536 | bytes 14680064 | tf_op jit(solution)/shard_map/in_projection/pallas_call | solution.py:216
  321.2 6.3 %product.1 = (bf16[2,512,512]{2,1,0:T(8,128)(2,1)S(1)}, f32[2,2,16,512]{3,2,1,0:T(8,128)S(1)}) custom-call(bf16[2,528,1536]{2,1,0:T(8,128)(2,1)S(1)} %in_projection.1.k_ref.v_ref.q_ref, bf16[2,528,1536]{2,1,0:T(8,128)(2,1)S(1)} %in_projection.1.k_ref.v_ref.q_ref, f32[3,7,512]{2,1,0:T(8,128)S(1)} %dynamic-slice_bitcast_fusion.1.taps_ref, ...), custom_call_target="tpu_custom_call" | custom-call | flops 268435456 | bytes 8388608 | tf_op jit(solution)/shard_map/product/pallas_call | solution.py:289
  327.5 1.0 copy-done.19
  328.5 0.7 fusion.6
  329.3 0.9 toeplitz.3.table_ref
  330.2 1.3 copy-done.4
  331.5 1.8 collective-permute-start.24
  333.3 3.5 collective-permute-start.25
  336.7 2.9 collective-permute-start.27
  339.7 1.8 collective-permute-start.28
  341.5 1.6 copy-done.5
  343.1 1.2 copy-done.20
  344.4 5.7 %local.1 = (f32[2,512,512]{2,1,0:T(8,128)S(1)}, f32[2,512,512]{2,1,0:T(8,128)S(1)}) custom-call(bf16[2,528,1536]{2,1,0:T(8,128)(2,1)S(1)} %in_projection.1.k_ref.v_ref.q_ref, f32[3,7,512]{2,1,0:T(8,128)S(1)} %dynamic-slice_bitcast_fusion.1.taps_ref, bf16[2,512,512]{2,1,0:T(8,128)(2,1)S(1)} %copy-done.20, bf16[4096,256]{1,0:T(8,128)(2,1)S(1)} %copy-done.5), custom_call_target="tpu_custom_call" | custom-call | flops 2147483648 | bytes 16777216 | tf_op jit(solution)/shard_map/local/pallas_call | solution.py:318
  350.2 0.9 add_bitcast_fusion
  351.2 3.2 finish.1
  354.4 1.6 collective-permute-start.29
  356.0 10.4 %collective-permute-done.29 = bf16[512,512]{1,0:T(8,128)(2,1)S(1)} collective-permute-done((bf16[512,512]{1,0:T(8,128)(2,1)S(1)}, bf16[512,512]{1,0:T(8,128)(2,1)S(1)}, u32[]{:S(2)}, u32[]{:S(2)}) %collective-permute-start.29) | collective-permute-done | bytes 524320 | tf_op jit(solution)/shard_map/ppermute | solution.py:415
  366.6 1.9 collective-permute-done.30
  369.3 1.4 copy.55
  (127 shorter events, 3.6 us)
Async XLA Ops:
  0.6 168.1 %copy-start = (f32[7,3,2048]{2,0,1:T(8,128)S(1)}, f32[7,3,2048]{2,0,1:T(8,128)}, u32[]{:S(2)}) copy-start(f32[7,3,2048]{2,0,1:T(8,128)} %param.17) | copy-start | bytes 516100
  0.6 6.9 %copy-start.21 = (bf16[128,3,2048]{2,0,1:T(8,128)(2,1)S(1)}, bf16[128,3,2048]{2,0,1:T(8,128)(2,1)}, u32[]{:S(2)}) copy-start(bf16[128,3,2048]{2,0,1:T(8,128)(2,1)} %param.16) | copy-start | bytes 4718596
  4.1 23.5 %collective-permute-start = (bf16[304,2048]{1,0:T(8,128)(2,1)}, bf16[304,2048]{1,0:T(8,128)(2,1)}, u32[]{:S(2)}, u32[]{:S(2)}) collective-permute-start(bf16[304,2048]{1,0:T(8,128)(2,1)} %pad_maximum_fusion), channel_id=1, source_target_pairs={{0,1},{1,2},{2,3},{3,4},{4,5},{5,6},{6,7},{7,8},{8,9},{9,10},{10,1... | collective-permute-start | bytes 3735560 | tf_op jit(solution)/shard_map/ppermute | solution.py:365
  7.5 8.4 %copy-start.31 = (f32[128,128]{1,0:T(8,128)S(1)}, f32[128,128]{1,0:T(8,128)}, u32[]{:S(2)}) copy-start(f32[128,128]{1,0:T(8,128)} %param.13) | copy-start | bytes 196612
  9.2 13.9 %collective-permute-start.1 = (bf16[128,1536]{0,1:T(8,128)(2,1)S(1)}, bf16[128,1536]{0,1:T(8,128)(2,1)}, u32[]{:S(2)}, u32[]{:S(2)}) collective-permute-start(bf16[128,1536]{0,1:T(8,128)(2,1)S(1)} %bitcast.105), channel_id=1, source_target_pairs={{0,1},{1,0},{2,3},{3,2},{4,5},{5,4},{6,7},{7,6},{8,9},{9,8},{10,11... | collective-permute-start | bytes 1179656 | tf_op jit(solution)/shard_map/ppermute | solution.py:412
  10.8 56.9 %collective-permute-start.3 = (bf16[2048,128]{1,0:T(8,128)(2,1)}, bf16[2048,128]{1,0:T(8,128)(2,1)}, u32[]{:S(2)}, u32[]{:S(2)}) collective-permute-start(bf16[2048,128]{1,0:T(8,128)(2,1)} %refs_0_.1), channel_id=1, source_target_pairs={{2,0},{3,1},{4,2},{5,3},{6,4},{7,5},{8,6},{9,7},{10,8},{11,9},{12,... | collective-permute-start | bytes 1572872 | tf_op jit(solution)/shard_map/ppermute | solution.py:375
  13.8 53.9 %collective-permute-start.4 = (bf16[2048,128]{1,0:T(8,128)(2,1)}, bf16[2048,128]{1,0:T(8,128)(2,1)}, u32[]{:S(2)}, u32[]{:S(2)}) collective-permute-start(bf16[2048,128]{1,0:T(8,128)(2,1)} %refs_0_.1), channel_id=1, source_target_pairs={{4,0},{5,1},{6,2},{7,3},{8,4},{9,5},{10,6},{11,7},{12,8},{13,9},{1... | collective-permute-start | bytes 1572872 | tf_op jit(solution)/shard_map/ppermute | solution.py:375
  15.9 53.5 %collective-permute-start.5 = (bf16[2048,128]{1,0:T(8,128)(2,1)}, bf16[2048,128]{1,0:T(8,128)(2,1)}, u32[]{:S(2)}, u32[]{:S(2)}) collective-permute-start(bf16[2048,128]{1,0:T(8,128)(2,1)} %refs_0_.1), channel_id=1, source_target_pairs={{6,0},{7,1},{8,2},{9,3},{10,4},{11,5},{12,6},{13,7},{14,8},{15,9},... | collective-permute-start | bytes 1572872 | tf_op jit(solution)/shard_map/ppermute | solution.py:375
  16.3 6.8 %copy-start.22 = (bf16[128,3,1,512]{0,3,2,1:T(8,128)(2,1)S(1)}, bf16[128,3,1,512]{0,3,2,1:T(8,128)(2,1)}, u32[]{:S(2)}) copy-start(bf16[128,3,1,512]{0,3,2,1:T(8,128)(2,1)} %get-tuple-element.34) | copy-start | bytes 1179652
  19.8 3.3 copy-start.1
  23.1 4.5 %copy-start.3 = (bf16[256,3,2048]{2,0,1:T(8,128)(2,1)S(1)}, bf16[256,3,2048]{2,0,1:T(8,128)(2,1)}, u32[]{:S(2)}) copy-start(bf16[256,3,2048]{2,0,1:T(8,128)(2,1)} %param.11) | copy-start | bytes 9437188
  23.1 4.5 %copy-start.13 = (f32[7,3,2048]{2,0,1:T(8,128)S(1)}, f32[7,3,2048]{2,0,1:T(8,128)}, u32[]{:S(2)}) copy-start(f32[7,3,2048]{2,0,1:T(8,128)} %param.12) | copy-start | bytes 516100
  27.6 3.4 copy-start.2
  45.1 88.1 %copy-start.8 = (bf16[256,2048]{1,0:T(8,128)(2,1)S(1)}, bf16[256,2048]{1,0:T(8,128)(2,1)}, u32[]{:S(2)}) copy-start(bf16[256,2048]{1,0:T(8,128)(2,1)} %in_ref.1) | copy-start | bytes 3145732
  45.1 88.1 %copy-start.14 = (f32[2048]{0:T(1024)S(1)}, f32[2048]{0:T(1024)}, u32[]{:S(2)}) copy-start(f32[2048]{0:T(1024)} %param.15) | copy-start | bytes 24580
  45.1 80.4 %collective-permute-start.2 = (bf16[256,2048]{1,0:T(8,128)(2,1)S(1)}, bf16[256,2048]{1,0:T(8,128)(2,1)S(1)}, u32[]{:S(2)}, u32[]{:S(2)}) collective-permute-start(bf16[256,2048]{1,0:T(8,128)(2,1)S(1)} %medium.1.a_ref), channel_id=1, source_target_pairs={{0,1},{1,0},{2,3},{3,2},{4,5},{5,4},{6,7},{7,6},{8,9},{9,8},{10,11... | collective-permute-start | bytes 3145736 | tf_op jit(solution)/shard_map/ppermute | solution.py:412
  52.0 62.2 %collective-permute-start.6 = (bf16[2048,128]{1,0:T(8,128)(2,1)}, bf16[2048,128]{1,0:T(8,128)(2,1)S(1)}, u32[]{:S(2)}, u32[]{:S(2)}) collective-permute-start(bf16[2048,128]{1,0:T(8,128)(2,1)} %refs_0_.1), channel_id=1, source_target_pairs={{8,0},{9,1},{10,2},{11,3},{12,4},{13,5},{14,6},{15,7},{0,8},{1,9},... | collective-permute-start | bytes 1572872 | tf_op jit(solution)/shard_map/ppermute | solution.py:375
  67.7 57.8 %collective-permute-start.7 = (bf16[2048,128]{1,0:T(8,128)(2,1)}, bf16[2048,128]{1,0:T(8,128)(2,1)S(1)}, u32[]{:S(2)}, u32[]{:S(2)}) collective-permute-start(bf16[2048,128]{1,0:T(8,128)(2,1)} %refs_0_.1), channel_id=1, source_target_pairs={{10,0},{11,1},{12,2},{13,3},{14,4},{15,5},{0,6},{1,7},{2,8},{3,9},... | collective-permute-start | bytes 1572872 | tf_op jit(solution)/shard_map/ppermute | solution.py:375
  67.7 57.8 %collective-permute-start.8 = (bf16[2048,128]{1,0:T(8,128)(2,1)}, bf16[2048,128]{1,0:T(8,128)(2,1)S(1)}, u32[]{:S(2)}, u32[]{:S(2)}) collective-permute-start(bf16[2048,128]{1,0:T(8,128)(2,1)} %refs_0_.1), channel_id=1, source_target_pairs={{12,0},{13,1},{14,2},{15,3},{0,4},{1,5},{2,6},{3,7},{4,8},{5,9},{6... | collective-permute-start | bytes 1572872 | tf_op jit(solution)/shard_map/ppermute | solution.py:375
  69.4 56.1 %collective-permute-start.9 = (bf16[2048,128]{1,0:T(8,128)(2,1)}, bf16[2048,128]{1,0:T(8,128)(2,1)S(1)}, u32[]{:S(2)}, u32[]{:S(2)}) collective-permute-start(bf16[2048,128]{1,0:T(8,128)(2,1)} %refs_0_.1), channel_id=1, source_target_pairs={{14,0},{15,1},{0,2},{1,3},{2,4},{3,5},{4,6},{5,7},{6,8},{7,9},{8,1... | collective-permute-start | bytes 1572872 | tf_op jit(solution)/shard_map/ppermute | solution.py:375
  130.3 31.1 %copy-start.32 = (f32[128,16]{0,1:T(8,128)S(1)}, f32[128,16]{0,1:T(8,128)}, u32[]{:S(2)}) copy-start(f32[128,16]{0,1:T(8,128)} %param.19) | copy-start | bytes 24580
  130.3 31.1 %copy-start.33 = (f32[128,16]{0,1:T(8,128)S(1)}, f32[128,16]{0,1:T(8,128)}, u32[]{:S(2)}) copy-start(f32[128,16]{0,1:T(8,128)} %param.18) | copy-start | bytes 24580
  130.3 2.9 collective-permute-start.10
  136.0 32.7 %copy-start.9 = (bf16[2,128,1536]{2,1,0:T(8,128)(2,1)S(1)}, bf16[2,128,1536]{2,1,0:T(8,128)(2,1)}, u32[]{:S(2)}) copy-start(bf16[2,128,1536]{2,1,0:T(8,128)(2,1)} %copy.45) | copy-start | bytes 2359300
  136.0 25.4 %collective-permute-start.12 = (bf16[8,256,256]{2,1,0:T(8,128)(2,1)}, bf16[8,256,256]{2,1,0:T(8,128)(2,1)S(1)}, u32[]{:S(2)}, u32[]{:S(2)}) collective-permute-start(bf16[8,256,256]{2,1,0:T(8,128)(2,1)} %get-tuple-element.16.refs_0_), channel_id=1, source_target_pairs={{0,16},{16,0},{1,17},{17,1},{2,18},{18,2},{3,19},{19,3},{4,20},{20... | collective-permute-start | bytes 3145736 | tf_op jit(solution)/shard_map/ppermute | solution.py:415
  137.5 26.6 %collective-permute-start.11 = (bf16[8,256,256]{2,1,0:T(8,128)(2,1)}, bf16[8,256,256]{2,1,0:T(8,128)(2,1)S(1)}, u32[]{:S(2)}, u32[]{:S(2)}) collective-permute-start(bf16[8,256,256]{2,1,0:T(8,128)(2,1)} %get-tuple-element.16.refs_0_), channel_id=1, source_target_pairs={{0,1},{1,0},{2,3},{3,2},{4,5},{5,4},{6,7},{7,6},{8,9},{9,8},{10,11... | collective-permute-start | bytes 3145736 | tf_op jit(solution)/shard_map/ppermute | solution.py:412
  161.4 109.0 %copy-start.15 = (bf16[8,256,256]{2,1,0:T(8,128)(2,1)}, bf16[8,256,256]{2,1,0:T(8,128)(2,1)S(1)}, u32[]{:S(2)}) copy-start(bf16[8,256,256]{2,1,0:T(8,128)(2,1)S(1)} %collective-permute-done.12.refs_2_) | copy-start | bytes 3145732
  161.4 3.7 collective-permute-start.13
  163.1 20.3 %collective-permute-start.15 = (bf16[256,1536]{1,0:T(8,128)(2,1)}, bf16[256,1536]{1,0:T(8,128)(2,1)}, u32[]{:S(2)}, u32[]{:S(2)}) collective-permute-start(bf16[256,1536]{1,0:T(8,128)(2,1)} %bitcast.86), channel_id=1, source_target_pairs={{2,0},{3,1},{4,2},{5,3},{6,4},{7,5},{8,6},{9,7},{10,8},{11,9},{12,... | collective-permute-start | bytes 2359304 | tf_op jit(solution)/shard_map/ppermute | solution.py:375
  163.1 35.2 %collective-permute-start.16 = (bf16[256,1536]{1,0:T(8,128)(2,1)}, bf16[256,1536]{1,0:T(8,128)(2,1)}, u32[]{:S(2)}, u32[]{:S(2)}) collective-permute-start(bf16[256,1536]{1,0:T(8,128)(2,1)} %bitcast.87), channel_id=1, source_target_pairs={{4,0},{5,1},{6,2},{7,3},{8,4},{9,5},{10,6},{11,7},{12,8},{13,9},{1... | collective-permute-start | bytes 2359304 | tf_op jit(solution)/shard_map/ppermute | solution.py:375
  164.2 141.9 %copy-start.17 = (bf16[8,256,256]{2,1,0:T(8,128)(2,1)}, bf16[8,256,256]{2,1,0:T(8,128)(2,1)S(1)}, u32[]{:S(2)}) copy-start(bf16[8,256,256]{2,1,0:T(8,128)(2,1)S(1)} %collective-permute-done.11.refs_1_) | copy-start | bytes 3145732
  166.6 102.6 %collective-permute-start.14 = (bf16[2,8,16,256]{3,2,1,0:T(8,128)(2,1)}, bf16[2,8,16,256]{3,2,1,0:T(8,128)(2,1)S(1)}, u32[]{:S(2)}, u32[]{:S(2)}) collective-permute-start(bf16[2,8,16,256]{3,2,1,0:T(8,128)(2,1)} %pad_maximum_fusion.2), channel_id=1, source_target_pairs={{14,0},{15,1},{0,2},{1,3},{2,4},{3,5},{4,6},{5,7},{6,8},{7,9},{8,1... | collective-permute-start | bytes 393224 | tf_op jit(solution)/shard_map/ppermute | solution.py:375
  168.7 101.7 %collective-permute-start.17 = (bf16[256,1536]{1,0:T(8,128)(2,1)S(1)}, bf16[256,1536]{1,0:T(8,128)(2,1)S(1)}, u32[]{:S(2)}, u32[]{:S(2)}) collective-permute-start(bf16[256,1536]{1,0:T(8,128)(2,1)S(1)} %bitcast.88), channel_id=1, source_target_pairs={{6,0},{7,1},{8,2},{9,3},{10,4},{11,5},{12,6},{13,7},{14,8},{15,9},... | collective-permute-start | bytes 2359304 | tf_op jit(solution)/shard_map/ppermute | solution.py:375
  172.3 129.9 %collective-permute-start.18 = (bf16[256,1536]{1,0:T(8,128)(2,1)S(1)}, bf16[256,1536]{1,0:T(8,128)(2,1)S(1)}, u32[]{:S(2)}, u32[]{:S(2)}) collective-permute-start(bf16[256,1536]{1,0:T(8,128)(2,1)S(1)} %bitcast.89), channel_id=1, source_target_pairs={{8,0},{9,1},{10,2},{11,3},{12,4},{13,5},{14,6},{15,7},{0,8},{1,9},... | collective-permute-start | bytes 2359304 | tf_op jit(solution)/shard_map/ppermute | solution.py:375
  183.3 122.8 %collective-permute-start.19 = (bf16[256,1536]{1,0:T(8,128)(2,1)S(1)}, bf16[256,1536]{1,0:T(8,128)(2,1)S(1)}, u32[]{:S(2)}, u32[]{:S(2)}) collective-permute-start(bf16[256,1536]{1,0:T(8,128)(2,1)S(1)} %bitcast.90), channel_id=1, source_target_pairs={{10,0},{11,1},{12,2},{13,3},{14,4},{15,5},{0,6},{1,7},{2,8},{3,9},... | collective-permute-start | bytes 2359304 | tf_op jit(solution)/shard_map/ppermute | solution.py:375
  198.3 107.8 %collective-permute-start.20 = (bf16[256,1536]{1,0:T(8,128)(2,1)S(1)}, bf16[256,1536]{1,0:T(8,128)(2,1)S(1)}, u32[]{:S(2)}, u32[]{:S(2)}) collective-permute-start(bf16[256,1536]{1,0:T(8,128)(2,1)S(1)} %bitcast.91), channel_id=1, source_target_pairs={{12,0},{13,1},{14,2},{15,3},{0,4},{1,5},{2,6},{3,7},{4,8},{5,9},{6... | collective-permute-start | bytes 2359304 | tf_op jit(solution)/shard_map/ppermute | solution.py:375
  269.3 36.8 %collective-permute-start.21 = (bf16[256,1536]{1,0:T(8,128)(2,1)S(1)}, bf16[256,1536]{1,0:T(8,128)(2,1)S(1)}, u32[]{:S(2)}, u32[]{:S(2)}) collective-permute-start(bf16[256,1536]{1,0:T(8,128)(2,1)S(1)} %bitcast.92), channel_id=1, source_target_pairs={{14,0},{15,1},{0,2},{1,3},{2,4},{3,5},{4,6},{5,7},{6,8},{7,9},{8,1... | collective-permute-start | bytes 2359304 | tf_op jit(solution)/shard_map/ppermute | solution.py:375
  306.1 1.1 copy-start.10
  307.2 1.2 copy-start.16
  308.5 1.2 copy-start.18
  321.2 8.0 %copy-start.30 = (f32[32,129]{1,0:T(8,128)S(1)}, f32[32,129]{1,0:T(8,128)}, u32[]{:S(2)}) copy-start(f32[32,129]{1,0:T(8,128)} %slice.152) | copy-start | bytes 49540
  327.5 1.0 copy-start.19
  329.2 7.6 %collective-permute-start.22 = (f32[2,16,512]{2,1,0:T(8,128)}, f32[2,16,512]{2,1,0:T(8,128)}, u32[]{:S(2)}, u32[]{:S(2)}) collective-permute-start(f32[2,16,512]{2,1,0:T(8,128)} %fusion.6), channel_id=1, source_target_pairs={{14,0},{15,1},{0,2},{1,3},{2,4},{3,5},{4,6},{5,7},{6,8},{7,9},{8,1... | collective-permute-start | bytes 196616 | tf_op jit(solution)/shard_map/ppermute | solution.py:375
  329.2 10.5 %collective-permute-start.23 = (f32[2,16,512]{2,1,0:T(8,128)}, f32[2,16,512]{2,1,0:T(8,128)}, u32[]{:S(2)}, u32[]{:S(2)}) collective-permute-start(f32[2,16,512]{2,1,0:T(8,128)} %fusion.6), channel_id=1, source_target_pairs={{12,0},{13,1},{14,2},{15,3},{0,4},{1,5},{2,6},{3,7},{4,8},{5,9},{6... | collective-permute-start | bytes 196616 | tf_op jit(solution)/shard_map/ppermute | solution.py:375
  330.2 1.3 copy-start.4
  331.5 18.6 %collective-permute-start.24 = (f32[2,16,512]{2,1,0:T(8,128)}, f32[2,16,512]{2,1,0:T(8,128)S(1)}, u32[]{:S(2)}, u32[]{:S(2)}) collective-permute-start(f32[2,16,512]{2,1,0:T(8,128)} %fusion.6), channel_id=1, source_target_pairs={{10,0},{11,1},{12,2},{13,3},{14,4},{15,5},{0,6},{1,7},{2,8},{3,9},... | collective-permute-start | bytes 196616 | tf_op jit(solution)/shard_map/ppermute | solution.py:375
  333.3 16.8 %collective-permute-start.25 = (f32[2,16,512]{2,1,0:T(8,128)}, f32[2,16,512]{2,1,0:T(8,128)S(1)}, u32[]{:S(2)}, u32[]{:S(2)}) collective-permute-start(f32[2,16,512]{2,1,0:T(8,128)} %fusion.6), channel_id=1, source_target_pairs={{8,0},{9,1},{10,2},{11,3},{12,4},{13,5},{14,6},{15,7},{0,8},{1,9},... | collective-permute-start | bytes 196616 | tf_op jit(solution)/shard_map/ppermute | solution.py:375
  336.7 13.3 %collective-permute-start.26 = (f32[2,16,512]{2,1,0:T(8,128)}, f32[2,16,512]{2,1,0:T(8,128)S(1)}, u32[]{:S(2)}, u32[]{:S(2)}) collective-permute-start(f32[2,16,512]{2,1,0:T(8,128)} %fusion.6), channel_id=1, source_target_pairs={{6,0},{7,1},{8,2},{9,3},{10,4},{11,5},{12,6},{13,7},{14,8},{15,9},... | collective-permute-start | bytes 196616 | tf_op jit(solution)/shard_map/ppermute | solution.py:375
  336.7 13.3 %collective-permute-start.27 = (f32[2,16,512]{2,1,0:T(8,128)}, f32[2,16,512]{2,1,0:T(8,128)S(1)}, u32[]{:S(2)}, u32[]{:S(2)}) collective-permute-start(f32[2,16,512]{2,1,0:T(8,128)} %fusion.6), channel_id=1, source_target_pairs={{4,0},{5,1},{6,2},{7,3},{8,4},{9,5},{10,6},{11,7},{12,8},{13,9},{1... | collective-permute-start | bytes 196616 | tf_op jit(solution)/shard_map/ppermute | solution.py:375
  339.7 10.4 %collective-permute-start.28 = (f32[2,16,512]{2,1,0:T(8,128)}, f32[2,16,512]{2,1,0:T(8,128)S(1)}, u32[]{:S(2)}, u32[]{:S(2)}) collective-permute-start(f32[2,16,512]{2,1,0:T(8,128)} %fusion.6), channel_id=1, source_target_pairs={{2,0},{3,1},{4,2},{5,3},{6,4},{7,5},{8,6},{9,7},{10,8},{11,9},{12,... | collective-permute-start | bytes 196616 | tf_op jit(solution)/shard_map/ppermute | solution.py:375
  341.5 1.6 copy-start.5
  343.1 1.2 copy-start.20
  344.3 5.8 %copy-start.12 = (f32[2,2,16,512]{3,2,1,0:T(8,128)S(1)}, f32[2,2,16,512]{3,2,1,0:T(8,128)}, u32[]{:S(2)}) copy-start(f32[2,2,16,512]{3,2,1,0:T(8,128)} %copy-done.11) | copy-start | bytes 393220
  344.3 5.8 %copy-start.23 = (f32[16,512]{1,0:T(8,128)S(1)}, f32[16,512]{1,0:T(8,128)}, u32[]{:S(2)}) copy-start(f32[16,512]{1,0:T(8,128)} %get-tuple-element.38) | copy-start | bytes 98308
  344.3 5.8 %copy-start.24 = (f32[16,512]{1,0:T(8,128)S(1)}, f32[16,512]{1,0:T(8,128)}, u32[]{:S(2)}) copy-start(f32[16,512]{1,0:T(8,128)} %get-tuple-element.39) | copy-start | bytes 98308
  344.3 5.8 %copy-start.25 = (f32[16,512]{1,0:T(8,128)S(1)}, f32[16,512]{1,0:T(8,128)}, u32[]{:S(2)}) copy-start(f32[16,512]{1,0:T(8,128)} %get-tuple-element.40) | copy-start | bytes 98308
  344.3 5.8 %copy-start.26 = (f32[16,512]{1,0:T(8,128)S(1)}, f32[16,512]{1,0:T(8,128)}, u32[]{:S(2)}) copy-start(f32[16,512]{1,0:T(8,128)} %get-tuple-element.41) | copy-start | bytes 98308
  344.3 5.8 %copy-start.27 = (f32[16,512]{1,0:T(8,128)S(1)}, f32[16,512]{1,0:T(8,128)}, u32[]{:S(2)}) copy-start(f32[16,512]{1,0:T(8,128)} %get-tuple-element.42) | copy-start | bytes 98308
  344.3 5.8 %copy-start.28 = (f32[16,512]{1,0:T(8,128)S(1)}, f32[16,512]{1,0:T(8,128)}, u32[]{:S(2)}) copy-start(f32[16,512]{1,0:T(8,128)} %get-tuple-element.43) | copy-start | bytes 98308
  344.3 5.8 %copy-start.29 = (f32[16,512]{1,0:T(8,128)S(1)}, f32[16,512]{1,0:T(8,128)}, u32[]{:S(2)}) copy-start(f32[16,512]{1,0:T(8,128)} %get-tuple-element.44) | copy-start | bytes 98308
  344.3 6.8 %copy-start.6 = (bf16[256,512]{1,0:T(8,128)(2,1)S(1)}, bf16[256,512]{1,0:T(8,128)(2,1)}, u32[]{:S(2)}) copy-start(bf16[256,512]{1,0:T(8,128)(2,1)} %get-tuple-element.47.low_ref) | copy-start | bytes 786436
  344.4 6.8 %copy-start.7 = (bf16[256,512]{1,0:T(8,128)(2,1)S(1)}, bf16[256,512]{1,0:T(8,128)(2,1)}, u32[]{:S(2)}) copy-start(bf16[256,512]{1,0:T(8,128)(2,1)} %get-tuple-element.48.high_ref) | copy-start | bytes 786436
  354.4 12.0 %collective-permute-start.29 = (bf16[512,512]{1,0:T(8,128)(2,1)S(1)}, bf16[512,512]{1,0:T(8,128)(2,1)S(1)}, u32[]{:S(2)}, u32[]{:S(2)}) collective-permute-start(bf16[512,512]{1,0:T(8,128)(2,1)S(1)} %dynamic-slice_bitcast_fusion), channel_id=1, source_target_pairs={{0,16},{16,0},{1,17},{17,1},{2,18},{18,2},{3,19},{19,3},{4,20},{20... | collective-permute-start | bytes 1572872 | tf_op jit(solution)/shard_map/ppermute | solution.py:415
  366.6 2.0 collective-permute-start.30
  (1 other events, 0.7 us)

commit v3 on v2

--- a/solution.py
+++ b/solution.py
@@ -75,7 +75,44 @@
     return total
 
 
-def medium_kernel(x_ref, rim_ref, taps_ref, table_ref, out_ref):
+def medium_kernel(cores, x_ref, rim_ref, taps_ref, table_ref, *refs):
+    if cores == 2:
+        wo_ref, wi_ref, out_ref, wo_all, wi_all, send_sem, recv_sem = refs
+        count = lax.axis_size("seq")
+        me = lax.axis_index("seq")
+        chips = count // cores
+
+        def copies():
+            made = []
+            for which, (own, everyone) in enumerate(((wo_ref, wo_all), (wi_ref, wi_all))):
+                for step in range(1, chips):
+                    made.append(
+                        pltpu.make_async_remote_copy(
+                            src_ref=own,
+                            dst_ref=everyone.at[step - 1],
+                            send_sem=send_sem.at[which, step - 1],
+                            recv_sem=recv_sem.at[which, step - 1],
+                            device_id={"seq": lax.rem(me + count - step * cores, count)},
+                            device_id_type=pl.DeviceIdType.MESH,
+                        )
+                    )
+            return made
+
+        @pl.when(pl.program_id(0) == 0)
+        def _():
+            barrier = pltpu.get_barrier_semaphore()
+            for step in range(1, chips):
+                pl.semaphore_signal(
+                    barrier,
+                    inc=1,
+                    device_id={"seq": lax.rem(me + step * cores, count)},
+                    device_id_type=pl.DeviceIdType.MESH,
+                )
+            pl.semaphore_wait(barrier, chips - 1)
+            for copy in copies():
+                copy.start()
+    else:
+        (out_ref,) = refs
     own = x_ref.shape[1]
     ahead = BLK + RIM
 
@@ -94,27 +131,42 @@
         out_ref[(n + 1) * BLK : (n + 2) * BLK] = (q[(n + 1) * BLK : (n + 2) * BLK] * y1).astype(bf16)
 
 
-def medium(features, rim, taps, table):
+    if cores == 2:
+
+        @pl.when(pl.program_id(0) == pl.num_programs(0) - 1)
+        def _():
+            for copy in copies():
+                copy.wait()
+
+
+def medium(features, rim, taps, table, weights, cores):
     _, own, channels = features.shape
-    return pl.pallas_call(
-        medium_kernel,
+    chips = lax.axis_size("seq") // cores
+    others = [jax.ShapeDtypeStruct((chips - 1,) + w.shape, w.dtype) for w in weights]
+    anywhere = pl.BlockSpec(memory_space=pl.ANY)
+    scratch = [pltpu.SemaphoreType.DMA((2, chips - 1))] * 2 if weights else []
+    extra = dict(collective_id=0, has_side_effects=True) if weights else {}
+    return pl.pallas_call(
+        functools.partial(medium_kernel, cores),
         grid=(channels // LANES,),
         in_specs=[
             pl.BlockSpec((3, own, LANES), lambda i: (0, 0, i)),
             pl.BlockSpec((rim.shape[0], LANES), lambda i: (0, i)),
             pl.BlockSpec((3, SHORT, LANES), lambda i: (0, 0, i)),
             pl.BlockSpec((PER * BLK, 2 * BLK), lambda i: (i, 0)),
-        ],
-        out_specs=pl.BlockSpec((own, LANES), lambda i: (0, i)),
-        out_shape=jax.ShapeDtypeStruct((own, channels), bf16),
-        compiler_params=params(),
+        ]
+        + [anywhere] * len(weights),
+        out_specs=[pl.BlockSpec((own, LANES), lambda i: (0, i))] + [anywhere] * len(weights),
+        out_shape=[jax.ShapeDtypeStruct((own, channels), bf16)] + others,
+        scratch_shapes=scratch,
+        compiler_params=pltpu.CompilerParams(vmem_limit_bytes=40 * 1024 * 1024, **extra),
         cost_estimate=cost(channels // LANES * 2 * 1024 * 256 * 256, 16 * 2**20),
         name="medium",
-    )(features, rim, taps, table)
-
-
-def out_kernel(a_ref, b_ref, *refs):
-    pieces, (mine, theirs) = refs[:-2], refs[-2:]
+    )(features, rim, taps, table, *weights)
+
+
+def out_kernel(a_ref, b_ref, own_ref, all_ref, mine, theirs):
+    pieces = [own_ref] + [all_ref.at[j] for j in range(all_ref.shape[0])]
     for n in range(0, len(pieces), 2):
         weight = jnp.concatenate([pieces[n][...], pieces[n + 1][...]], axis=1)
         for source, target in ((a_ref, mine), (b_ref, theirs)):
@@ -124,16 +176,16 @@
             target[n + 1] = result[:, half:]
 
 
-def out_projection(gated, other, pieces):
+def out_projection(gated, other, own, everyone):
     rows = gated.shape[0]
-    shape = jax.ShapeDtypeStruct((len(pieces), rows, pieces[0].shape[1]), f32)
+    shape = jax.ShapeDtypeStruct((everyone.shape[0] + 1, rows, own.shape[1]), f32)
     return pl.pallas_call(
         out_kernel,
         out_shape=[shape, shape],
         compiler_params=params(),
         cost_estimate=cost(2**31, 9 * 2**20),
         name="out_projection",
-    )(gated, other, *pieces)
+    )(gated, other, own, everyone)
 
 
 def stream_kernel(where_ref, mine_ref, recv_ref, in_ref, gain_ref, stream_ref, normed_ref):
@@ -186,7 +238,8 @@
 
 
 def in_kernel(wide, chips, where_ref, ahead_ref, *refs):
-    sources, pieces, out_ref = refs[: 2 * wide], refs[2 * wide : -1], refs[-1]
+    sources, (own_ref, all_ref, out_ref) = refs[: 2 * wide], refs[2 * wide :]
+    pieces = [own_ref] + [all_ref.at[j] for j in range(chips - 1)]
     side, core, chip = where_ref[2], where_ref[1], where_ref[0]
     rows = sources[0].shape[1]
 
@@ -206,10 +259,10 @@
             out_ref[at, pl.ds(start, rows)] = result.astype(bf16)
 
 
-def in_projection(where, ahead, sources, pieces):
+def in_projection(where, ahead, sources, own, everyone):
     wide = len(sources) // 2
     chips, rows, depth = sources[0].shape
-    columns = pieces[0].shape[1]
+    columns = own.shape[1]
     step = 256
     fixed = pl.BlockSpec((chips, rows, depth), lambda n: (0, 0, 0))
     total = RIM + 2 * rows
@@ -221,13 +274,16 @@
             pl.BlockSpec(ahead.shape, lambda n: (0, 0, 0, 0)),
         ]
         + [fixed] * len(sources)
-        + [pl.BlockSpec((depth, step), lambda n: (0, n))] * chips,
+        + [
+            pl.BlockSpec((depth, step), lambda n: (0, n)),
+            pl.BlockSpec((chips - 1, depth, step), lambda n: (0, 0, n)),
+        ],
         out_specs=pl.BlockSpec((wide, total, step), lambda n: (0, 0, n)),
         out_shape=jax.ShapeDtypeStruct((wide, total, columns), bf16),
         compiler_params=params(),
         cost_estimate=cost(2 * wide * total * chips * depth * columns, 14 * 2**20),
         name="in_projection",
-    )(where, ahead, *sources, *pieces)
+    )(where, ahead, *sources, own, everyone)
 
 
 def product_kernel(segs, k_ref, v_ref, taps_ref, high_ref, low_ref, product_ref, state_ref):
@@ -375,10 +431,6 @@
     return lax.ppermute(
         value, "seq", [((s + steps * cores) % count, s) for s in range(count)]
     )
-
-
-def spread_pieces(piece, chips, cores):
-    return [piece] + [turn(piece, step, cores) for step in range(1, chips)]
 
 
 def body(
@@ -426,7 +478,6 @@
     rim = shift_seq(rim, 1)
 
     if cores == 2:
-        out_pieces = spread_pieces(mr_out_weight, chips, cores)
         weight = li_in_weight.reshape(-1, 3, share, part)
         mine = lax.dynamic_index_in_dim(weight, side * cores + core, 2, keepdims=False)
         theirs = lax.dynamic_index_in_dim(weight, side * cores + 1 - core, 2, keepdims=False)
@@ -461,14 +512,18 @@
     short_part = lax.dynamic_slice_in_dim(li_short, quarter * part, part, 2)
     short_part = jnp.transpose(short_part, (1, 0, 2))
 
-    if cores == 2:
-        in_piece, medium_table = lax.optimization_barrier((in_piece, medium_table))
-        in_pieces = spread_pieces(in_piece, chips, cores)
-    gated = medium(features, rim, jnp.transpose(mr_short, (1, 0, 2)), medium_table)
+    gated, *gathered = medium(
+        features,
+        rim,
+        jnp.transpose(mr_short, (1, 0, 2)),
+        medium_table,
+        [mr_out_weight, in_piece] if cores == 2 else [],
+        cores,
+    )
 
     if cores == 2:
         where = jnp.stack([seq_rank // cores, core, jnp.asarray(side, jnp.int32)])
-        mine, theirs = out_projection(gated, swap_core(gated), out_pieces)
+        mine, theirs = out_projection(gated, swap_core(gated), mr_out_weight, gathered[0])
         stream, normed = stream_norm(where, mine, swap_core(theirs), stream_in, li_gain[None])
         sources = []
         for own in [normed] + ([swap_side(normed)] if wide == 2 else []):
@@ -480,7 +535,10 @@
             ]
         )
         ahead = jnp.roll(turn(ahead, -1, cores), -1, axis=1)
-        projected = in_projection(where, ahead, sources, in_pieces)
+        tables = (long_table, spread_high, spread_low, tail_high, tail_low, seg_decay, gap_decays)
+        ahead, short_part, tables = lax.optimization_barrier((ahead, short_part, tables))
+        long_table, spread_high, spread_low, tail_high, tail_low, seg_decay, gap_decays = tables
+        projected = in_projection(where, ahead, sources, in_piece, gathered[1])
     else:
         summed = lax.psum(jnp.dot(gated, out_weight, preferred_element_type=f32), "tensor")
         stream = (stream_in.astype(f32) + summed).astype(bf16)

time: 372 us -> 370 us (level)
  Pallas kernels: 52.8 us -> 270 us
  starting transfers between devices: 128 us -> 16.5 us
  waiting for transfers between devices: 152 us -> 50 us
  local copies, waits for them, and re-layouts: 26.5 us -> 22 us
    pallas_call x1, Pallas kernels: 14.1 us -> 233 us  [medium(): pl.pallas_call(functools.partial(medium_kernel, cores), grid=(channels //...]
    ppermute x22 -> x8, waiting for transfers between devices: 113 us -> 7.68 us  [turn(): lax.ppermute(value, 'seq', [((s + steps * cores) % count, s) for s in ran...]
    ppermute x22 -> x8, starting transfers between devices: 113 us -> 7.97 us  [turn(): lax.ppermute(value, 'seq', [((s + steps * cores) % count, s) for s in ran...]
    ppermute x6, starting transfers between devices: 8.61 us -> 1.97 us  [swap_core(): return lax.ppermute(value, 'seq', swap_pairs)]
    unnamed x75 -> x55, local copies, waits for them, and re-layouts: 19 us -> 14.4 us
  transfers between devices with their start and end apart: 31 -> 17, of which waited for: 10 -> 7; matrix products, arithmetic and copies ran while one was open for 4% -> 4% of each run, Pallas kernels for 7% -> 3%
where the time goes in v3:
time: 370 us; the launch traced here: 369 us
  Pallas kernels  270 us (73%)
  waiting for transfers between devices  50 us (14%)
  local copies, waits for them, and re-layouts  22 us (6%)
  starting transfers between devices  16.5 us (4%)
  other arithmetic  9.92 us (3%)
    pallas_call x1, Pallas kernels, medium(): pl.pallas_call(functools.partial(medium_kernel, cores), grid=(channels //...  233 us
    ppermute x2, waiting for transfers between devices, swap_side(): return lax.ppermute(value, 'parts', [(0, 1), (1, 0)])  35.1 us
    unnamed x55, local copies, waits for them, and re-layouts  14.4 us
    pallas_call x1, Pallas kernels, in_projection(): pl.pallas_call(functools.partial(in_kernel, wide, chips), grid=(columns /...  11.5 us
    ppermute x8, starting transfers between devices, turn(): lax.ppermute(value, 'seq', [((s + steps * cores) % count, s) for s in ran...  7.97 us
    ppermute x8, waiting for transfers between devices, turn(): lax.ppermute(value, 'seq', [((s + steps * cores) % count, s) for s in ran...  7.68 us
  transfers between devices with their start and end apart: 17, of which 7 were waited for; matrix products, arithmetic and copies ran while one was open for 4% of the time, Pallas kernels for 3%

profile of v3, /device:TPU:0, one launch (start us, length us, event | category | flops | bytes accessed | tf_op | source)
XLA Modules:
  0.0 369.2 jit_solution(8333319870645587166)
XLA Ops:
  0.7 1.0 slice_bitcast_fusion.4
  1.6 1.3 slice_bitcast_fusion.1
  3.0 1.1 pad_maximum_fusion
  4.1 3.5 collective-permute-start
  7.6 0.9 copy.45
  8.5 0.9 constant_dynamic-slice_fusion.1
  9.5 1.6 collective-permute-start.1
  11.1 0.1 copy.44
  11.2 0.2 reverse.4
  11.4 0.1 slice.144
  11.5 3.5 toeplitz.2.table_ref
  15.0 3.3 copy-done.1
  18.3 1.2 bitcast_select_fusion.3
  19.5 0.9 pad_maximum_fusion.1
  20.5 2.3 copy.46
  22.8 1.1 copy-done.3
  23.9 1.0 copy-done.9
  25.0 232.6 %medium.1 = (bf16[256,2048]{1,0:T(8,128)(2,1)S(1)}, bf16[7,2048,128]{2,1,0:T(8,128)(2,1)S(1)}, bf16[7,256,1536]{2,1,0:T(8,128)(2,1)}) custom-call(bf16[3,256,2048]{2,1,0:T(8,128)(2,1)S(1)} %bitcast.85, bf16[304,2048]{1,0:T(8,128)(2,1)} %collective-permute-done.rim_ref, f32[3,7,2048]{2,1,0:T(8,128)S(1)} %bitcast.88, bf16[16384,256]{1,0:T(8,128)(2,1)} %copy-done.1, ...), custom_call_target="tpu_custom_call" | custom-call | flops 2147483648 | bytes 16777216 | tf_op jit(solution)/shard_map/medium/pallas_call | solution.py:149
  257.6 2.6 collective-permute-done.2.b_ref
  260.3 3.3 out_projection.1
  263.6 0.1 collective-permute-start.3
  263.7 0.1 pad_add_fusion.where_ref
  263.8 2.7 collective-permute-done.3.recv_ref
  266.5 2.9 stream_norm.1
  269.3 1.5 collective-permute-start.5
  270.8 0.1 sqrt_multiply_fusion
  271.1 0.1 broadcast_in_dim.26
  271.2 0.2 neg.34
  271.5 0.2 multiply_reduce_fusion
  271.7 23.0 %collective-permute-done.5.refs_2_ = bf16[8,256,256]{2,1,0:T(8,128)(2,1)S(1)} collective-permute-done((bf16[8,256,256]{2,1,0:T(8,128)(2,1)}, bf16[8,256,256]{2,1,0:T(8,128)(2,1)S(1)}, u32[]{:S(2)}, u32[]{:S(2)}) %collective-permute-start.5) | collective-permute-done | bytes 1048608 | tf_op jit(solution)/shard_map/ppermute | solution.py:467
  294.8 0.1 neg.32
  294.8 0.1 mul.185
  295.0 0.7 slice.95
  295.7 0.1 reverse.5
  295.9 0.1 slice.145
  295.9 0.8 exponential_select_fusion
  296.7 1.0 fusion.1
  297.7 0.9 fusion
  298.6 0.9 fusion.8
  299.5 1.0 copy-done.15
  300.4 0.9 fusion.7
  301.3 0.7 pad_maximum_fusion.2
  301.9 0.8 pad_maximum_fusion.5.base_ref
  302.7 0.9 toeplitz.3.table_ref
  303.6 7.1 %collective-permute-done.7 = bf16[2,8,16,256]{3,2,1,0:T(8,128)(2,1)S(1)} collective-permute-done((bf16[2,8,16,256]{3,2,1,0:T(8,128)(2,1)}, bf16[2,8,16,256]{3,2,1,0:T(8,128)(2,1)S(1)}, u32[]{:S(2)}, u32[]{:S(2)}) %collective-permute-start.7) | collective-permute-done | bytes 131104 | tf_op jit(solution)/shard_map/ppermute | solution.py:431
  310.8 1.2 copy-done.14
  312.0 1.2 copy-done.16
  313.2 2.6 copy-done.17
  315.8 11.5 %in_projection.1.k_ref.v_ref.q_ref = bf16[2,528,1536]{2,1,0:T(8,128)(2,1)S(1)} custom-call(s32[3]{0:T(128)S(1)} %pad_add_fusion.where_ref, bf16[2,8,16,256]{3,2,1,0:T(8,128)(2,1)S(1)} %pad_maximum_fusion.3.ahead_ref, bf16[8,256,256]{2,1,0:T(8,128)(2,1)} %get-tuple-element.27.refs_0_, bf16[8,256,256]{2,1,0:T(8,128)(2,1)S(1)} %copy-done.16, ...), custom_call_target="tpu_custom_call" | custom-call | flops 6643777536 | bytes 14680064 | tf_op jit(solution)/shard_map/in_projection/pallas_call | solution.py:269
  327.3 6.3 %product.1 = (bf16[2,512,512]{2,1,0:T(8,128)(2,1)S(1)}, f32[2,2,16,512]{3,2,1,0:T(8,128)S(1)}) custom-call(bf16[2,528,1536]{2,1,0:T(8,128)(2,1)S(1)} %in_projection.1.k_ref.v_ref.q_ref, bf16[2,528,1536]{2,1,0:T(8,128)(2,1)S(1)} %in_projection.1.k_ref.v_ref.q_ref, f32[3,7,512]{2,1,0:T(8,128)S(1)} %dynamic-slice_bitcast_fusion.1.taps_ref, ...), custom_call_target="tpu_custom_call" | custom-call | flops 268435456 | bytes 8388608 | tf_op jit(solution)/shard_map/product/pallas_call | solution.py:345
  333.8 1.1 collective-permute-start.12
  334.8 3.3 collective-permute-start.11
  338.1 2.1 collective-permute-start.9
  340.2 1.5 collective-permute-start.8
  341.6 5.7 %local.1 = (f32[2,512,512]{2,1,0:T(8,128)S(1)}, f32[2,512,512]{2,1,0:T(8,128)S(1)}) custom-call(bf16[2,528,1536]{2,1,0:T(8,128)(2,1)S(1)} %in_projection.1.k_ref.v_ref.q_ref, f32[3,7,512]{2,1,0:T(8,128)S(1)} %dynamic-slice_bitcast_fusion.1.taps_ref, bf16[2,512,512]{2,1,0:T(8,128)(2,1)S(1)} %get-tuple-element.33.product_ref, ...), custom_call_target="tpu_custom_call" | custom-call | flops 2147483648 | bytes 16777216 | tf_op jit(solution)/shard_map/local/pallas_call | solution.py:374
  347.3 0.6 collective-permute-done.10
  348.0 3.2 finish.1
  351.3 1.6 collective-permute-start.15
  352.8 12.1 %collective-permute-done.15 = bf16[512,512]{1,0:T(8,128)(2,1)S(1)} collective-permute-done((bf16[512,512]{1,0:T(8,128)(2,1)S(1)}, bf16[512,512]{1,0:T(8,128)(2,1)S(1)}, u32[]{:S(2)}, u32[]{:S(2)}) %collective-permute-start.15) | collective-permute-done | bytes 524320 | tf_op jit(solution)/shard_map/ppermute | solution.py:467
  365.1 1.9 collective-permute-done.16
  367.0 0.1 select_bitcast_fusion.1
  367.1 0.1 maximum_bitcast_fusion
  367.2 0.5 copy.54
  367.7 1.4 copy.55
  (79 shorter events, 1.0 us)
Async XLA Ops:
  0.6 303.0 %copy-start = (f32[7,3,2048]{2,0,1:T(8,128)S(1)}, f32[7,3,2048]{2,0,1:T(8,128)}, u32[]{:S(2)}) copy-start(f32[7,3,2048]{2,0,1:T(8,128)} %param.17) | copy-start | bytes 516100
  0.6 7.0 %copy-start.18 = (bf16[128,3,2048]{2,0,1:T(8,128)(2,1)S(1)}, bf16[128,3,2048]{2,0,1:T(8,128)(2,1)}, u32[]{:S(2)}) copy-start(bf16[128,3,2048]{2,0,1:T(8,128)(2,1)} %param.16) | copy-start | bytes 4718596
  4.1 7.0 %copy-start.21 = (f32[128,128]{1,0:T(8,128)S(1)}, f32[128,128]{1,0:T(8,128)}, u32[]{:S(2)}) copy-start(f32[128,128]{1,0:T(8,128)} %param.13) | copy-start | bytes 196612
  4.1 18.7 %collective-permute-start = (bf16[304,2048]{1,0:T(8,128)(2,1)}, bf16[304,2048]{1,0:T(8,128)(2,1)}, u32[]{:S(2)}, u32[]{:S(2)}) collective-permute-start(bf16[304,2048]{1,0:T(8,128)(2,1)} %pad_maximum_fusion), channel_id=1, source_target_pairs={{0,1},{1,2},{2,3},{3,4},{4,5},{5,6},{6,7},{7,8},{8,9},{9,10},{10,1... | collective-permute-start | bytes 3735560 | tf_op jit(solution)/shard_map/ppermute | solution.py:421
  9.5 8.9 %collective-permute-start.1 = (bf16[128,1536]{0,1:T(8,128)(2,1)}, bf16[128,1536]{0,1:T(8,128)(2,1)}, u32[]{:S(2)}, u32[]{:S(2)}) collective-permute-start(bf16[128,1536]{0,1:T(8,128)(2,1)} %bitcast.11), channel_id=1, source_target_pairs={{0,1},{1,0},{2,3},{3,2},{4,5},{5,4},{6,7},{7,6},{8,9},{9,8},{10,11... | collective-permute-start | bytes 1179656 | tf_op jit(solution)/shard_map/ppermute | solution.py:464
  11.5 6.8 %copy-start.19 = (bf16[128,3,1,512]{0,3,2,1:T(8,128)(2,1)S(1)}, bf16[128,3,1,512]{0,3,2,1:T(8,128)(2,1)}, u32[]{:S(2)}) copy-start(bf16[128,3,1,512]{0,3,2,1:T(8,128)(2,1)} %get-tuple-element.54) | copy-start | bytes 1179652
  15.0 3.3 copy-start.1
  18.3 4.5 %copy-start.2 = (bf16[256,3,2048]{2,0,1:T(8,128)(2,1)S(1)}, bf16[256,3,2048]{2,0,1:T(8,128)(2,1)}, u32[]{:S(2)}) copy-start(bf16[256,3,2048]{2,0,1:T(8,128)(2,1)} %param.11) | copy-start | bytes 9437188
  18.3 4.5 %copy-start.11 = (f32[7,3,2048]{2,0,1:T(8,128)S(1)}, f32[7,3,2048]{2,0,1:T(8,128)}, u32[]{:S(2)}) copy-start(f32[7,3,2048]{2,0,1:T(8,128)} %param.12) | copy-start | bytes 516100
  22.8 1.1 copy-start.3
  23.9 1.0 copy-start.9
  25.0 235.3 %copy-start.10 = (bf16[2048,128]{1,0:T(8,128)(2,1)S(1)}, bf16[2048,128]{1,0:T(8,128)(2,1)}, u32[]{:S(2)}) copy-start(bf16[2048,128]{1,0:T(8,128)(2,1)} %own_ref.1) | copy-start | bytes 1572868
  257.6 2.7 collective-permute-start.2
  260.3 6.2 %copy-start.8 = (bf16[256,2048]{1,0:T(8,128)(2,1)S(1)}, bf16[256,2048]{1,0:T(8,128)(2,1)}, u32[]{:S(2)}) copy-start(bf16[256,2048]{1,0:T(8,128)(2,1)} %in_ref.1) | copy-start | bytes 3145732
  260.3 6.2 %copy-start.12 = (f32[2048]{0:T(1024)S(1)}, f32[2048]{0:T(1024)}, u32[]{:S(2)}) copy-start(f32[2048]{0:T(1024)} %param.15) | copy-start | bytes 24580
  263.6 7.2 %copy-start.22 = (f32[128,16]{0,1:T(8,128)S(1)}, f32[128,16]{0,1:T(8,128)}, u32[]{:S(2)}) copy-start(f32[128,16]{0,1:T(8,128)} %param.19) | copy-start | bytes 24580
  263.6 7.2 %copy-start.23 = (f32[128,16]{0,1:T(8,128)S(1)}, f32[128,16]{0,1:T(8,128)}, u32[]{:S(2)}) copy-start(f32[128,16]{0,1:T(8,128)} %param.18) | copy-start | bytes 24580
  263.6 2.9 collective-permute-start.3
  269.3 25.4 %collective-permute-start.5 = (bf16[8,256,256]{2,1,0:T(8,128)(2,1)}, bf16[8,256,256]{2,1,0:T(8,128)(2,1)S(1)}, u32[]{:S(2)}, u32[]{:S(2)}) collective-permute-start(bf16[8,256,256]{2,1,0:T(8,128)(2,1)} %get-tuple-element.27.refs_0_), channel_id=1, source_target_pairs={{0,16},{16,0},{1,17},{17,1},{2,18},{18,2},{3,19},{19,3},{4,20},{20... | collective-permute-start | bytes 3145736 | tf_op jit(solution)/shard_map/ppermute | solution.py:467
  271.4 27.2 %collective-permute-start.4 = (bf16[8,256,256]{2,1,0:T(8,128)(2,1)}, bf16[8,256,256]{2,1,0:T(8,128)(2,1)S(1)}, u32[]{:S(2)}, u32[]{:S(2)}) collective-permute-start(bf16[8,256,256]{2,1,0:T(8,128)(2,1)} %get-tuple-element.27.refs_0_), channel_id=1, source_target_pairs={{0,1},{1,0},{2,3},{3,2},{4,5},{5,4},{6,7},{7,6},{8,9},{9,8},{10,11... | collective-permute-start | bytes 3145736 | tf_op jit(solution)/shard_map/ppermute | solution.py:464
  294.7 8.0 %copy-start.13 = (bf16[8,256,256]{2,1,0:T(8,128)(2,1)}, bf16[8,256,256]{2,1,0:T(8,128)(2,1)S(1)}, u32[]{:S(2)}) copy-start(bf16[8,256,256]{2,1,0:T(8,128)(2,1)S(1)} %collective-permute-done.5.refs_2_) | copy-start | bytes 3145732
  294.8 5.7 %collective-permute-start.6 = (bf16[8,256,256]{2,1,0:T(8,128)(2,1)S(1)}, bf16[8,256,256]{2,1,0:T(8,128)(2,1)}, u32[]{:S(2)}, u32[]{:S(2)}) collective-permute-start(bf16[8,256,256]{2,1,0:T(8,128)(2,1)S(1)} %collective-permute-done.5.refs_2_), channel_id=1, source_target_pairs={{0,1},{1,0},{2,3},{3,2},{4,5},{5,4},{6,7},{7,6},{8,9},{9,8},{10,11... | collective-permute-start | bytes 3145736 | tf_op jit(solution)/shard_map/ppermute | solution.py:464
  295.7 15.1 %copy-start.4 = (bf16[2,128,1536]{2,1,0:T(8,128)(2,1)S(1)}, bf16[2,128,1536]{2,1,0:T(8,128)(2,1)}, u32[]{:S(2)}) copy-start(bf16[2,128,1536]{2,1,0:T(8,128)(2,1)} %copy.46) | copy-start | bytes 2359300
  299.4 1.0 copy-start.15
  301.9 8.8 %collective-permute-start.7 = (bf16[2,8,16,256]{3,2,1,0:T(8,128)(2,1)}, bf16[2,8,16,256]{3,2,1,0:T(8,128)(2,1)S(1)}, u32[]{:S(2)}, u32[]{:S(2)}) collective-permute-start(bf16[2,8,16,256]{3,2,1,0:T(8,128)(2,1)} %pad_maximum_fusion.2), channel_id=1, source_target_pairs={{14,0},{15,1},{0,2},{1,3},{2,4},{3,5},{4,6},{5,7},{6,8},{7,9},{8,1... | collective-permute-start | bytes 393224 | tf_op jit(solution)/shard_map/ppermute | solution.py:431
  310.8 1.2 copy-start.14
  312.0 1.2 copy-start.16
  313.2 2.6 copy-start.17
  315.8 11.5 %copy-start.6 = (bf16[512,256]{1,0:T(8,128)(2,1)S(1)}, bf16[512,256]{1,0:T(8,128)(2,1)}, u32[]{:S(2)}) copy-start(bf16[512,256]{1,0:T(8,128)(2,1)} %get-tuple-element.32.low_ref) | copy-start | bytes 786436
  315.8 11.5 %copy-start.7 = (bf16[512,256]{1,0:T(8,128)(2,1)S(1)}, bf16[512,256]{1,0:T(8,128)(2,1)}, u32[]{:S(2)}) copy-start(bf16[512,256]{1,0:T(8,128)(2,1)} %get-tuple-element.31.high_ref) | copy-start | bytes 786436
  327.3 10.8 %copy-start.20 = (f32[7,16,512]{2,1,0:T(8,128)S(1)}, f32[7,16,512]{2,1,0:T(8,128)}, u32[]{:S(2)}) copy-start(f32[7,16,512]{2,1,0:T(8,128)} %exponential_select_fusion) | copy-start | bytes 688132
  333.6 4.5 %collective-permute-start.14 = (f32[2,16,512]{2,1,0:T(8,128)S(1)}, f32[2,16,512]{2,1,0:T(8,128)S(1)}, u32[]{:S(2)}, u32[]{:S(2)}) collective-permute-start(f32[2,16,512]{2,1,0:T(8,128)S(1)} %fusion.6), channel_id=1, source_target_pairs={{2,0},{3,1},{4,2},{5,3},{6,4},{7,5},{8,6},{9,7},{10,8},{11,9},{12,... | collective-permute-start | bytes 196616 | tf_op jit(solution)/shard_map/ppermute | solution.py:431
  333.7 6.5 %collective-permute-start.13 = (f32[2,16,512]{2,1,0:T(8,128)S(1)}, f32[2,16,512]{2,1,0:T(8,128)S(1)}, u32[]{:S(2)}, u32[]{:S(2)}) collective-permute-start(f32[2,16,512]{2,1,0:T(8,128)S(1)} %fusion.6), channel_id=1, source_target_pairs={{4,0},{5,1},{6,2},{7,3},{8,4},{9,5},{10,6},{11,7},{12,8},{13,9},{1... | collective-permute-start | bytes 196616 | tf_op jit(solution)/shard_map/ppermute | solution.py:431
  333.8 13.6 %collective-permute-start.12 = (f32[2,16,512]{2,1,0:T(8,128)S(1)}, f32[2,16,512]{2,1,0:T(8,128)S(1)}, u32[]{:S(2)}, u32[]{:S(2)}) collective-permute-start(f32[2,16,512]{2,1,0:T(8,128)S(1)} %fusion.6), channel_id=1, source_target_pairs={{6,0},{7,1},{8,2},{9,3},{10,4},{11,5},{12,6},{13,7},{14,8},{15,9},... | collective-permute-start | bytes 196616 | tf_op jit(solution)/shard_map/ppermute | solution.py:431
  334.8 12.5 %collective-permute-start.11 = (f32[2,16,512]{2,1,0:T(8,128)S(1)}, f32[2,16,512]{2,1,0:T(8,128)S(1)}, u32[]{:S(2)}, u32[]{:S(2)}) collective-permute-start(f32[2,16,512]{2,1,0:T(8,128)S(1)} %fusion.6), channel_id=1, source_target_pairs={{8,0},{9,1},{10,2},{11,3},{12,4},{13,5},{14,6},{15,7},{0,8},{1,9},... | collective-permute-start | bytes 196616 | tf_op jit(solution)/shard_map/ppermute | solution.py:431
  338.1 9.9 %collective-permute-start.10 = (f32[2,16,512]{2,1,0:T(8,128)S(1)}, f32[2,16,512]{2,1,0:T(8,128)S(1)}, u32[]{:S(2)}, u32[]{:S(2)}) collective-permute-start(f32[2,16,512]{2,1,0:T(8,128)S(1)} %fusion.6), channel_id=1, source_target_pairs={{10,0},{11,1},{12,2},{13,3},{14,4},{15,5},{0,6},{1,7},{2,8},{3,9},... | collective-permute-start | bytes 196616 | tf_op jit(solution)/shard_map/ppermute | solution.py:431
  338.1 9.8 %collective-permute-start.9 = (f32[2,16,512]{2,1,0:T(8,128)S(1)}, f32[2,16,512]{2,1,0:T(8,128)S(1)}, u32[]{:S(2)}, u32[]{:S(2)}) collective-permute-start(f32[2,16,512]{2,1,0:T(8,128)S(1)} %fusion.6), channel_id=1, source_target_pairs={{12,0},{13,1},{14,2},{15,3},{0,4},{1,5},{2,6},{3,7},{4,8},{5,9},{6... | collective-permute-start | bytes 196616 | tf_op jit(solution)/shard_map/ppermute | solution.py:431
  340.2 7.8 %collective-permute-start.8 = (f32[2,16,512]{2,1,0:T(8,128)S(1)}, f32[2,16,512]{2,1,0:T(8,128)S(1)}, u32[]{:S(2)}, u32[]{:S(2)}) collective-permute-start(f32[2,16,512]{2,1,0:T(8,128)S(1)} %fusion.6), channel_id=1, source_target_pairs={{14,0},{15,1},{0,2},{1,3},{2,4},{3,5},{4,6},{5,7},{6,8},{7,9},{8,1... | collective-permute-start | bytes 196616 | tf_op jit(solution)/shard_map/ppermute | solution.py:431
  341.6 6.4 %copy-start.5 = (bf16[256,512]{1,0:T(8,128)(2,1)S(1)}, bf16[256,512]{1,0:T(8,128)(2,1)}, u32[]{:S(2)}) copy-start(bf16[256,512]{1,0:T(8,128)(2,1)} %get-tuple-element.40.high_ref) | copy-start | bytes 786436
  351.3 13.6 %collective-permute-start.15 = (bf16[512,512]{1,0:T(8,128)(2,1)S(1)}, bf16[512,512]{1,0:T(8,128)(2,1)S(1)}, u32[]{:S(2)}, u32[]{:S(2)}) collective-permute-start(bf16[512,512]{1,0:T(8,128)(2,1)S(1)} %dynamic-slice_bitcast_fusion), channel_id=1, source_target_pairs={{0,16},{16,0},{1,17},{17,1},{2,18},{18,2},{3,19},{19,3},{4,20},{20... | collective-permute-start | bytes 1572872 | tf_op jit(solution)/shard_map/ppermute | solution.py:467
  365.1 2.0 collective-permute-start.16

commit v4 on v3

--- a/solution.py
+++ b/solution.py
@@ -82,17 +82,30 @@
         me = lax.axis_index("seq")
         chips = count // cores
 
-        def copies():
+        chip, core = me // cores, lax.rem(me, cores)
+        place = chip // 2 + lax.rem(chip, 2) * (chips - 1 - 2 * (chip // 2))
+
+        def chip_at(spot):
+            spot = lax.rem(spot + 2 * chips, chips)
+            column = spot // (chips // 2)
+            return 2 * (spot + column * (chips - 1 - 2 * spot)) + column
+
+        def copies(step):
             made = []
-            for which, (own, everyone) in enumerate(((wo_ref, wo_all), (wi_ref, wi_all))):
-                for step in range(1, chips):
+            for way, sign in enumerate((1, -1)):
+                owner, target = chip_at(place - sign * step), chip_at(place + sign)
+                for which, (own, everyone) in enumerate(((wo_ref, wo_all), (wi_ref, wi_all))):
+                    half = own.shape[0] // 2
+                    rows = pl.ds(way * half, half)
+                    here = lax.rem(owner - chip + chips, chips) - 1
+                    there = lax.rem(owner - target + chips, chips) - 1
                     made.append(
                         pltpu.make_async_remote_copy(
-                            src_ref=own,
-                            dst_ref=everyone.at[step - 1],
-                            send_sem=send_sem.at[which, step - 1],
-                            recv_sem=recv_sem.at[which, step - 1],
-                            device_id={"seq": lax.rem(me + count - step * cores, count)},
+                            src_ref=everyone.at[here, rows] if step else own.at[rows],
+                            dst_ref=everyone.at[there, rows],
+                            send_sem=send_sem.at[2 * way + which, step],
+                            recv_sem=recv_sem.at[2 * way + which, step],
+                            device_id={"seq": target * cores + core},
                             device_id_type=pl.DeviceIdType.MESH,
                         )
                     )
@@ -101,15 +114,15 @@
         @pl.when(pl.program_id(0) == 0)
         def _():
             barrier = pltpu.get_barrier_semaphore()
-            for step in range(1, chips):
+            for sign in (1, -1):
                 pl.semaphore_signal(
                     barrier,
                     inc=1,
-                    device_id={"seq": lax.rem(me + step * cores, count)},
+                    device_id={"seq": chip_at(place + sign) * cores + core},
                     device_id_type=pl.DeviceIdType.MESH,
                 )
-            pl.semaphore_wait(barrier, chips - 1)
-            for copy in copies():
+            pl.semaphore_wait(barrier, 2)
+            for copy in copies(0):
                 copy.start()
     else:
         (out_ref,) = refs
@@ -135,8 +148,15 @@
 
         @pl.when(pl.program_id(0) == pl.num_programs(0) - 1)
         def _():
-            for copy in copies():
-                copy.wait()
+            for step in range(1, chips - 1):
+                for before, copy in zip(copies(step - 1), copies(step)):
+                    before.wait_recv()
+                    copy.start()
+            for copy in copies(chips - 2):
+                copy.wait_recv()
+            for step in range(chips - 1):
+                for copy in copies(step):
+                    copy.wait_send()
 
 
 def medium(features, rim, taps, table, weights, cores):
@@ -144,7 +164,7 @@
     chips = lax.axis_size("seq") // cores
     others = [jax.ShapeDtypeStruct((chips - 1,) + w.shape, w.dtype) for w in weights]
     anywhere = pl.BlockSpec(memory_space=pl.ANY)
-    scratch = [pltpu.SemaphoreType.DMA((2, chips - 1))] * 2 if weights else []
+    scratch = [pltpu.SemaphoreType.DMA((4, chips - 1))] * 2 if weights else []
     extra = dict(collective_id=0, has_side_effects=True) if weights else {}
     return pl.pallas_call(
         functools.partial(medium_kernel, cores),

time: 370 us -> 243 us (0.66)
  Pallas kernels: 270 us -> 142 us
    pallas_call x1, Pallas kernels: 233 us -> 105 us  [medium(): pl.pallas_call(functools.partial(medium_kernel, cores), grid=(channels //...]
  transfers between devices with their start and end apart: 17 -> 17, of which waited for: 7 -> 7; matrix products, arithmetic and copies ran while one was open for 4% -> 5% of each run, Pallas kernels for 3% -> 4%
where the time goes in v4:
time: 243 us; the launch traced here: 242 us
  Pallas kernels  142 us (58%)
  waiting for transfers between devices  49 us (20%)
  local copies, waits for them, and re-layouts  22 us (9%)
  starting transfers between devices  18 us (7%)
  other arithmetic  9.92 us (4%)
    pallas_call x1, Pallas kernels, medium(): pl.pallas_call(functools.partial(medium_kernel, cores), grid=(channels //...  105 us
    ppermute x2, waiting for transfers between devices, swap_side(): return lax.ppermute(value, 'parts', [(0, 1), (1, 0)])  35.1 us
    unnamed x55, local copies, waits for them, and re-layouts  14.4 us
    pallas_call x1, Pallas kernels, in_projection(): pl.pallas_call(functools.partial(in_kernel, wide, chips), grid=(columns /...  11.5 us
    ppermute x8, starting transfers between devices, turn(): lax.ppermute(value, 'seq', [((s + steps * cores) % count, s) for s in ran...  9.48 us
    ppermute x6, waiting for transfers between devices, swap_core(): return lax.ppermute(value, 'seq', swap_pairs)  7.2 us
    ppermute x8, waiting for transfers between devices, turn(): lax.ppermute(value, 'seq', [((s + steps * cores) % count, s) for s in ran...  6.69 us
    pallas_call x1, Pallas kernels, long_product(): pl.pallas_call(functools.partial(product_kernel, segs), grid=(blocks, gro...  6.26 us
  transfers between devices with their start and end apart: 17, of which 7 were waited for; matrix products, arithmetic and copies ran while one was open for 5% of the time, Pallas kernels for 4%

profile of v4, /device:TPU:0, one launch (start us, length us, event | category | flops | bytes accessed | tf_op | source)
XLA Modules:
  0.0 242.4 jit_solution(3088266437003774970)
XLA Ops:
  0.7 1.0 slice_bitcast_fusion.4
  1.6 1.3 slice_bitcast_fusion.1
  3.0 1.1 pad_maximum_fusion
  4.1 3.5 %collective-permute-start = (bf16[304,2048]{1,0:T(8,128)(2,1)}, bf16[304,2048]{1,0:T(8,128)(2,1)}, u32[]{:S(2)}, u32[]{:S(2)}) collective-permute-start(bf16[304,2048]{1,0:T(8,128)(2,1)} %pad_maximum_fusion), channel_id=1, source_target_pairs={{0,1},{1,2},{2,3},{3,4},{4,5},{5,6},{6,7},{7,8},{8,9},{9,10},{10,1... | collective-permute-start | bytes 3735560 | tf_op jit(solution)/shard_map/ppermute | solution.py:441
  7.6 0.9 copy.45
  8.5 0.9 constant_dynamic-slice_fusion.1
  9.5 1.6 collective-permute-start.1
  11.1 0.1 copy.44
  11.2 0.2 reverse.4
  11.4 0.1 slice.144
  11.5 3.5 %toeplitz.2.table_ref = bf16[16384,256]{1,0:T(8,128)(2,1)S(1)} custom-call(f32[128,256]{1,0:T(8,128)S(1)} %concatenate.17.base_ref), custom_call_target="tpu_custom_call" | custom-call | bytes 16777216 | tf_op jit(solution)/shard_map/toeplitz/pallas_call | solution.py:43
  15.0 3.3 %copy-done.1 = bf16[16384,256]{1,0:T(8,128)(2,1)} copy-done((bf16[16384,256]{1,0:T(8,128)(2,1)}, bf16[16384,256]{1,0:T(8,128)(2,1)S(1)}, u32[]{:S(2)}) %copy-start.1) | copy-done | bytes 8388632
  18.3 1.2 bitcast_select_fusion.3
  19.5 0.9 pad_maximum_fusion.1
  20.5 2.3 copy.46
  22.8 1.1 copy-done.3
  23.9 1.0 copy-done.9
  25.0 105.3 %medium.1 = (bf16[256,2048]{1,0:T(8,128)(2,1)S(1)}, bf16[7,2048,128]{2,1,0:T(8,128)(2,1)S(1)}, bf16[7,256,1536]{2,1,0:T(8,128)(2,1)}) custom-call(bf16[3,256,2048]{2,1,0:T(8,128)(2,1)S(1)} %bitcast.85, bf16[304,2048]{1,0:T(8,128)(2,1)} %collective-permute-done.rim_ref, f32[3,7,2048]{2,1,0:T(8,128)S(1)} %bitcast.88, bf16[16384,256]{1,0:T(8,128)(2,1)} %copy-done.1, ...), custom_call_target="tpu_custom_call" | custom-call | flops 2147483648 | bytes 16777216 | tf_op jit(solution)/shard_map/medium/pallas_call | solution.py:169
  130.4 2.6 %collective-permute-done.2.b_ref = bf16[256,2048]{1,0:T(8,128)(2,1)S(1)} collective-permute-done((bf16[256,2048]{1,0:T(8,128)(2,1)S(1)}, bf16[256,2048]{1,0:T(8,128)(2,1)S(1)}, u32[]{:S(2)}, u32[]{:S(2)}) %collective-permute-start.2) | collective-permute-done | bytes 1048608 | tf_op jit(solution)/shard_map/ppermute | solution.py:484
  133.0 3.3 %out_projection.1 = (f32[8,256,128]{2,1,0:T(8,128)S(1)}, f32[8,256,128]{2,1,0:T(8,128)}) custom-call(bf16[256,2048]{1,0:T(8,128)(2,1)S(1)} %get-tuple-element.22.a_ref, bf16[256,2048]{1,0:T(8,128)(2,1)S(1)} %collective-permute-done.2.b_ref, bf16[2048,128]{1,0:T(8,128)(2,1)S(1)} %copy-done.10, bf16[7,2048,128]{2,1,0:T(8,128)(2,1)S(1)} %get-tuple-element.23.all_ref), custom_call_target="tpu_custom_call" | custom-call | flops 2147483648 | bytes 9437184 | tf_op jit(solution)/shard_map/out_projection/pallas_call | solution.py:202
  136.3 0.1 collective-permute-start.3
  136.5 2.7 %collective-permute-done.3.recv_ref = f32[8,256,128]{2,1,0:T(8,128)S(1)} collective-permute-done((f32[8,256,128]{2,1,0:T(8,128)}, f32[8,256,128]{2,1,0:T(8,128)S(1)}, u32[]{:S(2)}, u32[]{:S(2)}) %collective-permute-start.3) | collective-permute-done | bytes 1048608 | tf_op jit(solution)/shard_map/ppermute | solution.py:484
  139.2 2.9 %stream_norm.1 = (bf16[256,2048]{1,0:T(8,128)(2,1)}, bf16[8,256,256]{2,1,0:T(8,128)(2,1)}) custom-call(s32[3]{0:T(128)S(1)} %pad_add_fusion.where_ref, f32[8,256,128]{2,1,0:T(8,128)S(1)} %get-tuple-element.24.mine_ref, f32[8,256,128]{2,1,0:T(8,128)S(1)} %collective-permute-done.3.recv_ref, bf16[256,2048]{1,0:T(8,128)(2,1)S(1)} %copy-done.8, ...), custom_call_target="tpu_custom_call" | custom-call | flops 4194304 | bytes 6291456 | tf_op jit(solution)/shard_map/stream_norm/pallas_call | solution.py:239
  142.0 1.5 collective-permute-start.5
  143.5 0.1 sqrt_multiply_fusion
  143.8 0.1 broadcast_in_dim.26
  143.9 0.2 neg.34
  144.2 0.2 multiply_reduce_fusion
  144.4 23.0 %collective-permute-done.5.refs_2_ = bf16[8,256,256]{2,1,0:T(8,128)(2,1)S(1)} collective-permute-done((bf16[8,256,256]{2,1,0:T(8,128)(2,1)}, bf16[8,256,256]{2,1,0:T(8,128)(2,1)S(1)}, u32[]{:S(2)}, u32[]{:S(2)}) %collective-permute-start.5) | collective-permute-done | bytes 1048608 | tf_op jit(solution)/shard_map/ppermute | solution.py:487
  167.5 0.1 neg.32
  167.6 0.1 mul.185
  167.7 0.7 slice.95
  168.4 0.1 reverse.5
  168.6 0.1 slice.145
  168.6 0.8 exponential_select_fusion
  169.5 1.0 fusion.1
  170.4 0.9 fusion
  171.3 0.9 fusion.8
  172.2 1.0 copy-done.15
  173.1 0.9 fusion.7
  174.0 0.7 pad_maximum_fusion.2
  174.6 1.5 collective-permute-start.7
  176.1 0.8 pad_maximum_fusion.5.base_ref
  176.9 0.9 toeplitz.3.table_ref
  177.9 5.6 %collective-permute-done.7 = bf16[2,8,16,256]{3,2,1,0:T(8,128)(2,1)S(1)} collective-permute-done((bf16[2,8,16,256]{3,2,1,0:T(8,128)(2,1)}, bf16[2,8,16,256]{3,2,1,0:T(8,128)(2,1)S(1)}, u32[]{:S(2)}, u32[]{:S(2)}) %collective-permute-start.7) | collective-permute-done | bytes 131104 | tf_op jit(solution)/shard_map/ppermute | solution.py:451
  183.5 1.2 copy-done.14
  184.7 1.2 copy-done.16
  185.9 2.6 %copy-done.17 = bf16[7,256,1536]{2,1,0:T(8,128)(2,1)S(1)} copy-done((bf16[7,256,1536]{2,1,0:T(8,128)(2,1)S(1)}, bf16[7,256,1536]{2,1,0:T(8,128)(2,1)}, u32[]{:S(2)}) %copy-start.17) | copy-done | bytes 5505048
  188.5 11.5 %in_projection.1.k_ref.v_ref.q_ref = bf16[2,528,1536]{2,1,0:T(8,128)(2,1)S(1)} custom-call(s32[3]{0:T(128)S(1)} %pad_add_fusion.where_ref, bf16[2,8,16,256]{3,2,1,0:T(8,128)(2,1)S(1)} %pad_maximum_fusion.3.ahead_ref, bf16[8,256,256]{2,1,0:T(8,128)(2,1)} %get-tuple-element.27.refs_0_, bf16[8,256,256]{2,1,0:T(8,128)(2,1)S(1)} %copy-done.16, ...), custom_call_target="tpu_custom_call" | custom-call | flops 6643777536 | bytes 14680064 | tf_op jit(solution)/shard_map/in_projection/pallas_call | solution.py:289
  200.0 6.3 %product.1 = (bf16[2,512,512]{2,1,0:T(8,128)(2,1)S(1)}, f32[2,2,16,512]{3,2,1,0:T(8,128)S(1)}) custom-call(bf16[2,528,1536]{2,1,0:T(8,128)(2,1)S(1)} %in_projection.1.k_ref.v_ref.q_ref, bf16[2,528,1536]{2,1,0:T(8,128)(2,1)S(1)} %in_projection.1.k_ref.v_ref.q_ref, f32[3,7,512]{2,1,0:T(8,128)S(1)} %dynamic-slice_bitcast_fusion.1.taps_ref, ...), custom_call_target="tpu_custom_call" | custom-call | flops 268435456 | bytes 8388608 | tf_op jit(solution)/shard_map/product/pallas_call | solution.py:365
  206.4 1.2 collective-permute-start.13
  207.6 1.5 collective-permute-start.12
  209.1 2.4 collective-permute-start.11
  211.5 1.8 collective-permute-start.9
  213.2 1.1 collective-permute-start.8
  214.4 5.7 %local.1 = (f32[2,512,512]{2,1,0:T(8,128)S(1)}, f32[2,512,512]{2,1,0:T(8,128)S(1)}) custom-call(bf16[2,528,1536]{2,1,0:T(8,128)(2,1)S(1)} %in_projection.1.k_ref.v_ref.q_ref, f32[3,7,512]{2,1,0:T(8,128)S(1)} %dynamic-slice_bitcast_fusion.1.taps_ref, bf16[2,512,512]{2,1,0:T(8,128)(2,1)S(1)} %get-tuple-element.33.product_ref, ...), custom_call_target="tpu_custom_call" | custom-call | flops 2147483648 | bytes 16777216 | tf_op jit(solution)/shard_map/local/pallas_call | solution.py:394
  220.0 1.1 collective-permute-done.10
  221.3 3.2 %finish.1 = bf16[2,512,512]{2,1,0:T(8,128)(2,1)S(1)} custom-call(f32[2,512,512]{2,1,0:T(8,128)S(1)} %get-tuple-element.35.q_ref, f32[2,512,512]{2,1,0:T(8,128)S(1)} %get-tuple-element.36.y_ref, f32[2,2,16,512]{3,2,1,0:T(8,128)S(1)} %pad_maximum_fusion.4.state_ref, bf16[256,512]{1,0:T(8,128)(2,1)S(1)} %copy-done.5, bf16[256,512]{1,0:T(8,128)(2,1)S(1)} %get-tuple-element.41.low_ref), custom_call_target="tpu_custom_call" | custom-call | flops 268435456 | bytes 8388608 | tf_op jit(solution)/shard_map/finish/pallas_call | solution.py:416
  224.5 1.5 collective-permute-start.15
  226.1 12.1 %collective-permute-done.15 = bf16[512,512]{1,0:T(8,128)(2,1)S(1)} collective-permute-done((bf16[512,512]{1,0:T(8,128)(2,1)S(1)}, bf16[512,512]{1,0:T(8,128)(2,1)S(1)}, u32[]{:S(2)}, u32[]{:S(2)}) %collective-permute-start.15) | collective-permute-done | bytes 524320 | tf_op jit(solution)/shard_map/ppermute | solution.py:487
  238.4 1.9 collective-permute-done.16
  240.4 0.1 maximum_bitcast_fusion
  240.5 0.5 copy.54
  241.0 1.4 copy.55
  (79 shorter events, 1.1 us)
Async XLA Ops:
  0.6 177.2 %copy-start = (f32[7,3,2048]{2,0,1:T(8,128)S(1)}, f32[7,3,2048]{2,0,1:T(8,128)}, u32[]{:S(2)}) copy-start(f32[7,3,2048]{2,0,1:T(8,128)} %param.17) | copy-start | bytes 516100
  0.6 7.0 %copy-start.18 = (bf16[128,3,2048]{2,0,1:T(8,128)(2,1)S(1)}, bf16[128,3,2048]{2,0,1:T(8,128)(2,1)}, u32[]{:S(2)}) copy-start(bf16[128,3,2048]{2,0,1:T(8,128)(2,1)} %param.16) | copy-start | bytes 4718596
  4.1 7.0 %copy-start.21 = (f32[128,128]{1,0:T(8,128)S(1)}, f32[128,128]{1,0:T(8,128)}, u32[]{:S(2)}) copy-start(f32[128,128]{1,0:T(8,128)} %param.13) | copy-start | bytes 196612
  4.1 18.7 %collective-permute-start = (bf16[304,2048]{1,0:T(8,128)(2,1)}, bf16[304,2048]{1,0:T(8,128)(2,1)}, u32[]{:S(2)}, u32[]{:S(2)}) collective-permute-start(bf16[304,2048]{1,0:T(8,128)(2,1)} %pad_maximum_fusion), channel_id=1, source_target_pairs={{0,1},{1,2},{2,3},{3,4},{4,5},{5,6},{6,7},{7,8},{8,9},{9,10},{10,1... | collective-permute-start | bytes 3735560 | tf_op jit(solution)/shard_map/ppermute | solution.py:441
  9.5 8.9 %collective-permute-start.1 = (bf16[128,1536]{0,1:T(8,128)(2,1)}, bf16[128,1536]{0,1:T(8,128)(2,1)}, u32[]{:S(2)}, u32[]{:S(2)}) collective-permute-start(bf16[128,1536]{0,1:T(8,128)(2,1)} %bitcast.11), channel_id=1, source_target_pairs={{0,1},{1,0},{2,3},{3,2},{4,5},{5,4},{6,7},{7,6},{8,9},{9,8},{10,11... | collective-permute-start | bytes 1179656 | tf_op jit(solution)/shard_map/ppermute | solution.py:484
  11.5 6.8 %copy-start.19 = (bf16[128,3,1,512]{0,3,2,1:T(8,128)(2,1)S(1)}, bf16[128,3,1,512]{0,3,2,1:T(8,128)(2,1)}, u32[]{:S(2)}) copy-start(bf16[128,3,1,512]{0,3,2,1:T(8,128)(2,1)} %get-tuple-element.54) | copy-start | bytes 1179652
  15.0 3.3 %copy-start.1 = (bf16[16384,256]{1,0:T(8,128)(2,1)}, bf16[16384,256]{1,0:T(8,128)(2,1)S(1)}, u32[]{:S(2)}) copy-start(bf16[16384,256]{1,0:T(8,128)(2,1)S(1)} %toeplitz.2.table_ref) | copy-start | bytes 25165828
  18.3 4.5 %copy-start.2 = (bf16[256,3,2048]{2,0,1:T(8,128)(2,1)S(1)}, bf16[256,3,2048]{2,0,1:T(8,128)(2,1)}, u32[]{:S(2)}) copy-start(bf16[256,3,2048]{2,0,1:T(8,128)(2,1)} %param.11) | copy-start | bytes 9437188
  18.3 4.5 %copy-start.11 = (f32[7,3,2048]{2,0,1:T(8,128)S(1)}, f32[7,3,2048]{2,0,1:T(8,128)}, u32[]{:S(2)}) copy-start(f32[7,3,2048]{2,0,1:T(8,128)} %param.12) | copy-start | bytes 516100
  22.8 1.1 copy-start.3
  23.9 1.0 copy-start.9
  25.0 108.0 %copy-start.10 = (bf16[2048,128]{1,0:T(8,128)(2,1)S(1)}, bf16[2048,128]{1,0:T(8,128)(2,1)}, u32[]{:S(2)}) copy-start(bf16[2048,128]{1,0:T(8,128)(2,1)} %own_ref.1) | copy-start | bytes 1572868
  130.3 2.7 %collective-permute-start.2 = (bf16[256,2048]{1,0:T(8,128)(2,1)S(1)}, bf16[256,2048]{1,0:T(8,128)(2,1)S(1)}, u32[]{:S(2)}, u32[]{:S(2)}) collective-permute-start(bf16[256,2048]{1,0:T(8,128)(2,1)S(1)} %get-tuple-element.22.a_ref), channel_id=1, source_target_pairs={{0,1},{1,0},{2,3},{3,2},{4,5},{5,4},{6,7},{7,6},{8,9},{9,8},{10,11... | collective-permute-start | bytes 3145736 | tf_op jit(solution)/shard_map/ppermute | solution.py:484
  133.0 6.2 %copy-start.8 = (bf16[256,2048]{1,0:T(8,128)(2,1)S(1)}, bf16[256,2048]{1,0:T(8,128)(2,1)}, u32[]{:S(2)}) copy-start(bf16[256,2048]{1,0:T(8,128)(2,1)} %in_ref.1) | copy-start | bytes 3145732
  133.0 6.2 %copy-start.12 = (f32[2048]{0:T(1024)S(1)}, f32[2048]{0:T(1024)}, u32[]{:S(2)}) copy-start(f32[2048]{0:T(1024)} %param.15) | copy-start | bytes 24580
  136.3 7.2 %copy-start.22 = (f32[128,16]{0,1:T(8,128)S(1)}, f32[128,16]{0,1:T(8,128)}, u32[]{:S(2)}) copy-start(f32[128,16]{0,1:T(8,128)} %param.19) | copy-start | bytes 24580
  136.3 7.2 %copy-start.23 = (f32[128,16]{0,1:T(8,128)S(1)}, f32[128,16]{0,1:T(8,128)}, u32[]{:S(2)}) copy-start(f32[128,16]{0,1:T(8,128)} %param.18) | copy-start | bytes 24580
  136.3 2.9 %collective-permute-start.3 = (f32[8,256,128]{2,1,0:T(8,128)}, f32[8,256,128]{2,1,0:T(8,128)S(1)}, u32[]{:S(2)}, u32[]{:S(2)}) collective-permute-start(f32[8,256,128]{2,1,0:T(8,128)} %get-tuple-element.25), channel_id=1, source_target_pairs={{0,1},{1,0},{2,3},{3,2},{4,5},{5,4},{6,7},{7,6},{8,9},{9,8},{10,11... | collective-permute-start | bytes 3145736 | tf_op jit(solution)/shard_map/ppermute | solution.py:484
  142.0 25.4 %collective-permute-start.5 = (bf16[8,256,256]{2,1,0:T(8,128)(2,1)}, bf16[8,256,256]{2,1,0:T(8,128)(2,1)S(1)}, u32[]{:S(2)}, u32[]{:S(2)}) collective-permute-start(bf16[8,256,256]{2,1,0:T(8,128)(2,1)} %get-tuple-element.27.refs_0_), channel_id=1, source_target_pairs={{0,16},{16,0},{1,17},{17,1},{2,18},{18,2},{3,19},{19,3},{4,20},{20... | collective-permute-start | bytes 3145736 | tf_op jit(solution)/shard_map/ppermute | solution.py:487
  144.1 27.2 %collective-permute-start.4 = (bf16[8,256,256]{2,1,0:T(8,128)(2,1)}, bf16[8,256,256]{2,1,0:T(8,128)(2,1)S(1)}, u32[]{:S(2)}, u32[]{:S(2)}) collective-permute-start(bf16[8,256,256]{2,1,0:T(8,128)(2,1)} %get-tuple-element.27.refs_0_), channel_id=1, source_target_pairs={{0,1},{1,0},{2,3},{3,2},{4,5},{5,4},{6,7},{7,6},{8,9},{9,8},{10,11... | collective-permute-start | bytes 3145736 | tf_op jit(solution)/shard_map/ppermute | solution.py:484
  167.5 9.5 %copy-start.13 = (bf16[8,256,256]{2,1,0:T(8,128)(2,1)}, bf16[8,256,256]{2,1,0:T(8,128)(2,1)S(1)}, u32[]{:S(2)}) copy-start(bf16[8,256,256]{2,1,0:T(8,128)(2,1)S(1)} %collective-permute-done.5.refs_2_) | copy-start | bytes 3145732
  167.5 5.7 %collective-permute-start.6 = (bf16[8,256,256]{2,1,0:T(8,128)(2,1)S(1)}, bf16[8,256,256]{2,1,0:T(8,128)(2,1)}, u32[]{:S(2)}, u32[]{:S(2)}) collective-permute-start(bf16[8,256,256]{2,1,0:T(8,128)(2,1)S(1)} %collective-permute-done.5.refs_2_), channel_id=1, source_target_pairs={{0,1},{1,0},{2,3},{3,2},{4,5},{5,4},{6,7},{7,6},{8,9},{9,8},{10,11... | collective-permute-start | bytes 3145736 | tf_op jit(solution)/shard_map/ppermute | solution.py:484
  168.4 15.1 %copy-start.4 = (bf16[2,128,1536]{2,1,0:T(8,128)(2,1)S(1)}, bf16[2,128,1536]{2,1,0:T(8,128)(2,1)}, u32[]{:S(2)}) copy-start(bf16[2,128,1536]{2,1,0:T(8,128)(2,1)} %copy.46) | copy-start | bytes 2359300
  172.2 1.0 copy-start.15
  174.6 8.8 %collective-permute-start.7 = (bf16[2,8,16,256]{3,2,1,0:T(8,128)(2,1)}, bf16[2,8,16,256]{3,2,1,0:T(8,128)(2,1)S(1)}, u32[]{:S(2)}, u32[]{:S(2)}) collective-permute-start(bf16[2,8,16,256]{3,2,1,0:T(8,128)(2,1)} %pad_maximum_fusion.2), channel_id=1, source_target_pairs={{14,0},{15,1},{0,2},{1,3},{2,4},{3,5},{4,6},{5,7},{6,8},{7,9},{8,1... | collective-permute-start | bytes 393224 | tf_op jit(solution)/shard_map/ppermute | solution.py:451
  183.5 1.2 copy-start.14
  184.7 1.2 copy-start.16
  185.9 2.6 %copy-start.17 = (bf16[7,256,1536]{2,1,0:T(8,128)(2,1)S(1)}, bf16[7,256,1536]{2,1,0:T(8,128)(2,1)}, u32[]{:S(2)}) copy-start(bf16[7,256,1536]{2,1,0:T(8,128)(2,1)} %get-tuple-element.29.refs_5_) | copy-start | bytes 16515076
  188.5 11.5 %copy-start.6 = (bf16[512,256]{1,0:T(8,128)(2,1)S(1)}, bf16[512,256]{1,0:T(8,128)(2,1)}, u32[]{:S(2)}) copy-start(bf16[512,256]{1,0:T(8,128)(2,1)} %get-tuple-element.32.low_ref) | copy-start | bytes 786436
  188.5 11.5 %copy-start.7 = (bf16[512,256]{1,0:T(8,128)(2,1)S(1)}, bf16[512,256]{1,0:T(8,128)(2,1)}, u32[]{:S(2)}) copy-start(bf16[512,256]{1,0:T(8,128)(2,1)} %get-tuple-element.31.high_ref) | copy-start | bytes 786436
  200.0 11.4 %copy-start.20 = (f32[7,16,512]{2,1,0:T(8,128)S(1)}, f32[7,16,512]{2,1,0:T(8,128)}, u32[]{:S(2)}) copy-start(f32[7,16,512]{2,1,0:T(8,128)} %exponential_select_fusion) | copy-start | bytes 688132
  206.3 5.1 %collective-permute-start.14 = (f32[2,16,512]{2,1,0:T(8,128)S(1)}, f32[2,16,512]{2,1,0:T(8,128)S(1)}, u32[]{:S(2)}, u32[]{:S(2)}) collective-permute-start(f32[2,16,512]{2,1,0:T(8,128)S(1)} %fusion.6), channel_id=1, source_target_pairs={{2,0},{3,1},{4,2},{5,3},{6,4},{7,5},{8,6},{9,7},{10,8},{11,9},{12,... | collective-permute-start | bytes 196616 | tf_op jit(solution)/shard_map/ppermute | solution.py:451
  206.4 6.8 %collective-permute-start.13 = (f32[2,16,512]{2,1,0:T(8,128)S(1)}, f32[2,16,512]{2,1,0:T(8,128)S(1)}, u32[]{:S(2)}, u32[]{:S(2)}) collective-permute-start(f32[2,16,512]{2,1,0:T(8,128)S(1)} %fusion.6), channel_id=1, source_target_pairs={{4,0},{5,1},{6,2},{7,3},{8,4},{9,5},{10,6},{11,7},{12,8},{13,9},{1... | collective-permute-start | bytes 196616 | tf_op jit(solution)/shard_map/ppermute | solution.py:451
  207.6 12.4 %collective-permute-start.12 = (f32[2,16,512]{2,1,0:T(8,128)S(1)}, f32[2,16,512]{2,1,0:T(8,128)S(1)}, u32[]{:S(2)}, u32[]{:S(2)}) collective-permute-start(f32[2,16,512]{2,1,0:T(8,128)S(1)} %fusion.6), channel_id=1, source_target_pairs={{6,0},{7,1},{8,2},{9,3},{10,4},{11,5},{12,6},{13,7},{14,8},{15,9},... | collective-permute-start | bytes 196616 | tf_op jit(solution)/shard_map/ppermute | solution.py:451
  209.1 11.0 %collective-permute-start.11 = (f32[2,16,512]{2,1,0:T(8,128)S(1)}, f32[2,16,512]{2,1,0:T(8,128)S(1)}, u32[]{:S(2)}, u32[]{:S(2)}) collective-permute-start(f32[2,16,512]{2,1,0:T(8,128)S(1)} %fusion.6), channel_id=1, source_target_pairs={{8,0},{9,1},{10,2},{11,3},{12,4},{13,5},{14,6},{15,7},{0,8},{1,9},... | collective-permute-start | bytes 196616 | tf_op jit(solution)/shard_map/ppermute | solution.py:451
  211.4 9.7 %collective-permute-start.10 = (f32[2,16,512]{2,1,0:T(8,128)S(1)}, f32[2,16,512]{2,1,0:T(8,128)S(1)}, u32[]{:S(2)}, u32[]{:S(2)}) collective-permute-start(f32[2,16,512]{2,1,0:T(8,128)S(1)} %fusion.6), channel_id=1, source_target_pairs={{10,0},{11,1},{12,2},{13,3},{14,4},{15,5},{0,6},{1,7},{2,8},{3,9},... | collective-permute-start | bytes 196616 | tf_op jit(solution)/shard_map/ppermute | solution.py:451
  211.5 9.7 %collective-permute-start.9 = (f32[2,16,512]{2,1,0:T(8,128)S(1)}, f32[2,16,512]{2,1,0:T(8,128)S(1)}, u32[]{:S(2)}, u32[]{:S(2)}) collective-permute-start(f32[2,16,512]{2,1,0:T(8,128)S(1)} %fusion.6), channel_id=1, source_target_pairs={{12,0},{13,1},{14,2},{15,3},{0,4},{1,5},{2,6},{3,7},{4,8},{5,9},{6... | collective-permute-start | bytes 196616 | tf_op jit(solution)/shard_map/ppermute | solution.py:451
  213.2 7.9 %collective-permute-start.8 = (f32[2,16,512]{2,1,0:T(8,128)S(1)}, f32[2,16,512]{2,1,0:T(8,128)S(1)}, u32[]{:S(2)}, u32[]{:S(2)}) collective-permute-start(f32[2,16,512]{2,1,0:T(8,128)S(1)} %fusion.6), channel_id=1, source_target_pairs={{14,0},{15,1},{0,2},{1,3},{2,4},{3,5},{4,6},{5,7},{6,8},{7,9},{8,1... | collective-permute-start | bytes 196616 | tf_op jit(solution)/shard_map/ppermute | solution.py:451
  214.4 6.9 %copy-start.5 = (bf16[256,512]{1,0:T(8,128)(2,1)S(1)}, bf16[256,512]{1,0:T(8,128)(2,1)}, u32[]{:S(2)}) copy-start(bf16[256,512]{1,0:T(8,128)(2,1)} %get-tuple-element.40.high_ref) | copy-start | bytes 786436
  224.5 13.6 %collective-permute-start.15 = (bf16[512,512]{1,0:T(8,128)(2,1)S(1)}, bf16[512,512]{1,0:T(8,128)(2,1)S(1)}, u32[]{:S(2)}, u32[]{:S(2)}) collective-permute-start(bf16[512,512]{1,0:T(8,128)(2,1)S(1)} %dynamic-slice_bitcast_fusion), channel_id=1, source_target_pairs={{0,16},{16,0},{1,17},{17,1},{2,18},{18,2},{3,19},{19,3},{4,20},{20... | collective-permute-start | bytes 1572872 | tf_op jit(solution)/shard_map/ppermute | solution.py:487
  238.3 2.0 collective-permute-start.16
